TPU v7x, 512 devices: a whole 4x8x8 slice. The times are simulated.
512 devices in a mesh: member: 16 (over z, core), point: 32 (over y, x).
Axes of the slice: x: 4, y: 8, z: 8, core: 2. Of those that a mesh axis runs over, the one named last changes fastest.
Arguments:
- ensemble: float32 [32, 655360], P('member', 'point'), may hold values from -6 to 6
- inputs: bfloat16 [6144, 1024], P('point'), may hold values from -6 to 6
- features: bfloat16 [128, 256], replicated, may hold values from -6 to 6
- query_index: int32 [393216], P('point'), may hold values from 0 to 127
- observed: float32 [393216], P('point'), may hold values from -6 to 6
- perturb: float32 [32, 393216], P('member', 'point'), may hold values from -3 to 3
Outputs:
- theta_next: float32 [32, 655360], P('member', 'point')
- coefficients: float32 [32, 32], replicated
All inputs are finite; a program needn't handle non-finite values.
Results may differ from a plain program's by a relative error of at most 0.0003.
Values may be sent and summed in bfloat16 or wider, within the bound.
No kernel may reach another device: no remote copies, remote signals or barrier semaphores. Data moves between devices by JAX's collectives and lax.ppermute only.
A program may use at most 64 MiB of HBM per device.

v0:
```python
import jax
import jax.numpy as jnp
from jax import lax
from jax.sharding import PartitionSpec as P

SENSORS = 1024
WIDTH = 256
BASIS = 512
FEATS = 256
QOBS = 64
SUBSTEPS = 2


NOISE_STD = 0.5
RIDGE_SHARE = 0.5


def evaluate_members(gathered, inputs, features, query_index):
    count = gathered.shape[0]
    first = SENSORS * WIDTH
    second = first + WIDTH * WIDTH
    third = second + WIDTH * BASIS
    fourth = third + FEATS * WIDTH
    branch_in = gathered[:, :first].reshape(count, SENSORS, WIDTH)
    branch_mid = gathered[:, first:second].reshape(count, WIDTH, WIDTH)
    branch_out = gathered[:, second:third].reshape(count, WIDTH, BASIS)
    trunk_in = gathered[:, third:fourth].reshape(count, FEATS, WIDTH)
    trunk_out = gathered[:, fourth:].reshape(count, WIDTH, BASIS)
    hidden = jnp.tanh(
        jnp.einsum("is,msw->miw", inputs, branch_in, preferred_element_type=jnp.float32)
        * SENSORS ** (-0.5)
    ).astype(jnp.bfloat16)
    hidden = jnp.tanh(
        jnp.einsum("miv,mvw->miw", hidden, branch_mid, preferred_element_type=jnp.float32)
        * WIDTH ** (-0.5)
    ).astype(jnp.bfloat16)
    branch = (
        jnp.einsum("miv,mvb->mib", hidden, branch_out, preferred_element_type=jnp.float32)
        * WIDTH ** (-0.5)
    ).astype(jnp.bfloat16)
    trunk_hidden = jnp.tanh(
        jnp.einsum("qf,mfw->mqw", features, trunk_in, preferred_element_type=jnp.float32)
        * FEATS ** (-0.5)
    ).astype(jnp.bfloat16)
    trunk = (
        jnp.einsum("mqv,mvb->mqb", trunk_hidden, trunk_out, preferred_element_type=jnp.float32)
        * WIDTH ** (-0.5)
    ).astype(jnp.bfloat16)
    whole = jnp.einsum(
        "mib,mqb->miq", branch, trunk, preferred_element_type=jnp.float32
    ) * BASIS ** (-0.5)
    picks = query_index.reshape(inputs.shape[0], QOBS)
    candidates = lax.broadcasted_iota(jnp.int32, (1, 1, whole.shape[2]), 2)
    selector = (picks[:, :, None] == candidates).astype(jnp.float32)
    chosen = jnp.einsum("miq,ioq->mio", whole, selector, precision=lax.Precision.HIGHEST)
    return chosen.reshape(count, -1)


def member_sums(all_preds, all_innov):
    members = all_preds.shape[0]
    pred_vals = all_preds.astype(jnp.float32)
    pred_anom = (pred_vals - jnp.mean(pred_vals, axis=0)) / (NOISE_STD * (members - 1) ** 0.5)
    gram_obs = jnp.dot(pred_anom, pred_anom.T, precision=lax.Precision.HIGHEST)
    cross_obs = jnp.dot(pred_anom, all_innov.astype(jnp.float32).T, precision=lax.Precision.HIGHEST)
    return (gram_obs, cross_obs)


def substep(weights, param_major, inputs, features, query_index, observed, perturb):
    gathered = lax.all_gather(weights, "point", axis=1, tiled=True)
    preds = evaluate_members(gathered, inputs, features, query_index).astype(jnp.bfloat16)
    preds = lax.optimization_barrier(preds)
    innov = ((observed[None, :] + perturb - preds.astype(jnp.float32)) / NOISE_STD).astype(
        jnp.bfloat16
    )
    members = param_major.shape[0]
    par_anom = (param_major - jnp.mean(param_major, axis=0)) / (members - 1) ** 0.5
    gram_par = jnp.dot(par_anom, par_anom.T, precision=lax.Precision.HIGHEST)
    cross_par = -jnp.dot(par_anom, param_major.T, precision=lax.Precision.HIGHEST)
    all_preds, all_innov = (
        lax.all_gather(preds, "member", axis=0, tiled=True),
        lax.all_gather(innov, "member", axis=0, tiled=True),
    )
    gram_obs, cross_obs = member_sums(all_preds, all_innov)
    gram_obs, cross_obs = lax.psum((gram_obs, cross_obs), "point")
    gram_par, cross_par = lax.psum((gram_par, cross_par), ("member", "point"))
    gram = gram_obs + gram_par
    cross = cross_obs + cross_par
    ridge = RIDGE_SHARE * jnp.trace(gram) / members
    system = gram + ridge * jnp.eye(members, dtype=jnp.float32)
    factor = jnp.linalg.cholesky(system)
    coefficients = jax.scipy.linalg.cho_solve((factor, True), cross)
    updated = param_major + jnp.dot(coefficients.T, par_anom, precision=lax.Precision.HIGHEST)
    return (coefficients, updated)


def local(ensemble, inputs, features, query_index, observed, perturb):
    current = ensemble
    for repeat in range(SUBSTEPS):
        param_major = lax.all_to_all(current, "member", split_axis=1, concat_axis=0, tiled=True)
        coefficients, updated = substep(
            current.astype(jnp.bfloat16),
            param_major,
            inputs,
            features,
            query_index,
            observed,
            perturb,
        )
        current = lax.all_to_all(updated, "member", split_axis=0, concat_axis=1, tiled=True)
    return (current, coefficients)


def solution(mesh):
    in_specs = (
        P("member", "point"),
        P("point", None),
        P(),
        P("point"),
        P("point"),
        P("member", "point"),
    )
    out_specs = (P("member", "point"), P())
    return jax.shard_map(local, mesh=mesh, in_specs=in_specs, out_specs=out_specs, check_vma=False)
```

profile of v0, /device:TPU:1, one launch (start us, length us, event | category | flops | bytes accessed | tf_op | source)
XLA Modules:
  0.0 675.9 jit_solution(14981827967099968341)
XLA Ops:
  7.2 1.6 convert_element_type.85
  8.9 11.8 %all-to-all-start = ((f32[2,16,1280]{2,0,1:T(2,128)}), f32[2,16,1280]{2,0,1:T(2,128)S(1)}, u32[]{:S(2)}, u32[]{:S(2)}) async-start(f32[2,16,1280]{2,0,1:T(2,128)} %bitcast.126), calls=%async_computation | async-start | bytes 327680 | tf_op jit(solution)/shard_map/all_to_all | solution.py:99
  20.8 0.9 eq.35
  21.7 8.7 %all-to-all-done = f32[2,16,1280]{2,0,1:T(2,128)S(1)} async-done(((f32[2,16,1280]{2,0,1:T(2,128)}), f32[2,16,1280]{2,0,1:T(2,128)S(1)}, u32[]{:S(2)}, u32[]{:S(2)}) %all-to-all-start) | async-done | bytes 163872 | tf_op jit(solution)/shard_map/all_to_all | solution.py:99
  31.4 98.2 %all-reduce.1 = (f32[32,32]{0,1:T(8,128)}, f32[32,32]{1,0:T(8,128)}) all-reduce(f32[32,32]{0,1:T(8,128)S(1)} %fusion.128, f32[32,32]{1,0:T(8,128)S(1)} %convolution_negate_fusion.1), channel_id=1, replica_groups=mesh['member'=16,'point'=32] {'member','point'}, use_global_device_ids=true, to_apply=%region_3.0 | all-reduce | flops 2048 | bytes 16384 | tf_op jit(solution)/shard_map/psum | solution.py:85
  129.6 2.0 fusion.126
  131.6 1.4 fusion.127
  135.2 6.4 fusion.31
  141.8 18.9 %all-gather = bf16[16,2,12288]{2,1,0:T(2,128)(2,1)S(1)} all-gather(bf16[1,2,12288]{2,1,0:T(2,128)(2,1)S(1)} %bitcast.132), channel_id=1, replica_groups=mesh['member'=16,'point'=32] {'member'}, dimensions={0}, use_global_device_ids=true | all-gather | bytes 835584 | tf_op jit(solution)/shard_map/all_gather | solution.py:80
  160.9 0.7 convert_reduce_fusion.1
  162.4 16.6 %all-gather.1 = bf16[16,2,12288]{2,1,0:T(2,128)(2,1)S(1)} all-gather(bf16[1,2,12288]{2,1,0:T(2,128)(2,1)S(1)} %fusion.96), channel_id=1, replica_groups=mesh['member'=16,'point'=32] {'member'}, dimensions={0}, use_global_device_ids=true | all-gather | bytes 835584 | tf_op jit(solution)/shard_map/all_gather | solution.py:81
  179.3 2.5 fusion.5
  181.8 1.0 fusion.4
  182.8 111.7 %all-reduce.3 = (f32[32,32]{0,1:T(8,128)S(1)}, f32[32,32]{1,0:T(8,128)S(1)}) all-reduce(f32[32,32]{0,1:T(8,128)S(1)} %fusion.5, f32[32,32]{1,0:T(8,128)S(1)} %fusion.4), channel_id=1, replica_groups=mesh['member'=16,'point'=32] {'point'}, use_global_device_ids=true, to_apply=%region_1.0 | all-reduce | flops 2048 | bytes 16384 | tf_op jit(solution)/shard_map/psum | solution.py:84
  295.9 2.9 cholesky.44
  300.1 2.4 custom-call.8
  303.4 40.8 %all_to_all.70 = f32[16,2,1280]{2,1,0:T(2,128)S(1)} all-to-all(f32[16,2,1280]{2,1,0:T(2,128)S(1)} %all_to_all.56), channel_id=1, replica_groups=mesh['member'=16,'point'=32] {'member'}, dimensions={0} | all-to-all | bytes 327680 | tf_op jit(solution)/shard_map/all_to_all | solution.py:109
  344.9 12.3 %all_to_all.71 = f32[2,16,1280]{2,0,1:T(2,128)S(1)} all-to-all(f32[2,16,1280]{2,0,1:T(2,128)S(1)} %bitcast.125), channel_id=1, replica_groups=mesh['member'=16,'point'=32] {'member'}, dimensions={1} | all-to-all | bytes 327680 | tf_op jit(solution)/shard_map/all_to_all | solution.py:99
  358.2 94.2 %all-reduce = (f32[32,32]{0,1:T(8,128)}, f32[32,32]{1,0:T(8,128)}) all-reduce(f32[32,32]{0,1:T(8,128)S(1)} %fusion.129, f32[32,32]{1,0:T(8,128)S(1)} %convolution_negate_fusion), channel_id=1, replica_groups=mesh['member'=16,'point'=32] {'member','point'}, use_global_device_ids=true, to_apply=%region_12.15 | all-reduce | flops 2048 | bytes 16384 | tf_op jit(solution)/shard_map/psum | solution.py:85
  452.4 1.5 fusion.125
  454.4 2.0 fusion.124
  457.4 6.4 fusion.30
  464.7 18.0 %all-gather.2 = bf16[16,2,12288]{2,1,0:T(2,128)(2,1)S(1)} all-gather(bf16[1,2,12288]{2,1,0:T(2,128)(2,1)S(1)} %bitcast.133), channel_id=1, replica_groups=mesh['member'=16,'point'=32] {'member'}, dimensions={0}, use_global_device_ids=true | all-gather | bytes 835584 | tf_op jit(solution)/shard_map/all_gather | solution.py:80
  482.9 1.3 convert_reduce_fusion
  484.2 17.3 %all-gather.3 = bf16[16,2,12288]{2,1,0:T(2,128)(2,1)S(1)} all-gather(bf16[1,2,12288]{2,1,0:T(2,128)(2,1)} %fusion.97), channel_id=1, replica_groups=mesh['member'=16,'point'=32] {'member'}, dimensions={0}, use_global_device_ids=true | all-gather | bytes 835584 | tf_op jit(solution)/shard_map/all_gather | solution.py:81
  501.8 0.8 broadcast_multiply_fusion
  502.6 1.4 fusion.7
  504.0 1.0 fusion.6
  505.0 112.9 %all-reduce.2 = (f32[32,32]{0,1:T(8,128)S(1)}, f32[32,32]{1,0:T(8,128)S(1)}) all-reduce(f32[32,32]{0,1:T(8,128)S(1)} %fusion.7, f32[32,32]{1,0:T(8,128)S(1)} %fusion.6), channel_id=1, replica_groups=mesh['member'=16,'point'=32] {'point'}, use_global_device_ids=true, to_apply=%region_10.13 | all-reduce | flops 2048 | bytes 16384 | tf_op jit(solution)/shard_map/psum | solution.py:84
  619.2 2.9 cholesky.55
  623.5 2.4 custom-call.9
  626.8 41.6 %all_to_all.72 = f32[16,2,1280]{2,1,0:T(2,128)S(1)} all-to-all(f32[16,2,1280]{2,1,0:T(2,128)S(1)} %all_to_all.62), channel_id=1, replica_groups=mesh['member'=16,'point'=32] {'member'}, dimensions={0} | all-to-all | bytes 327680 | tf_op jit(solution)/shard_map/all_to_all | solution.py:109
  (103 shorter events, 15.5 us)
Async XLA Ops:
  7.2 126.4 %copy-start = (bf16[192,1024]{1,0:T(8,128)(2,1)S(1)}, bf16[192,1024]{1,0:T(8,128)(2,1)}, u32[]{:S(2)}) copy-start(bf16[192,1024]{1,0:T(8,128)(2,1)} %param.10) | copy-start | bytes 1179652
  7.2 122.4 %all-gather.7.cloned.1.call-start = ((), (), s32[]{:S(2)}) async-start(), calls=%async_computation.4 | async-start | bytes 2703360 | tf_op jit(solution)/shard_map/all_gather | solution.py:69
  8.9 21.5 %all-to-all-start = ((f32[2,16,1280]{2,0,1:T(2,128)}), f32[2,16,1280]{2,0,1:T(2,128)S(1)}, u32[]{:S(2)}, u32[]{:S(2)}) async-start(f32[2,16,1280]{2,0,1:T(2,128)} %bitcast.126), calls=%async_computation | async-start | bytes 327680 | tf_op jit(solution)/shard_map/all_to_all | solution.py:99
  20.7 431.6 %all-gather.9.cloned.1.call-start = ((), (), s32[]{:S(2)}) async-start(), calls=%async_computation.5 | async-start | bytes 2703360 | tf_op jit(solution)/shard_map/all_gather | solution.py:69
  21.7 113.5 %copy-start.10 = (s32[192,64]{1,0:T(8,128)}, s32[192,64]{1,0:T(8,128)S(1)}, u32[]{:S(2)}) copy-start(s32[192,64]{1,0:T(8,128)S(1)} %eq.35) | copy-start | bytes 147460
  30.8 102.2 %copy-start.3 = (f32[32,1280]{1,0:T(8,128)}, f32[32,1280]{1,0:T(8,128)S(1)}, u32[]{:S(2)}) copy-start(f32[32,1280]{1,0:T(8,128)S(1)} %all_to_all.55) | copy-start | bytes 491524
  129.6 3.4 copy-start.17
  133.0 1.2 slice-start
  160.7 1.6 copy-start.6
  160.7 1.6 copy-start.8
  179.3 2.5 copy-start.5
  181.8 112.7 %copy-start.14 = (f32[32,32]{0,1:T(8,128)S(1)}, f32[32,32]{0,1:T(8,128)}, u32[]{:S(2)}) copy-start(f32[32,32]{0,1:T(8,128)} %get-tuple-element.6) | copy-start | bytes 12292
  181.8 120.7 %copy-start.16 = (f32[32,32]{1,0:T(8,128)S(1)}, f32[32,32]{1,0:T(8,128)}, u32[]{:S(2)}) copy-start(f32[32,32]{1,0:T(8,128)} %get-tuple-element.7) | copy-start | bytes 12292
  181.8 121.1 %copy-start.4 = (f32[32,1280]{1,0:T(8,128)S(1)}, f32[32,1280]{1,0:T(8,128)}, u32[]{:S(2)}) copy-start(f32[32,1280]{1,0:T(8,128)} %copy-done.3) | copy-start | bytes 491524
  357.6 94.7 %copy-start.1 = (f32[32,1280]{1,0:T(8,128)}, f32[32,1280]{1,0:T(8,128)S(1)}, u32[]{:S(2)}) copy-start(f32[32,1280]{1,0:T(8,128)S(1)} %all_to_all.61) | copy-start | bytes 491524
  452.4 1.5 slice-start.1
  454.4 2.0 copy-start.18
  456.4 1.0 copy-start.11
  457.4 6.6 copy-start.7
  457.4 6.6 copy-start.9
  504.0 113.9 %copy-start.13 = (f32[32,32]{0,1:T(8,128)S(1)}, f32[32,32]{0,1:T(8,128)}, u32[]{:S(2)}) copy-start(f32[32,32]{0,1:T(8,128)} %get-tuple-element.4) | copy-start | bytes 12292
  504.0 121.9 %copy-start.15 = (f32[32,32]{1,0:T(8,128)S(1)}, f32[32,32]{1,0:T(8,128)}, u32[]{:S(2)}) copy-start(f32[32,32]{1,0:T(8,128)} %get-tuple-element.5) | copy-start | bytes 12292
  504.0 122.3 %copy-start.2 = (f32[32,1280]{1,0:T(8,128)S(1)}, f32[32,1280]{1,0:T(8,128)}, u32[]{:S(2)}) copy-start(f32[32,1280]{1,0:T(8,128)} %copy-done.1) | copy-start | bytes 491524
  626.3 42.8 %copy-start.12 = (f32[32,32]{1,0:T(8,128)}, f32[32,32]{1,0:T(8,128)S(1)}, u32[]{:S(2)}) copy-start(f32[32,32]{1,0:T(8,128)S(1)} %fusion.100) | copy-start | bytes 12292
Sparse Core Ops, SparseCore 0:
  11.2 86.3 all-gather.6
  345.0 73.1 all-gather.8
where the time goes:
time: 677 us; the launch traced here: 676 us
  blocking collectives  583 us (86%)
  matrix products  24.1 us (4%)
  other arithmetic  21.5 us (3%)
  between operations  15.9 us (2%)
  starting transfers between devices  11.9 us (2%)
  local copies, waits for them, and re-layouts  11.2 us (2%)
  waiting for transfers between devices  8.75 us (1%)
    psum x2, blocking collectives, substep(): gram_obs, cross_obs = lax.psum((gram_obs, cross_obs), 'point')  225 us
    psum x2, blocking collectives, substep(): gram_par, cross_par = lax.psum((gram_par, cross_par), ('member', 'point'))  192 us
    all_to_all x2, blocking collectives, local(): lax.all_to_all(updated, 'member', split_axis=0, concat_axis=1, tiled=True)  82.4 us
    all_gather x2, blocking collectives, substep(): lax.all_gather(preds, 'member', axis=0, tiled=True)  36.9 us
    all_gather x2, blocking collectives, substep(): lax.all_gather(innov, 'member', axis=0, tiled=True)  33.9 us
  transfers between devices with their start and end apart: 3, of which 1 were waited for; matrix products, arithmetic and copies ran while one was open for 0% of the time, Pallas kernels for 0%

commit v1 on v0

v1 whole, which is shorter than its diff:
```python
import functools

import jax
import jax.numpy as jnp
from jax import lax
from jax.experimental import pallas as pl
from jax.experimental.pallas import tpu as pltpu
from jax.sharding import Mesh, PartitionSpec as P

SENSORS = 1024
WIDTH = 256
BASIS = 512
FEATS = 256
QOBS = 64
SUBSTEPS = 2
MEMBERS = 32
NOISE_STD = 0.5
RIDGE_SHARE = 0.5
ROWS = 40
F32, BF16 = jnp.float32, jnp.bfloat16
HIGHEST = lax.Precision.HIGHEST
VMEM = pl.BlockSpec(memory_space=pltpu.VMEM)
SMEM = pl.BlockSpec(memory_space=pltpu.SMEM)


def mxu(a, b):
    return jnp.dot(a, b, preferred_element_type=F32)


def interleave_matrix():
    r = lax.broadcasted_iota(jnp.int32, (256, 256), 0)
    s = lax.broadcasted_iota(jnp.int32, (256, 256), 1)
    return (s == (r % 2) * 128 + r // 2).astype(F32).astype(BF16)


def evaluate_kernel(w_ref, x_ref, features_ref, out_ref, whole_ref):
    mix = interleave_matrix()

    def narrow(start):
        both = jnp.concatenate([w_ref[0, start : start + 128, :], w_ref[1, start : start + 128, :]], 0)
        return mxu(mix, both).astype(BF16)

    branch_in, branch_mid, branch_out, trunk_in, trunk_out = 0, 512, 640, 896, 1024
    trunk_hidden = jnp.tanh(mxu(features_ref[...], narrow(trunk_in)) * FEATS ** (-0.5)).astype(BF16)
    trunk = [
        (mxu(trunk_hidden, w_ref[c, trunk_out : trunk_out + 256, :]) * WIDTH ** (-0.5)).astype(BF16)
        for c in range(2)
    ]
    total = None
    for i in range(4):
        part = mxu(x_ref[:, 256 * i : 256 * i + 256], narrow(branch_in + 128 * i))
        total = part if total is None else total + part
    hidden = jnp.tanh(total * SENSORS ** (-0.5)).astype(BF16)
    hidden = jnp.tanh(mxu(hidden, narrow(branch_mid)) * WIDTH ** (-0.5)).astype(BF16)
    whole = None
    for c in range(2):
        branch = (mxu(hidden, w_ref[c, branch_out : branch_out + 256, :]) * WIDTH ** (-0.5)).astype(BF16)
        part = lax.dot_general(branch, trunk[c], (((1,), (1,)), ((), ())), preferred_element_type=F32)
        whole = part if whole is None else whole + part
    whole = whole * BASIS ** (-0.5)
    picks = x_ref[:, SENSORS : SENSORS + 128].astype(F32).astype(jnp.int32)
    whole_ref[...] = jnp.take_along_axis(whole, picks, axis=1, mode="promise_in_bounds")
    left = lax.broadcasted_iota(jnp.int32, (8, 128), 1) < QOBS
    for x in range(4):
        for k in range(0, 12, 2):
            first = whole_ref[pl.ds(x * 96 + k, 8, stride=12), :]
            second = whole_ref[pl.ds(x * 96 + k + 1, 8, stride=12), :]
            out_ref[x * 8 : x * 8 + 8, k * QOBS : k * QOBS + 128] = jnp.where(left, first, second)


def evaluate(weights, inputs_ext, features):
    return pl.pallas_call(
        evaluate_kernel,
        out_shape=jax.ShapeDtypeStruct((32, 12 * QOBS), F32),
        in_specs=[VMEM] * 3,
        out_specs=VMEM,
        scratch_shapes=[pltpu.VMEM((384, 128), F32)],
        name="evaluate",
    )(weights, inputs_ext, features).astype(BF16)


def contract_last(a, b):
    return lax.dot_general(a, b, (((1,), (1,)), ((), ())), precision=HIGHEST, preferred_element_type=F32)


def fold(square):
    return jnp.concatenate([square[8 * i : 8 * i + 8, :] for i in range(4)], 1)


def unfold(tile):
    return jnp.concatenate([tile[:, 32 * i : 32 * i + 32] for i in range(4)], 0)


def sums_kernel(first, where_ref, preds_ref, target_ref, state_ref, mix_ref, out_ref):
    r = lax.broadcasted_iota(jnp.int32, (32, 32), 0)
    s = lax.broadcasted_iota(jnp.int32, (32, 32), 1)
    order = (s == (r % 4) * 8 + r // 4).astype(F32).astype(BF16)
    preds = mxu(order, preds_ref[...])
    innov = ((target_ref[...] - preds) / NOISE_STD).astype(BF16).astype(F32)
    anom = (preds - jnp.mean(preds, axis=0, keepdims=True)) / (NOISE_STD * (MEMBERS - 1) ** 0.5)
    gram = contract_last(anom, anom)
    cross = contract_last(anom, innov)
    gram_par = jnp.zeros((32, 32), F32)
    cross_par = jnp.zeros((32, 32), F32)
    for row in range(8):
        state = state_ref[:, row, :]
        if not first:
            state = jnp.dot(mix_ref[...], state, precision=HIGHEST, preferred_element_type=F32)
        par_anom = (state - jnp.mean(state, axis=0, keepdims=True)) / (MEMBERS - 1) ** 0.5
        gram_par += contract_last(par_anom, par_anom)
        cross_par += contract_last(par_anom, state)
    share = where_ref[2].astype(F32)
    out_ref[0:8, :] = fold(gram + share * gram_par)
    out_ref[8:16, :] = fold(cross - share * cross_par)


def member_sums(first, where, preds, target, slab, mix):
    whole = lambda shape: pl.BlockSpec(shape, lambda i, w: (0,) * len(shape))
    return pl.pallas_call(
        functools.partial(sums_kernel, first),
        out_shape=jax.ShapeDtypeStruct((16, 128), F32),
        grid_spec=pltpu.PrefetchScalarGridSpec(
            num_scalar_prefetch=1,
            grid=(1,),
            in_specs=[
                whole((32, 768)),
                whole((32, 768)),
                pl.BlockSpec((32, 8, 256), lambda i, w: (0, w[0], w[1])),
                whole((32, 32)),
            ],
            out_specs=whole((16, 128)),
        ),
        name="member_sums",
    )(where, preds, target, slab, mix)


def solve_kernel(first, parts_ref, mix_ref, coefficients_ref, mix_out_ref):
    both = parts_ref[0]
    for i in range(1, 16):
        both = both + parts_ref[i]
    gram, cross = unfold(both[0:8, :]), unfold(both[8:16, :])
    r = lax.broadcasted_iota(jnp.int32, (32, 32), 0)
    s = lax.broadcasted_iota(jnp.int32, (32, 32), 1)
    eye = (r == s).astype(F32)
    trace = jnp.sum(jnp.sum(gram * eye, axis=1, keepdims=True), axis=0, keepdims=True)
    system = gram + (RIDGE_SHARE / MEMBERS) * trace * eye
    table = jnp.concatenate([system, cross], 1)
    line = lax.broadcasted_iota(jnp.int32, (32, 64), 0)
    for k in range(32):
        row = table[k : k + 1, :] / table[k : k + 1, k : k + 1]
        table = jnp.where(line == k, row, table - table[:, k : k + 1] * row)
    coefficients = table[:, 32:64]
    coefficients_ref[...] = coefficients
    turned = lax.dot_general(
        coefficients, eye, (((0,), (0,)), ((), ())), precision=HIGHEST, preferred_element_type=F32
    )
    centred = turned - jnp.mean(turned, axis=1, keepdims=True)
    step = eye + centred / (MEMBERS - 1) ** 0.5
    if not first:
        step = jnp.dot(step, mix_ref[...], precision=HIGHEST, preferred_element_type=F32)
    mix_out_ref[...] = step


def solve(first, parts, mix):
    square = jax.ShapeDtypeStruct((32, 32), F32)
    return pl.pallas_call(
        functools.partial(solve_kernel, first),
        out_shape=(square, square),
        in_specs=[VMEM] * 2,
        out_specs=(VMEM, VMEM),
        name="solve",
    )(parts, mix)


def combine_kernel(count, where_ref, mix_ref, state_ref, out_ref):
    start = where_ref[0]
    for i in range(count):
        total = None
        for j in range(MEMBERS):
            part = mix_ref[start + i, j] * state_ref[j]
            total = part if total is None else total + part
        out_ref[i] = total.astype(out_ref.dtype)


def combine(count, where, mix, slab, width, dtype):
    return pl.pallas_call(
        functools.partial(combine_kernel, count),
        out_shape=jax.ShapeDtypeStruct((count, ROWS, width), dtype),
        grid_spec=pltpu.PrefetchScalarGridSpec(
            num_scalar_prefetch=1,
            grid=(1,),
            in_specs=[
                pl.BlockSpec(memory_space=pltpu.SMEM),
                pl.BlockSpec((MEMBERS, ROWS, width), lambda i, w: (0, 0, w[1])),
            ],
            out_specs=pl.BlockSpec((count, ROWS, width), lambda i, w: (0, 0, 0)),
        ),
        name="combine",
    )(where, mix, slab)


def exchange(blocks, axes):
    return lax.all_to_all(blocks, axes, 0, 0, tiled=True)


def to_all(block, axes, count):
    return exchange(jnp.broadcast_to(block[None], (count,) + block.shape), axes)


def spread_weights(plane):
    blocks = jnp.broadcast_to(plane[None], (8, 4, ROWS, 256)).reshape(32, ROWS, 256)
    half = exchange(blocks, ("y", "x")).reshape(32 * ROWS, 256)
    return to_all(half, "core", 2)


def local(ensemble, inputs, features, query_index, observed, perturb):
    z, core = lax.axis_index("z"), lax.axis_index("core")
    own = ensemble.reshape(2, ROWS, 512)
    slab = lax.all_gather(own, ("z", "core"), axis=0, tiled=True)
    plane = own.astype(BF16).reshape(2, ROWS, 2, 256).transpose(2, 0, 1, 3)
    plane = exchange(plane, "core").reshape(4, ROWS, 256)
    picks = query_index.reshape(192, QOBS).astype(BF16)
    ext = jnp.concatenate([inputs, picks, picks], 1)
    ext = lax.dynamic_slice_in_dim(ext, core * 96, 96, 0)
    ext = lax.all_gather(ext, "x", axis=0, tiled=True)
    noise = perturb.reshape(2, 2, 8, 768).transpose(2, 1, 0, 3).reshape(16, 2, 768)
    noise = exchange(noise, ("z", "core")).reshape(32, 768)
    place = (core * 8 + z) * 768
    target = lax.dynamic_slice_in_dim(observed, place, 768, 0)[None, :] + noise
    e = z * 2 + core
    shared = jnp.stack([jnp.minimum(e, 9) // 2, e % 2, (e < 10).astype(jnp.int32)])
    mix = jnp.zeros((32, 32), F32)
    for repeat in range(SUBSTEPS):
        first = repeat == 0
        if not first:
            plane = combine(4, jnp.stack([4 * z, core]), mix, slab, 256, BF16)
        weights = spread_weights(plane)
        preds = evaluate(weights, ext, features)
        preds = exchange(preds, ("x", "z"))
        part = member_sums(first, shared, preds, target, slab, mix)
        part = jnp.sum(to_all(part, ("z", "x"), 32), axis=0)
        parts = to_all(part, ("y", "core"), 16)
        coefficients, mix = solve(first, parts, mix)
    theta = combine(2, jnp.stack([2 * e, 0]), mix, slab, 512, F32)
    return (theta.reshape(2, ROWS * 512), coefficients)


def solution(mesh):
    grid = Mesh(mesh.devices.reshape(8, 2, 8, 4), ("z", "core", "y", "x"))
    member, point = ("z", "core"), ("y", "x")
    in_specs = (
        P(member, point),
        P(point, None),
        P(),
        P(point),
        P(point),
        P(member, point),
    )
    out_specs = (P(member, point), P())
    return jax.shard_map(local, mesh=grid, in_specs=in_specs, out_specs=out_specs, check_vma=False)
```

time: 677 us -> 243 us (0.36)
  blocking collectives: 583 us -> 108 us
  Pallas kernels: 0 us -> 31.7 us
  starting transfers between devices: 11.9 us -> 40.7 us
  matrix products: 24.1 us -> 0 us
  waiting for transfers between devices: 8.75 us -> 25.5 us
  other arithmetic: 21.5 us -> 6.52 us
    psum x4 -> x0, blocking collectives: 417 us -> none  [the longest x2 225 us: substep(): gram_obs, cross_obs = lax.psum((gram_obs, cross_obs), 'point')]
    all_gather x4 -> x1, blocking collectives: 70.8 us -> 18.6 us  [local(): ext = lax.all_gather(ext, 'x', axis=0, tiled=True)]
    pallas_call x0 -> x8, Pallas kernels: none -> 31.7 us  [the longest x2 9.55 us: solve(): pl.pallas_call(functools.partial(solve_kernel, first), out_shape=(square,...]
    all_to_all x1 -> x5, starting transfers between devices: 11.8 us -> 40.7 us  [exchange(): return lax.all_to_all(blocks, axes, 0, 0, tiled=True)]
    dot_general x18 -> x0, matrix products: 23.4 us -> none  [the longest x2 12.8 us: evaluate_members(): jnp.einsum('miq,ioq->mio', whole, selector, precision=lax.Precision.HIGHEST)]
    all_to_all x1 -> x5, waiting for transfers between devices: 8.71 us -> 25.4 us  [exchange(): return lax.all_to_all(blocks, axes, 0, 0, tiled=True)]
    another operation x10 -> x3, other arithmetic: 13.4 us -> 1.76 us  [the longest x1 0.6 us: local(): theta = combine(2, jnp.stack([2 * e, 0]), mix, slab, 512, F32)]
    slice x8 -> x0, local copies, waits for them, and re-layouts: 7.45 us -> none  [the longest x2 3.91 us: evaluate_members(): branch_out = gathered[:, second:third].reshape(count, WIDTH, BASIS)]
  transfers between devices with their start and end apart: 3 -> 6, of which waited for: 1 -> 4; matrix products, arithmetic and copies ran while one was open for 0% -> 4% of each run, Pallas kernels for 0% -> 2%
where the time goes in v1:
time: 243 us; the launch traced here: 242 us
  blocking collectives  108 us (44%)
  starting transfers between devices  40.7 us (17%)
  Pallas kernels  31.7 us (13%)
  waiting for transfers between devices  25.5 us (10%)
  local copies, waits for them, and re-layouts  15.3 us (6%)
  between operations  14.2 us (6%)
  other arithmetic  6.52 us (3%)
    all_to_all x7, blocking collectives, exchange(): return lax.all_to_all(blocks, axes, 0, 0, tiled=True)  89.6 us
    all_to_all x5, starting transfers between devices, exchange(): return lax.all_to_all(blocks, axes, 0, 0, tiled=True)  40.7 us
    all_to_all x5, waiting for transfers between devices, exchange(): return lax.all_to_all(blocks, axes, 0, 0, tiled=True)  25.4 us
    all_gather x1, blocking collectives, local(): ext = lax.all_gather(ext, 'x', axis=0, tiled=True)  18.6 us
    pallas_call x2, Pallas kernels, solve(): pl.pallas_call(functools.partial(solve_kernel, first), out_shape=(square,...  9.55 us
    pallas_call x2, Pallas kernels, evaluate(): pl.pallas_call(evaluate_kernel, out_shape=jax.ShapeDtypeStruct((32, 12 *...  7.89 us
    pallas_call x2, Pallas kernels, member_sums(): pl.pallas_call(functools.partial(sums_kernel, first), out_shape=jax.Shape...  7.86 us
    unnamed x17, local copies, waits for them, and re-layouts  7.52 us
  transfers between devices with their start and end apart: 6, of which 4 were waited for; matrix products, arithmetic and copies ran while one was open for 4% of the time, Pallas kernels for 2%

profile of v1, /device:TPU:1, one launch (start us, length us, event | category | flops | bytes accessed | tf_op | source)
XLA Modules:
  0.0 242.1 jit_solution(10998153075899932391)
XLA Ops:
  7.2 1.6 copy.33
  8.8 1.0 convert_element_type.20
  10.5 10.2 %all-to-all-start = ((bf16[2,2,40,256]{3,2,1,0:T(8,128)(2,1)}), bf16[2,2,40,256]{3,2,1,0:T(8,128)(2,1)S(1)}, u32[]{:S(2)}, u32[]{:S(2)}) async-start(bf16[2,2,40,256]{3,2,1,0:T(8,128)(2,1)} %copy.20), calls=%async_computation | async-start | bytes 163840 | tf_op jit(solution)/shard_map/all_to_all | solution.py:203
  20.7 0.9 copy.34
  21.8 13.6 %all_to_all.72 = f32[16,2,768]{2,1,0:T(2,128)S(1)} all-to-all(f32[16,2,768]{2,1,0:T(2,128)S(1)} %bitcast.43), channel_id=1, replica_groups=mesh['z'=8,'core'=2,'y'=8,'x'=4] {'z','core'}, dimensions={0} | all-to-all | bytes 196608 | tf_op jit(solution)/shard_map/all_to_all | solution.py:203
  35.4 0.9 broadcast_in_dim.25
  36.3 9.7 %all-to-all-start.1 = ((bf16[32,40,256]{2,1,0:T(8,128)(2,1)}), bf16[32,40,256]{2,1,0:T(8,128)(2,1)S(1)}, u32[]{:S(2)}, u32[]{:S(2)}) async-start(bf16[32,40,256]{2,1,0:T(8,128)(2,1)} %bitcast.8), calls=%async_computation.1 | async-start | bytes 1310720 | tf_op jit(solution)/shard_map/all_to_all | solution.py:203
  47.6 18.6 %all_gather.6.x_ref = bf16[384,1152]{1,0:T(8,128)(2,1)} all-gather(bf16[96,1152]{1,0:T(8,128)(2,1)S(1)} %constant_dynamic-slice_fusion), channel_id=1, replica_groups=mesh['z'=8,'core'=2,'y'=8,'x'=4] {'x'}, dimensions={0}, use_global_device_ids=true | all-gather | bytes 1105920 | tf_op jit(solution)/shard_map/all_gather | solution.py:225
  66.4 6.6 %all_to_all.73.w_ref = bf16[2,1280,256]{2,1,0:T(8,128)(2,1)} all-to-all(bf16[2,1280,256]{2,1,0:T(8,128)(2,1)S(1)} %broadcast_in_dim.27), channel_id=1, replica_groups=mesh['z'=8,'core'=2,'y'=8,'x'=4] {'core'}, dimensions={0} | all-to-all | bytes 2621440 | tf_op jit(solution)/shard_map/all_to_all | solution.py:203
  73.0 3.9 %evaluate.2 = f32[32,768]{1,0:T(8,128)} custom-call(bf16[2,1280,256]{2,1,0:T(8,128)(2,1)} %all_to_all.73.w_ref, bf16[384,1152]{1,0:T(8,128)(2,1)} %all_gather.6.x_ref, bf16[128,256]{1,0:T(8,128)(2,1)} %features_ref.3), custom_call_target="tpu_custom_call" | custom-call | tf_op jit(solution)/shard_map/evaluate/pallas_call | solution.py:72
  76.9 0.9 convert_bitcast_fusion.1
  79.6 4.5 %all-to-all-start.3 = ((bf16[32,2,384]{2,1,0:T(2,128)(2,1)}), bf16[32,2,384]{2,1,0:T(2,128)(2,1)S(1)}, u32[]{:S(2)}, u32[]{:S(2)}) async-start(bf16[32,2,384]{2,1,0:T(2,128)(2,1)} %reshape.51), calls=%async_computation.3 | async-start | bytes 98304 | tf_op jit(solution)/shard_map/all_to_all | solution.py:203
  84.8 8.2 %all-to-all-done.3 = bf16[32,2,384]{2,1,0:T(2,128)(2,1)S(1)} async-done(((bf16[32,2,384]{2,1,0:T(2,128)(2,1)}), bf16[32,2,384]{2,1,0:T(2,128)(2,1)S(1)}, u32[]{:S(2)}, u32[]{:S(2)}) %all-to-all-start.3) | async-done | bytes 49184 | tf_op jit(solution)/shard_map/all_to_all | solution.py:203
  94.3 3.2 %member_sums.2 = f32[16,128]{1,0:T(8,128)} custom-call(s32[3]{0:T(128)} %pad_add_fusion.1.where_ref, bf16[32,768]{1,0:T(8,128)(2,1)} %bitcast.47, f32[32,768]{1,0:T(8,128)} %broadcast_add_fusion.target_ref, f32[32,40,512]{2,1,0:T(8,128)} %all-gather.2.cloned.1.call-done.state_ref, f32[32,32]{1,0:T(8,128)} %broadcast_in_dim.28.mix_ref), custom_call_target="tpu_custom_call" | custom-call | tf_op jit(solution)/shard_map/member_sums/pallas_call | solution.py:119
  98.2 13.4 %all_to_all.74 = f32[32,16,128]{2,1,0:T(8,128)S(1)} all-to-all(f32[32,16,128]{2,1,0:T(8,128)S(1)} %broadcast_in_dim.29), channel_id=1, replica_groups=mesh['z'=8,'core'=2,'y'=8,'x'=4] {'z','x'}, dimensions={0} | all-to-all | bytes 524288 | tf_op jit(solution)/shard_map/all_to_all | solution.py:203
  112.3 9.2 %all-to-all-start.6 = ((f32[16,16,128]{2,1,0:T(8,128)}), f32[16,16,128]{2,1,0:T(8,128)S(1)}, u32[]{:S(2)}, u32[]{:S(2)}) async-start(f32[16,16,128]{2,1,0:T(8,128)} %broadcast_in_dim.30), calls=%async_computation.6 | async-start | bytes 262144 | tf_op jit(solution)/shard_map/all_to_all | solution.py:203
  122.1 8.6 %all-to-all-done.6.parts_ref = f32[16,16,128]{2,1,0:T(8,128)S(1)} async-done(((f32[16,16,128]{2,1,0:T(8,128)}), f32[16,16,128]{2,1,0:T(8,128)S(1)}, u32[]{:S(2)}, u32[]{:S(2)}) %all-to-all-start.6) | async-done | bytes 131104 | tf_op jit(solution)/shard_map/all_to_all | solution.py:203
  131.4 4.7 %solve.2 = (f32[32,32]{1,0:T(8,128)}, f32[32,32]{1,0:T(8,128)}) custom-call(f32[16,16,128]{2,1,0:T(8,128)} %copy-done, f32[32,32]{1,0:T(8,128)} %broadcast_in_dim.28.mix_ref), custom_call_target="tpu_custom_call" | custom-call | tf_op jit(solution)/shard_map/solve/pallas_call | solution.py:166
  136.0 3.0 %combine.2 = bf16[4,40,256]{2,1,0:T(8,128)(2,1)} custom-call(s32[2]{0:T(128)} %pad_add_fusion.2.where_ref, f32[32,32]{1,0:T(8,128)} %get-tuple-element.5.mix_ref, f32[32,40,512]{2,1,0:T(8,128)} %all-gather.2.cloned.1.call-done.state_ref), custom_call_target="tpu_custom_call" | custom-call | tf_op jit(solution)/shard_map/combine/pallas_call | solution.py:186
  139.0 0.9 broadcast_in_dim.62
  140.0 22.0 %all_to_all.75 = bf16[32,40,256]{2,1,0:T(8,128)(2,1)S(1)} all-to-all(bf16[32,40,256]{2,1,0:T(8,128)(2,1)S(1)} %bitcast.37), channel_id=1, replica_groups=mesh['z'=8,'core'=2,'y'=8,'x'=4] {'y','x'}, dimensions={0} | all-to-all | bytes 1310720 | tf_op jit(solution)/shard_map/all_to_all | solution.py:203
  162.1 7.4 %all_to_all.76.w_ref = bf16[2,1280,256]{2,1,0:T(8,128)(2,1)} all-to-all(bf16[2,1280,256]{2,1,0:T(8,128)(2,1)S(1)} %broadcast_in_dim.64), channel_id=1, replica_groups=mesh['z'=8,'core'=2,'y'=8,'x'=4] {'core'}, dimensions={0} | all-to-all | bytes 2621440 | tf_op jit(solution)/shard_map/all_to_all | solution.py:203
  169.4 3.9 %evaluate.3 = f32[32,768]{1,0:T(8,128)} custom-call(bf16[2,1280,256]{2,1,0:T(8,128)(2,1)} %all_to_all.76.w_ref, bf16[384,1152]{1,0:T(8,128)(2,1)} %all_gather.6.x_ref, bf16[128,256]{1,0:T(8,128)(2,1)} %features_ref.3), custom_call_target="tpu_custom_call" | custom-call | tf_op jit(solution)/shard_map/evaluate/pallas_call | solution.py:72
  173.4 0.9 convert_bitcast_fusion
  175.0 13.2 %all_to_all.77 = bf16[32,2,384]{2,1,0:T(2,128)(2,1)S(1)} all-to-all(bf16[32,2,384]{2,1,0:T(2,128)(2,1)S(1)} %reshape.53), channel_id=1, replica_groups=mesh['z'=8,'core'=2,'y'=8,'x'=4] {'x','z'}, dimensions={0} | all-to-all | bytes 98304 | tf_op jit(solution)/shard_map/all_to_all | solution.py:203
  188.8 4.7 %member_sums.3 = f32[16,128]{1,0:T(8,128)} custom-call(s32[3]{0:T(128)} %pad_add_fusion.1.where_ref, bf16[32,768]{1,0:T(8,128)(2,1)} %bitcast.48, f32[32,768]{1,0:T(8,128)} %broadcast_add_fusion.target_ref, f32[32,40,512]{2,1,0:T(8,128)} %all-gather.2.cloned.1.call-done.state_ref, f32[32,32]{1,0:T(8,128)} %get-tuple-element.5.mix_ref), custom_call_target="tpu_custom_call" | custom-call | tf_op jit(solution)/shard_map/member_sums/pallas_call | solution.py:119
  194.2 13.4 %all_to_all.78 = f32[32,16,128]{2,1,0:T(8,128)S(1)} all-to-all(f32[32,16,128]{2,1,0:T(8,128)S(1)} %broadcast_in_dim.65), channel_id=1, replica_groups=mesh['z'=8,'core'=2,'y'=8,'x'=4] {'z','x'}, dimensions={0} | all-to-all | bytes 524288 | tf_op jit(solution)/shard_map/all_to_all | solution.py:203
  208.3 7.1 %all-to-all-start.11 = ((f32[16,16,128]{2,1,0:T(8,128)}), f32[16,16,128]{2,1,0:T(8,128)S(1)}, u32[]{:S(2)}, u32[]{:S(2)}) async-start(f32[16,16,128]{2,1,0:T(8,128)} %broadcast_in_dim.66), calls=%async_computation.11 | async-start | bytes 262144 | tf_op jit(solution)/shard_map/all_to_all | solution.py:203
  216.0 8.6 %all-to-all-done.11.parts_ref = f32[16,16,128]{2,1,0:T(8,128)S(1)} async-done(((f32[16,16,128]{2,1,0:T(8,128)}), f32[16,16,128]{2,1,0:T(8,128)S(1)}, u32[]{:S(2)}, u32[]{:S(2)}) %all-to-all-start.11) | async-done | bytes 131104 | tf_op jit(solution)/shard_map/all_to_all | solution.py:203
  225.3 4.9 %solve.3 = (f32[32,32]{1,0:T(8,128)}, f32[32,32]{1,0:T(8,128)}) custom-call(f32[16,16,128]{2,1,0:T(8,128)} %copy-done.1, f32[32,32]{1,0:T(8,128)} %get-tuple-element.5.mix_ref), custom_call_target="tpu_custom_call" | custom-call | tf_op jit(solution)/shard_map/solve/pallas_call | solution.py:166
  230.1 3.5 %combine.3 = f32[2,40,512]{2,1,0:T(8,128)} custom-call(s32[2]{0:T(128)} %pad_add_fusion.where_ref, f32[32,32]{1,0:T(8,128)} %get-tuple-element.6.mix_ref, f32[32,40,512]{2,1,0:T(8,128)} %all-gather.2.cloned.1.call-done.state_ref), custom_call_target="tpu_custom_call" | custom-call | tf_op jit(solution)/shard_map/combine/pallas_call | solution.py:186
  233.6 1.7 copy.28
  (44 shorter events, 13.1 us)
Async XLA Ops:
  7.2 86.5 %all-gather.2.cloned.1.call-start = ((), (), s32[]{:S(2)}) async-start(), calls=%async_computation.12 | async-start | bytes 2785280 | tf_op jit(solution)/shard_map/all_gather | solution.py:219
  10.5 11.3 %all-to-all-start = ((bf16[2,2,40,256]{3,2,1,0:T(8,128)(2,1)}), bf16[2,2,40,256]{3,2,1,0:T(8,128)(2,1)S(1)}, u32[]{:S(2)}, u32[]{:S(2)}) async-start(bf16[2,2,40,256]{3,2,1,0:T(8,128)(2,1)} %copy.20), calls=%async_computation | async-start | bytes 163840 | tf_op jit(solution)/shard_map/all_to_all | solution.py:203
  21.6 24.4 %copy-start.3 = (s32[12288]{0:T(1024)S(1)}, s32[12288]{0:T(1024)}, u32[]{:S(2)}) copy-start(s32[12288]{0:T(1024)} %param.9) | copy-start | bytes 147460
  21.6 25.3 %copy-start.2 = (bf16[192,1024]{1,0:T(8,128)(2,1)S(1)}, bf16[192,1024]{1,0:T(8,128)(2,1)}, u32[]{:S(2)}) copy-start(bf16[192,1024]{1,0:T(8,128)(2,1)} %param.7) | copy-start | bytes 1179652
  36.3 30.0 %all-to-all-start.1 = ((bf16[32,40,256]{2,1,0:T(8,128)(2,1)}), bf16[32,40,256]{2,1,0:T(8,128)(2,1)S(1)}, u32[]{:S(2)}, u32[]{:S(2)}) async-start(bf16[32,40,256]{2,1,0:T(8,128)(2,1)} %bitcast.8), calls=%async_computation.1 | async-start | bytes 1310720 | tf_op jit(solution)/shard_map/all_to_all | solution.py:203
  79.6 13.4 %all-to-all-start.3 = ((bf16[32,2,384]{2,1,0:T(2,128)(2,1)}), bf16[32,2,384]{2,1,0:T(2,128)(2,1)S(1)}, u32[]{:S(2)}, u32[]{:S(2)}) async-start(bf16[32,2,384]{2,1,0:T(2,128)(2,1)} %reshape.51), calls=%async_computation.3 | async-start | bytes 98304 | tf_op jit(solution)/shard_map/all_to_all | solution.py:203
  112.3 18.4 %all-to-all-start.6 = ((f32[16,16,128]{2,1,0:T(8,128)}), f32[16,16,128]{2,1,0:T(8,128)S(1)}, u32[]{:S(2)}, u32[]{:S(2)}) async-start(f32[16,16,128]{2,1,0:T(8,128)} %broadcast_in_dim.30), calls=%async_computation.6 | async-start | bytes 262144 | tf_op jit(solution)/shard_map/all_to_all | solution.py:203
  130.7 0.7 copy-start
  208.3 16.3 %all-to-all-start.11 = ((f32[16,16,128]{2,1,0:T(8,128)}), f32[16,16,128]{2,1,0:T(8,128)S(1)}, u32[]{:S(2)}, u32[]{:S(2)}) async-start(f32[16,16,128]{2,1,0:T(8,128)} %broadcast_in_dim.66), calls=%async_computation.11 | async-start | bytes 262144 | tf_op jit(solution)/shard_map/all_to_all | solution.py:203
  224.6 0.7 copy-start.1
Sparse Core Ops, SparseCore 0:
  10.7 49.8 all-gather.1

commit v2 on v1

v2 whole, which is shorter than its diff:
```python
import functools

import jax
import jax.numpy as jnp
from jax import lax
from jax.experimental import pallas as pl
from jax.experimental.pallas import tpu as pltpu
from jax.sharding import Mesh, PartitionSpec as P

SENSORS = 1024
WIDTH = 256
BASIS = 512
FEATS = 256
QOBS = 64
SUBSTEPS = 2
MEMBERS = 32
NOISE_STD = 0.5
RIDGE_SHARE = 0.5
ROWS = 40
NOTES = 24
F32, BF16 = jnp.float32, jnp.bfloat16
HIGHEST = lax.Precision.HIGHEST
VMEM = pl.BlockSpec(memory_space=pltpu.VMEM)
SMEM = pl.BlockSpec(memory_space=pltpu.SMEM)


def mxu(a, b):
    return jnp.dot(a, b, preferred_element_type=F32)


def prepare_kernel(where_ref, ensemble_ref, inputs_ref, picks_ref, observed_ref, perturb_ref, own_ref, plane_ref, ext_ref):
    for i in range(2):
        for e in range(16):
            for part in range(3):
                at = 768 * e + 256 * part
                row, left = 3 * (e // 2) + part, 256 * (e % 2)
                own_ref[i, row : row + 1, left : left + 256] = (
                    observed_ref[0:1, at : at + 256] + perturb_ref[i : i + 1, at : at + 256]
                )
        for row in range(ROWS):
            own_ref[i, NOTES + row : NOTES + row + 1, :] = ensemble_ref[i : i + 1, 512 * row : 512 * row + 512]
        for c in range(2):
            plane_ref[c, i] = own_ref[i, NOTES:, 256 * c : 256 * c + 256].astype(BF16)
    core = where_ref[1]
    ext_ref[:, :SENSORS] = inputs_ref[pl.ds(pl.multiple_of(core * 96, 32), 96), :]
    picks = picks_ref[pl.ds(pl.multiple_of(core * 48, 16), 48), :]
    ext_ref[:48, SENSORS:] = picks.astype(F32).astype(BF16)
    ext_ref[48:, SENSORS:] = jnp.zeros((48, 128), BF16)


def prepare(where, ensemble, inputs, picks, observed, perturb):
    return pl.pallas_call(
        prepare_kernel,
        out_shape=(
            jax.ShapeDtypeStruct((2, NOTES + ROWS, 512), F32),
            jax.ShapeDtypeStruct((2, 2, ROWS, 256), BF16),
            jax.ShapeDtypeStruct((96, SENSORS + 128), BF16),
        ),
        in_specs=[SMEM] + [VMEM] * 5,
        out_specs=(VMEM,) * 3,
        name="prepare",
    )(where, ensemble, inputs, picks, observed, perturb)


def evaluate_kernel(where_ref, own_ref, other_ref, x_ref, features_ref, out_ref, whole_ref, chosen_ref):
    r = lax.broadcasted_iota(jnp.int32, (256, 256), 0)
    s = lax.broadcasted_iota(jnp.int32, (256, 256), 1)
    mix = (s == ((r + where_ref[1]) % 2) * 128 + r // 2).astype(F32).astype(BF16)

    def narrow(start):
        both = jnp.concatenate([own_ref[start : start + 128, :], other_ref[start : start + 128, :]], 0)
        return mxu(mix, both).astype(BF16)

    branch_in, branch_mid, branch_out, trunk_in, trunk_out = 0, 512, 640, 896, 1024
    halves = (own_ref, other_ref)
    trunk_hidden = jnp.tanh(mxu(features_ref[...], narrow(trunk_in)) * FEATS ** (-0.5)).astype(BF16)
    trunk = [
        (mxu(trunk_hidden, half[trunk_out : trunk_out + 256, :]) * WIDTH ** (-0.5)).astype(BF16) for half in halves
    ]
    total = None
    for i in range(4):
        part = mxu(x_ref[:, 256 * i : 256 * i + 256], narrow(branch_in + 128 * i))
        total = part if total is None else total + part
    hidden = jnp.tanh(total * SENSORS ** (-0.5)).astype(BF16)
    hidden = jnp.tanh(mxu(hidden, narrow(branch_mid)) * WIDTH ** (-0.5)).astype(BF16)
    whole = None
    for c, half in enumerate(halves):
        branch = (mxu(hidden, half[branch_out : branch_out + 256, :]) * WIDTH ** (-0.5)).astype(BF16)
        part = lax.dot_general(branch, trunk[c], (((1,), (1,)), ((), ())), preferred_element_type=F32)
        whole = part if whole is None else whole + part
    whole_ref[...] = whole * BASIS ** (-0.5)
    left = lax.broadcasted_iota(jnp.int32, (48, 128), 1) < QOBS
    for x in range(4):
        picks = x_ref[96 * x : 96 * x + 48, SENSORS:].astype(F32).astype(jnp.int32)
        even = whole_ref[pl.ds(96 * x, 48, stride=2), :]
        odd = whole_ref[pl.ds(96 * x + 1, 48, stride=2), :]
        chosen_ref[48 * x : 48 * x + 48, :] = jnp.where(
            left,
            jnp.take_along_axis(even, picks, axis=1, mode="promise_in_bounds"),
            jnp.take_along_axis(odd, picks, axis=1, mode="promise_in_bounds"),
        )
    for j in range(6):
        for x in range(0, 4, 2):
            pair = [chosen_ref[pl.ds(48 * (x + h) + j, 8, stride=6), :] for h in range(2)]
            out_ref[8 * x : 8 * x + 16, 128 * j : 128 * j + 128] = jnp.concatenate(pair, 0).astype(BF16)


def evaluate(where, own, other, inputs_ext, features):
    return pl.pallas_call(
        evaluate_kernel,
        out_shape=jax.ShapeDtypeStruct((32, 12 * QOBS), BF16),
        in_specs=[SMEM] + [VMEM] * 4,
        out_specs=VMEM,
        scratch_shapes=[pltpu.VMEM((384, 128), F32), pltpu.VMEM((192, 128), F32)],
        name="evaluate",
    )(where, own, other, inputs_ext, features)


def fold(square):
    return jnp.concatenate([square[8 * i : 8 * i + 8, :] for i in range(4)], 1)


def unfold(tile):
    return jnp.concatenate([tile[:, 32 * i : 32 * i + 32] for i in range(4)], 0)


def sums_kernel(first, where_ref, preds_ref, target_ref, state_ref, mix_ref, out_ref):
    r = lax.broadcasted_iota(jnp.int32, (32, 32), 0)
    s = lax.broadcasted_iota(jnp.int32, (32, 32), 1)
    order = (s == (r % 4) * 8 + r // 4).astype(F32).astype(BF16)
    preds = mxu(order, preds_ref[...])
    row = where_ref[4]
    target = jnp.concatenate([target_ref[:, row + i, :] for i in range(3)], 1)
    innov = ((target - preds) / NOISE_STD).astype(BF16).astype(F32)
    anom = (preds - jnp.mean(preds, axis=0, keepdims=True)) / (NOISE_STD * (MEMBERS - 1) ** 0.5)
    state = jnp.concatenate([state_ref[:, i, :] for i in range(8)], 1)
    if not first:
        state = jnp.dot(mix_ref[...], state, precision=HIGHEST, preferred_element_type=F32)
    par_anom = (state - jnp.mean(state, axis=0, keepdims=True)) / (MEMBERS - 1) ** 0.5
    share = where_ref[6].astype(F32)
    lhs = jnp.concatenate([anom, par_anom * share], 1)
    rhs = jnp.concatenate([jnp.concatenate([anom, par_anom], 1), jnp.concatenate([innov, -state], 1)], 0)
    both = lax.dot_general(lhs, rhs, (((1,), (1,)), ((), ())), precision=HIGHEST, preferred_element_type=F32)
    packed = jnp.concatenate([fold(both[:, :32]), fold(both[:, 32:])], 0)
    for i in range(32):
        out_ref[i] = packed


def member_sums(first, where, preds, slab, mix):
    whole = lambda shape: pl.BlockSpec(shape, lambda i, w: (0,) * len(shape))
    return pl.pallas_call(
        functools.partial(sums_kernel, first),
        out_shape=jax.ShapeDtypeStruct((32, 16, 128), F32),
        grid_spec=pltpu.PrefetchScalarGridSpec(
            num_scalar_prefetch=1,
            grid=(1,),
            in_specs=[
                whole((32, 768)),
                pl.BlockSpec((32, NOTES, 256), lambda i, w: (0, 0, w[3])),
                pl.BlockSpec((32, 8, 256), lambda i, w: (0, w[5], w[7])),
                whole((32, 32)),
            ],
            out_specs=whole((32, 16, 128)),
        ),
        name="member_sums",
    )(where, preds, slab, slab, mix)


def solve_kernel(last, where_ref, parts_ref, mix_ref, slab_ref, coefficients_ref, mix_out_ref, state_ref):
    both = parts_ref[0]
    for i in range(1, 16):
        both = both + parts_ref[i]
    gram, cross = unfold(both[0:8, :]), unfold(both[8:16, :])
    r = lax.broadcasted_iota(jnp.int32, (32, 32), 0)
    s = lax.broadcasted_iota(jnp.int32, (32, 32), 1)
    eye = (r == s).astype(F32)
    trace = jnp.sum(jnp.sum(gram * eye, axis=1, keepdims=True), axis=0, keepdims=True)
    system = gram + (RIDGE_SHARE / MEMBERS) * trace * eye
    table = jnp.concatenate([system, cross], 1)
    line = lax.broadcasted_iota(jnp.int32, (32, 64), 0)
    for k in range(0, 32, 2):
        upper, lower = table[k : k + 1, :], table[k + 1 : k + 2, :]
        a, b = upper[:, k : k + 1], upper[:, k + 1 : k + 2]
        c, d = lower[:, k : k + 1], lower[:, k + 1 : k + 2]
        inverse = 1.0 / (a * d - b * c)
        new_upper = (d * upper - b * lower) * inverse
        new_lower = (a * lower - c * upper) * inverse
        rest = table - table[:, k : k + 1] * new_upper - table[:, k + 1 : k + 2] * new_lower
        table = jnp.where(line == k, new_upper, jnp.where(line == k + 1, new_lower, rest))
    coefficients = table[:, 32:64]
    coefficients_ref[...] = coefficients
    turned = lax.dot_general(
        coefficients, eye, (((0,), (0,)), ((), ())), precision=HIGHEST, preferred_element_type=F32
    )
    centred = turned - jnp.mean(turned, axis=1, keepdims=True)
    step = eye + centred / (MEMBERS - 1) ** 0.5
    step = jnp.dot(step, mix_ref[...], precision=HIGHEST, preferred_element_type=F32)
    mix_out_ref[...] = step
    count = 2 if last else 4
    rows = mix_out_ref[pl.ds(where_ref[2 if last else 0], count), :]
    left = pl.multiple_of(where_ref[1] * 256, 256)
    for i in range(count):
        total = None
        for j in range(MEMBERS):
            part = slab_ref[j, NOTES:, :] if last else slab_ref[j, NOTES:, pl.ds(left, 256)]
            part = rows[i : i + 1, j : j + 1] * part
            total = part if total is None else total + part
        if last:
            for row in range(ROWS):
                state_ref[i : i + 1, 512 * row : 512 * row + 512] = total[row : row + 1, :]
        else:
            for y in range(8):
                state_ref[y, i] = total.astype(BF16)


def solve(last, where, parts, mix, slab):
    square = jax.ShapeDtypeStruct((32, 32), F32)
    state = (
        jax.ShapeDtypeStruct((2, ROWS * 512), F32) if last else jax.ShapeDtypeStruct((8, 4, ROWS, 256), BF16)
    )
    return pl.pallas_call(
        functools.partial(solve_kernel, last),
        out_shape=(square, square, state),
        in_specs=[SMEM] + [VMEM] * 3,
        out_specs=(VMEM,) * 3,
        name="solve",
    )(where, parts, mix, slab)


def exchange(blocks, axes):
    return lax.all_to_all(blocks, axes, 0, 0, tiled=True)


def local(ensemble, inputs, features, query_index, observed, perturb):
    z, core = lax.axis_index("z"), lax.axis_index("core")
    e, block = z * 2 + core, core * 8 + z
    where = jnp.stack(
        [4 * z, core, 2 * e, block % 2, 3 * (block // 2), 3 + jnp.minimum(e, 9) // 2, (e < 10).astype(jnp.int32), e % 2]
    )
    own, plane, ext = prepare(
        where, ensemble, inputs, query_index.reshape(96, 128), observed.reshape(1, -1), perturb
    )
    slab = lax.all_gather(own, ("z", "core"), axis=0, tiled=True)
    plane = exchange(plane, "core").reshape(4, ROWS, 256)
    plane = jnp.broadcast_to(plane[None], (8, 4, ROWS, 256))
    ext = lax.all_gather(ext, "x", axis=0, tiled=True)
    mix = jnp.eye(MEMBERS, dtype=F32)
    for repeat in range(SUBSTEPS):
        half = exchange(plane.reshape(32, ROWS, 256), ("y", "x")).reshape(32 * ROWS, 256)
        other = lax.ppermute(half, "core", [(0, 1), (1, 0)])
        preds = evaluate(where, half, other, ext, features)
        preds = exchange(preds, ("x", "z"))
        parts = exchange(member_sums(repeat == 0, where, preds, slab, mix), ("z", "x"))
        part = jnp.sum(parts, axis=0)
        parts = exchange(jnp.broadcast_to(part[None], (16, 16, 128)), ("y", "core"))
        coefficients, mix, plane = solve(repeat == SUBSTEPS - 1, where, parts, mix, slab)
    return (plane, coefficients)


def solution(mesh):
    grid = Mesh(mesh.devices.reshape(8, 2, 8, 4), ("z", "core", "y", "x"))
    member, point = ("z", "core"), ("y", "x")
    in_specs = (
        P(member, point),
        P(point, None),
        P(),
        P(point),
        P(point),
        P(member, point),
    )
    out_specs = (P(member, point), P())
    return jax.shard_map(local, mesh=grid, in_specs=in_specs, out_specs=out_specs, check_vma=False)
```

time: 243 us -> 232 us (0.955)
  blocking collectives: 108 us -> 148 us
  starting transfers between devices: 40.7 us -> 18.4 us
  waiting for transfers between devices: 25.5 us -> 9.92 us
  local copies, waits for them, and re-layouts: 15.3 us -> 4.96 us
  other arithmetic: 6.52 us -> 3.55 us
    all_to_all x7 -> x8, blocking collectives: 89.6 us -> 133 us  [exchange(): return lax.all_to_all(blocks, axes, 0, 0, tiled=True)]
    all_to_all x5 -> x1, starting transfers between devices: 40.7 us -> 11.3 us  [exchange(): return lax.all_to_all(blocks, axes, 0, 0, tiled=True)]
    all_to_all x5 -> x1, waiting for transfers between devices: 25.4 us -> 8.2 us  [exchange(): return lax.all_to_all(blocks, axes, 0, 0, tiled=True)]
    ppermute x0 -> x2, starting transfers between devices: none -> 7.02 us  [local(): other = lax.ppermute(half, 'core', [(0, 1), (1, 0)])]
    broadcast_in_dim x9 -> x3, local copies, waits for them, and re-layouts: 5.36 us -> 0.06 us  [the longest x1 0.04 us: local(): plane = jnp.broadcast_to(plane[None], (8, 4, ROWS, 256))]
    all_gather x1, blocking collectives: 18.6 us -> 14.7 us  [local(): ext = lax.all_gather(ext, 'x', axis=0, tiled=True)]
    unnamed x17 -> x14, local copies, waits for them, and re-layouts: 7.52 us -> 3.7 us
    pallas_call x4 -> x3, Pallas kernels: 16 us -> 17.5 us  [the longest x2 15.5 us: solve(): pl.pallas_call(functools.partial(solve_kernel, last), out_shape=(square,...]
  transfers between devices with their start and end apart: 6 -> 4, of which waited for: 4 -> 2; matrix products, arithmetic and copies ran while one was open for 4% -> 2% of each run, Pallas kernels for 2% -> 2%
where the time goes in v2:
time: 232 us; the launch traced here: 231 us
  blocking collectives  148 us (64%)
  Pallas kernels  32.5 us (14%)
  starting transfers between devices  18.4 us (8%)
  between operations  14.2 us (6%)
  waiting for transfers between devices  9.92 us (4%)
  local copies, waits for them, and re-layouts  4.96 us (2%)
  other arithmetic  3.55 us (2%)
    all_to_all x8, blocking collectives, exchange(): return lax.all_to_all(blocks, axes, 0, 0, tiled=True)  133 us
    pallas_call x2, Pallas kernels, solve(): pl.pallas_call(functools.partial(solve_kernel, last), out_shape=(square,...  15.5 us
    all_gather x1, blocking collectives, local(): ext = lax.all_gather(ext, 'x', axis=0, tiled=True)  14.7 us
    all_to_all x1, starting transfers between devices, exchange(): return lax.all_to_all(blocks, axes, 0, 0, tiled=True)  11.3 us
    all_to_all x1, waiting for transfers between devices, exchange(): return lax.all_to_all(blocks, axes, 0, 0, tiled=True)  8.2 us
    pallas_call x2, Pallas kernels, evaluate(): pl.pallas_call(evaluate_kernel, out_shape=jax.ShapeDtypeStruct((32, 12 *...  7.85 us
    pallas_call x2, Pallas kernels, member_sums(): pl.pallas_call(functools.partial(sums_kernel, first), out_shape=jax.Shape...  7.18 us
    ppermute x2, starting transfers between devices, local(): other = lax.ppermute(half, 'core', [(0, 1), (1, 0)])  7.02 us
  transfers between devices with their start and end apart: 4, of which 2 were waited for; matrix products, arithmetic and copies ran while one was open for 2% of the time, Pallas kernels for 2%

profile of v2, /device:TPU:1, one launch (start us, length us, event | category | flops | bytes accessed | tf_op | source)
XLA Modules:
  0.0 231.3 jit_solution(9544549610388768672)
XLA Ops:
  7.2 0.0 all-gather.2.cloned.1.call-start
  7.2 0.6 stack.39.where_ref
  7.9 2.0 prepare.1
  9.9 11.3 %all_to_all.57 = bf16[2,2,40,256]{3,2,1,0:T(8,128)(2,1)S(1)} all-to-all(bf16[2,2,40,256]{3,2,1,0:T(8,128)(2,1)} %get-tuple-element.9), channel_id=1, replica_groups=mesh['z'=8,'core'=2,'y'=8,'x'=4] {'core'}, dimensions={0} | all-to-all | bytes 163840 | tf_op jit(solution)/shard_map/all_to_all | solution.py:231
  21.3 22.9 %all_to_all.58 = bf16[32,40,256]{2,1,0:T(8,128)(2,1)S(1)} all-to-all(bf16[32,40,256]{2,1,0:T(8,128)(2,1)S(1)} %bitcast.27), channel_id=1, replica_groups=mesh['z'=8,'core'=2,'y'=8,'x'=4] {'y','x'}, dimensions={0} | all-to-all | bytes 1310720 | tf_op jit(solution)/shard_map/all_to_all | solution.py:231
  44.1 4.3 %collective-permute-start = (bf16[1280,256]{1,0:T(8,128)(2,1)S(1)}, bf16[1280,256]{1,0:T(8,128)(2,1)S(1)}, u32[]{:S(2)}, u32[]{:S(2)}) collective-permute-start(bf16[1280,256]{1,0:T(8,128)(2,1)S(1)} %bitcast.23), channel_id=1, source_target_pairs={{0,32},{32,0},{1,33},{33,1},{2,34},{34,2},{3,35},{35,3},{4,36},{36... | collective-permute-start | bytes 1966088 | tf_op jit(solution)/shard_map/ppermute | solution.py:250
  48.4 14.7 %all_gather.6.x_ref = bf16[384,1152]{1,0:T(8,128)(2,1)} all-gather(bf16[96,1152]{1,0:T(8,128)(2,1)} %get-tuple-element.10), channel_id=1, replica_groups=mesh['z'=8,'core'=2,'y'=8,'x'=4] {'x'}, dimensions={0}, use_global_device_ids=true | all-gather | bytes 1105920 | tf_op jit(solution)/shard_map/all_gather | solution.py:246
  63.1 0.8 copy-done.2
  64.0 3.9 %evaluate.2 = bf16[32,768]{1,0:T(8,128)(2,1)} custom-call(s32[8]{0:T(128)} %stack.39.where_ref, bf16[1280,256]{1,0:T(8,128)(2,1)} %bitcast.24, bf16[1280,256]{1,0:T(8,128)(2,1)} %copy-done.2, bf16[384,1152]{1,0:T(8,128)(2,1)} %all_gather.6.x_ref, bf16[128,256]{1,0:T(8,128)(2,1)} %features_ref.3), custom_call_target="tpu_custom_call" | custom-call | tf_op jit(solution)/shard_map/evaluate/pallas_call | solution.py:109
  67.9 0.6 broadcast.6
  68.5 1.4 reduce
  69.9 0.6 reshape.36
  70.5 11.3 %all-to-all-start.2 = ((bf16[32,2,384]{2,1,0:T(2,128)(2,1)}), bf16[32,2,384]{2,1,0:T(2,128)(2,1)S(1)}, u32[]{:S(2)}, u32[]{:S(2)}) async-start(bf16[32,2,384]{2,1,0:T(2,128)(2,1)} %reshape.36), calls=%async_computation.2 | async-start | bytes 98304 | tf_op jit(solution)/shard_map/all_to_all | solution.py:231
  81.9 0.6 fusion.mix_ref
  82.5 8.2 %all-to-all-done.2 = bf16[32,2,384]{2,1,0:T(2,128)(2,1)S(1)} async-done(((bf16[32,2,384]{2,1,0:T(2,128)(2,1)}), bf16[32,2,384]{2,1,0:T(2,128)(2,1)S(1)}, u32[]{:S(2)}, u32[]{:S(2)}) %all-to-all-start.2) | async-done | bytes 49184 | tf_op jit(solution)/shard_map/all_to_all | solution.py:231
  90.7 0.6 copy.17
  91.4 3.5 %member_sums.2 = f32[32,16,128]{2,1,0:T(8,128)} custom-call(s32[8]{0:T(128)} %stack.39.where_ref, bf16[32,768]{1,0:T(8,128)(2,1)} %bitcast.30, f32[32,64,512]{2,1,0:T(8,128)} %all-gather.2.cloned.1.call-done.target_ref.state_ref.slab_ref, f32[32,64,512]{2,1,0:T(8,128)} %all-gather.2.cloned.1.call-done.target_ref.state_ref.slab_ref, f32[32,32]{1,0:T(8,128)} %fusion.mix_ref), custom_call_target="tpu_custom_call" | custom-call | tf_op jit(solution)/shard_map/member_sums/pallas_call | solution.py:151
  94.9 14.4 %all_to_all.59 = f32[32,16,128]{2,1,0:T(8,128)S(1)} all-to-all(f32[32,16,128]{2,1,0:T(8,128)} %member_sums.2), channel_id=1, replica_groups=mesh['z'=8,'core'=2,'y'=8,'x'=4] {'z','x'}, dimensions={0} | all-to-all | bytes 524288 | tf_op jit(solution)/shard_map/all_to_all | solution.py:231
  109.4 16.8 %all_to_all.60.parts_ref = f32[16,16,128]{2,1,0:T(8,128)} all-to-all(f32[16,16,128]{2,1,0:T(8,128)S(1)} %broadcast_in_dim.10), channel_id=1, replica_groups=mesh['z'=8,'core'=2,'y'=8,'x'=4] {'y','core'}, dimensions={0} | all-to-all | bytes 262144 | tf_op jit(solution)/shard_map/all_to_all | solution.py:231
  126.2 7.8 %solve.2 = (f32[32,32]{1,0:T(8,128)}, f32[32,32]{1,0:T(8,128)}, bf16[8,4,40,256]{3,2,1,0:T(8,128)(2,1)}) custom-call(s32[8]{0:T(128)} %stack.39.where_ref, f32[16,16,128]{2,1,0:T(8,128)} %all_to_all.60.parts_ref, f32[32,32]{1,0:T(8,128)} %fusion.mix_ref, f32[32,64,512]{2,1,0:T(8,128)} %all-gather.2.cloned.1.call-done.target_ref.state_ref.slab_ref), custom_call_target="tpu_custom_call" | custom-call | tf_op jit(solution)/shard_map/solve/pallas_call | solution.py:221
  134.0 24.0 %all_to_all.61 = bf16[32,40,256]{2,1,0:T(8,128)(2,1)S(1)} all-to-all(bf16[32,40,256]{2,1,0:T(8,128)(2,1)} %bitcast.28), channel_id=1, replica_groups=mesh['z'=8,'core'=2,'y'=8,'x'=4] {'y','x'}, dimensions={0} | all-to-all | bytes 1310720 | tf_op jit(solution)/shard_map/all_to_all | solution.py:231
  157.9 2.7 %collective-permute-start.1 = (bf16[1280,256]{1,0:T(8,128)(2,1)S(1)}, bf16[1280,256]{1,0:T(8,128)(2,1)S(1)}, u32[]{:S(2)}, u32[]{:S(2)}) collective-permute-start(bf16[1280,256]{1,0:T(8,128)(2,1)S(1)} %bitcast.25), channel_id=1, source_target_pairs={{0,32},{32,0},{1,33},{33,1},{2,34},{34,2},{3,35},{35,3},{4,36},{36... | collective-permute-start | bytes 1966088 | tf_op jit(solution)/shard_map/ppermute | solution.py:250
  160.7 1.7 collective-permute-done.1.other_ref
  162.4 0.9 copy-done.3
  163.2 3.9 %evaluate.3 = bf16[32,768]{1,0:T(8,128)(2,1)} custom-call(s32[8]{0:T(128)} %stack.39.where_ref, bf16[1280,256]{1,0:T(8,128)(2,1)} %bitcast.26, bf16[1280,256]{1,0:T(8,128)(2,1)} %copy-done.3, bf16[384,1152]{1,0:T(8,128)(2,1)} %all_gather.6.x_ref, bf16[128,256]{1,0:T(8,128)(2,1)} %features_ref.3), custom_call_target="tpu_custom_call" | custom-call | tf_op jit(solution)/shard_map/evaluate/pallas_call | solution.py:109
  167.2 1.4 reduce.1
  168.6 13.5 %all_to_all.62 = bf16[32,2,384]{2,1,0:T(2,128)(2,1)S(1)} all-to-all(bf16[32,2,384]{2,1,0:T(2,128)(2,1)S(1)} %reshape.38), channel_id=1, replica_groups=mesh['z'=8,'core'=2,'y'=8,'x'=4] {'x','z'}, dimensions={0} | all-to-all | bytes 98304 | tf_op jit(solution)/shard_map/all_to_all | solution.py:231
  182.2 0.6 copy.16
  182.8 3.7 %member_sums.3 = f32[32,16,128]{2,1,0:T(8,128)} custom-call(s32[8]{0:T(128)} %stack.39.where_ref, bf16[32,768]{1,0:T(8,128)(2,1)} %bitcast.31, f32[32,64,512]{2,1,0:T(8,128)} %all-gather.2.cloned.1.call-done.target_ref.state_ref.slab_ref, f32[32,64,512]{2,1,0:T(8,128)} %all-gather.2.cloned.1.call-done.target_ref.state_ref.slab_ref, ...), custom_call_target="tpu_custom_call" | custom-call | tf_op jit(solution)/shard_map/member_sums/pallas_call | solution.py:151
  186.5 14.4 %all_to_all.63 = f32[32,16,128]{2,1,0:T(8,128)S(1)} all-to-all(f32[32,16,128]{2,1,0:T(8,128)} %member_sums.3), channel_id=1, replica_groups=mesh['z'=8,'core'=2,'y'=8,'x'=4] {'z','x'}, dimensions={0} | all-to-all | bytes 524288 | tf_op jit(solution)/shard_map/all_to_all | solution.py:231
  200.9 15.8 %all_to_all.64.parts_ref = f32[16,16,128]{2,1,0:T(8,128)} all-to-all(f32[16,16,128]{2,1,0:T(8,128)S(1)} %broadcast_in_dim.22), channel_id=1, replica_groups=mesh['z'=8,'core'=2,'y'=8,'x'=4] {'y','core'}, dimensions={0} | all-to-all | bytes 262144 | tf_op jit(solution)/shard_map/all_to_all | solution.py:231
  216.8 7.6 %solve.3 = (f32[32,32]{1,0:T(8,128)}, f32[32,32]{1,0:T(8,128)}, f32[2,20480]{1,0:T(2,128)}) custom-call(s32[8]{0:T(128)} %stack.39.where_ref, f32[16,16,128]{2,1,0:T(8,128)} %all_to_all.64.parts_ref, f32[32,32]{1,0:T(8,128)} %get-tuple-element.13.mix_ref, f32[32,64,512]{2,1,0:T(8,128)} %all-gather.2.cloned.1.call-done.target_ref.state_ref.slab_ref), custom_call_target="tpu_custom_call" | custom-call | tf_op jit(solution)/shard_map/solve/pallas_call | solution.py:221
  (17 shorter events, 0.3 us)
Async XLA Ops:
  7.2 84.2 %all-gather.2.cloned.1.call-start = ((), (), s32[]{:S(2)}) async-start(), calls=%async_computation.9 | async-start | bytes 4456448 | tf_op jit(solution)/shard_map/all_gather | solution.py:243
  44.1 19.0 %copy-start = (bf16[32,40,256]{2,1,0:T(8,128)(2,1)}, bf16[32,40,256]{2,1,0:T(8,128)(2,1)S(1)}, u32[]{:S(2)}) copy-start(bf16[32,40,256]{2,1,0:T(8,128)(2,1)S(1)} %all_to_all.58) | copy-start | bytes 1966084
  44.1 19.0 %collective-permute-start = (bf16[1280,256]{1,0:T(8,128)(2,1)S(1)}, bf16[1280,256]{1,0:T(8,128)(2,1)S(1)}, u32[]{:S(2)}, u32[]{:S(2)}) collective-permute-start(bf16[1280,256]{1,0:T(8,128)(2,1)S(1)} %bitcast.23), channel_id=1, source_target_pairs={{0,32},{32,0},{1,33},{33,1},{2,34},{34,2},{3,35},{35,3},{4,36},{36... | collective-permute-start | bytes 1966088 | tf_op jit(solution)/shard_map/ppermute | solution.py:250
  63.1 0.9 copy-start.2
  70.5 20.2 %all-to-all-start.2 = ((bf16[32,2,384]{2,1,0:T(2,128)(2,1)}), bf16[32,2,384]{2,1,0:T(2,128)(2,1)S(1)}, u32[]{:S(2)}, u32[]{:S(2)}) async-start(bf16[32,2,384]{2,1,0:T(2,128)(2,1)} %reshape.36), calls=%async_computation.2 | async-start | bytes 98304 | tf_op jit(solution)/shard_map/all_to_all | solution.py:231
  157.9 4.4 %copy-start.1 = (bf16[32,40,256]{2,1,0:T(8,128)(2,1)}, bf16[32,40,256]{2,1,0:T(8,128)(2,1)S(1)}, u32[]{:S(2)}) copy-start(bf16[32,40,256]{2,1,0:T(8,128)(2,1)S(1)} %all_to_all.61) | copy-start | bytes 1966084
  157.9 4.4 %collective-permute-start.1 = (bf16[1280,256]{1,0:T(8,128)(2,1)S(1)}, bf16[1280,256]{1,0:T(8,128)(2,1)S(1)}, u32[]{:S(2)}, u32[]{:S(2)}) collective-permute-start(bf16[1280,256]{1,0:T(8,128)(2,1)S(1)} %bitcast.25), channel_id=1, source_target_pairs={{0,32},{32,0},{1,33},{33,1},{2,34},{34,2},{3,35},{35,3},{4,36},{36... | collective-permute-start | bytes 1966088 | tf_op jit(solution)/shard_map/ppermute | solution.py:250
  162.4 0.9 copy-start.3
Sparse Core Ops, SparseCore 0:
  10.1 51.5 all-gather.1

commit v3 on v2

--- a/solution.py
+++ b/solution.py
@@ -24,11 +24,15 @@
 SMEM = pl.BlockSpec(memory_space=pltpu.SMEM)
 
 
+def in_vmem(x):
+    return pltpu.with_memory_space_constraint(x, pltpu.VMEM)
+
+
 def mxu(a, b):
     return jnp.dot(a, b, preferred_element_type=F32)
 
 
-def prepare_kernel(where_ref, ensemble_ref, inputs_ref, picks_ref, observed_ref, perturb_ref, own_ref, plane_ref, ext_ref):
+def prepare_kernel(where_ref, ensemble_ref, inputs_ref, picks_ref, observed_ref, perturb_ref, own_ref, plane_ref, ext_ref, mix_ref):
     for i in range(2):
         for e in range(16):
             for part in range(3):
@@ -41,6 +45,9 @@
             own_ref[i, NOTES + row : NOTES + row + 1, :] = ensemble_ref[i : i + 1, 512 * row : 512 * row + 512]
         for c in range(2):
             plane_ref[c, i] = own_ref[i, NOTES:, 256 * c : 256 * c + 256].astype(BF16)
+    r = lax.broadcasted_iota(jnp.int32, (32, 32), 0)
+    s = lax.broadcasted_iota(jnp.int32, (32, 32), 1)
+    mix_ref[...] = (r == s).astype(F32)
     core = where_ref[1]
     ext_ref[:, :SENSORS] = inputs_ref[pl.ds(pl.multiple_of(core * 96, 32), 96), :]
     picks = picks_ref[pl.ds(pl.multiple_of(core * 48, 16), 48), :]
@@ -55,9 +62,10 @@
             jax.ShapeDtypeStruct((2, NOTES + ROWS, 512), F32),
             jax.ShapeDtypeStruct((2, 2, ROWS, 256), BF16),
             jax.ShapeDtypeStruct((96, SENSORS + 128), BF16),
+            jax.ShapeDtypeStruct((32, 32), F32),
         ),
         in_specs=[SMEM] + [VMEM] * 5,
-        out_specs=(VMEM,) * 3,
+        out_specs=(VMEM,) * 4,
         name="prepare",
     )(where, ensemble, inputs, picks, observed, perturb)
 
@@ -99,49 +107,53 @@
             jnp.take_along_axis(even, picks, axis=1, mode="promise_in_bounds"),
             jnp.take_along_axis(odd, picks, axis=1, mode="promise_in_bounds"),
         )
-    for j in range(6):
-        for x in range(0, 4, 2):
-            pair = [chosen_ref[pl.ds(48 * (x + h) + j, 8, stride=6), :] for h in range(2)]
-            out_ref[8 * x : 8 * x + 16, 128 * j : 128 * j + 128] = jnp.concatenate(pair, 0).astype(BF16)
+    for i in range(32):
+        out_ref[i] = chosen_ref[6 * i : 6 * i + 6, :].astype(BF16)
 
 
 def evaluate(where, own, other, inputs_ext, features):
     return pl.pallas_call(
         evaluate_kernel,
-        out_shape=jax.ShapeDtypeStruct((32, 12 * QOBS), BF16),
+        out_shape=jax.ShapeDtypeStruct((32, 6, 128), BF16),
         in_specs=[SMEM] + [VMEM] * 4,
         out_specs=VMEM,
         scratch_shapes=[pltpu.VMEM((384, 128), F32), pltpu.VMEM((192, 128), F32)],
         name="evaluate",
-    )(where, own, other, inputs_ext, features)
-
-
-def fold(square):
-    return jnp.concatenate([square[8 * i : 8 * i + 8, :] for i in range(4)], 1)
-
-
-def unfold(tile):
-    return jnp.concatenate([tile[:, 32 * i : 32 * i + 32] for i in range(4)], 0)
-
-
-def sums_kernel(first, where_ref, preds_ref, target_ref, state_ref, mix_ref, out_ref):
+    )(where, in_vmem(own), in_vmem(other), inputs_ext, features)
+
+
+def split(x):
+    high = x.astype(BF16)
+    rest = x - high.astype(F32)
+    middle = rest.astype(BF16)
+    return high, middle, (rest - middle.astype(F32)).astype(BF16)
+
+
+def sums_kernel(first, where_ref, preds_ref, target_ref, state_ref, mix_ref, out_ref, preds_f32_ref):
     r = lax.broadcasted_iota(jnp.int32, (32, 32), 0)
     s = lax.broadcasted_iota(jnp.int32, (32, 32), 1)
     order = (s == (r % 4) * 8 + r // 4).astype(F32).astype(BF16)
-    preds = mxu(order, preds_ref[...])
+    preds_f32_ref[...] = preds_ref[...].astype(F32)
+    preds = jnp.concatenate([preds_f32_ref[:, i, :] for i in range(6)], 1)
+    preds = mxu(order, preds.astype(BF16))
     row = where_ref[4]
     target = jnp.concatenate([target_ref[:, row + i, :] for i in range(3)], 1)
-    innov = ((target - preds) / NOISE_STD).astype(BF16).astype(F32)
+    innov = ((target - preds) / NOISE_STD).astype(BF16)
     anom = (preds - jnp.mean(preds, axis=0, keepdims=True)) / (NOISE_STD * (MEMBERS - 1) ** 0.5)
     state = jnp.concatenate([state_ref[:, i, :] for i in range(8)], 1)
     if not first:
         state = jnp.dot(mix_ref[...], state, precision=HIGHEST, preferred_element_type=F32)
-    par_anom = (state - jnp.mean(state, axis=0, keepdims=True)) / (MEMBERS - 1) ** 0.5
     share = where_ref[6].astype(F32)
-    lhs = jnp.concatenate([anom, par_anom * share], 1)
-    rhs = jnp.concatenate([jnp.concatenate([anom, par_anom], 1), jnp.concatenate([innov, -state], 1)], 0)
-    both = lax.dot_general(lhs, rhs, (((1,), (1,)), ((), ())), precision=HIGHEST, preferred_element_type=F32)
-    packed = jnp.concatenate([fold(both[:, :32]), fold(both[:, 32:])], 0)
+    par_anom = (state - jnp.mean(state, axis=0, keepdims=True)) * (share / (MEMBERS - 1) ** 0.5)
+    lefts = [jnp.concatenate(pair, 1) for pair in zip(split(anom), split(par_anom))]
+    nothing = jnp.zeros_like(innov)
+    rights = [jnp.concatenate(pair, 1) for pair in zip((innov, nothing, nothing), split(-state))]
+    lhs = jnp.concatenate(lefts, 0)
+    rhs = jnp.concatenate([term for pair in zip(lefts, rights) for term in pair], 0)
+    terms = lax.dot_general(lhs, rhs, (((1,), (1,)), ((), ())), preferred_element_type=F32)
+    terms = terms[0:32] + terms[32:64] + terms[64:96]
+    both = terms[:, 0:64] + terms[:, 64:128] + terms[:, 128:192]
+    packed = jnp.concatenate([both[0:16], both[16:32]], 1)
     for i in range(32):
         out_ref[i] = packed
 
@@ -155,22 +167,30 @@
             num_scalar_prefetch=1,
             grid=(1,),
             in_specs=[
-                whole((32, 768)),
+                whole((32, 6, 128)),
                 pl.BlockSpec((32, NOTES, 256), lambda i, w: (0, 0, w[3])),
                 pl.BlockSpec((32, 8, 256), lambda i, w: (0, w[5], w[7])),
                 whole((32, 32)),
             ],
             out_specs=whole((32, 16, 128)),
+            scratch_shapes=[pltpu.VMEM((32, 6, 128), F32)],
         ),
         name="member_sums",
-    )(where, preds, slab, slab, mix)
-
-
-def solve_kernel(last, where_ref, parts_ref, mix_ref, slab_ref, coefficients_ref, mix_out_ref, state_ref):
+    )(where, in_vmem(preds), slab, slab, mix)
+
+
+def solve_kernel(last, where_ref, parts_ref, mix_ref, slab_ref, coefficients_ref, mix_out_ref, state_ref, held_ref, sem):
+    if last:
+        wanted = slab_ref.at[:, pl.ds(NOTES, ROWS), :]
+    else:
+        wanted = slab_ref.at[:, pl.ds(NOTES, ROWS), pl.ds(pl.multiple_of(where_ref[1] * 256, 256), 256)]
+    fetch = pltpu.make_async_copy(wanted, held_ref, sem)
+    fetch.start()
     both = parts_ref[0]
     for i in range(1, 16):
         both = both + parts_ref[i]
-    gram, cross = unfold(both[0:8, :]), unfold(both[8:16, :])
+    gram = jnp.concatenate([both[:, 0:32], both[:, 64:96]], 0)
+    cross = jnp.concatenate([both[:, 32:64], both[:, 96:128]], 0)
     r = lax.broadcasted_iota(jnp.int32, (32, 32), 0)
     s = lax.broadcasted_iota(jnp.int32, (32, 32), 1)
     eye = (r == s).astype(F32)
@@ -179,13 +199,14 @@
     table = jnp.concatenate([system, cross], 1)
     line = lax.broadcasted_iota(jnp.int32, (32, 64), 0)
     for k in range(0, 32, 2):
+        first = jnp.broadcast_to(table[:, k : k + 1], (32, 64))
+        second = jnp.broadcast_to(table[:, k + 1 : k + 2], (32, 64))
         upper, lower = table[k : k + 1, :], table[k + 1 : k + 2, :]
-        a, b = upper[:, k : k + 1], upper[:, k + 1 : k + 2]
-        c, d = lower[:, k : k + 1], lower[:, k + 1 : k + 2]
+        a, b, c, d = first[k : k + 1], second[k : k + 1], first[k + 1 : k + 2], second[k + 1 : k + 2]
         inverse = 1.0 / (a * d - b * c)
         new_upper = (d * upper - b * lower) * inverse
         new_lower = (a * lower - c * upper) * inverse
-        rest = table - table[:, k : k + 1] * new_upper - table[:, k + 1 : k + 2] * new_lower
+        rest = table - first * new_upper - second * new_lower
         table = jnp.where(line == k, new_upper, jnp.where(line == k + 1, new_lower, rest))
     coefficients = table[:, 32:64]
     coefficients_ref[...] = coefficients
@@ -194,16 +215,16 @@
     )
     centred = turned - jnp.mean(turned, axis=1, keepdims=True)
     step = eye + centred / (MEMBERS - 1) ** 0.5
-    step = jnp.dot(step, mix_ref[...], precision=HIGHEST, preferred_element_type=F32)
+    if last:
+        step = jnp.dot(step, mix_ref[...], precision=HIGHEST, preferred_element_type=F32)
     mix_out_ref[...] = step
     count = 2 if last else 4
     rows = mix_out_ref[pl.ds(where_ref[2 if last else 0], count), :]
-    left = pl.multiple_of(where_ref[1] * 256, 256)
+    fetch.wait()
     for i in range(count):
         total = None
         for j in range(MEMBERS):
-            part = slab_ref[j, NOTES:, :] if last else slab_ref[j, NOTES:, pl.ds(left, 256)]
-            part = rows[i : i + 1, j : j + 1] * part
+            part = rows[i : i + 1, j : j + 1] * held_ref[j]
             total = part if total is None else total + part
         if last:
             for row in range(ROWS):
@@ -221,10 +242,11 @@
     return pl.pallas_call(
         functools.partial(solve_kernel, last),
         out_shape=(square, square, state),
-        in_specs=[SMEM] + [VMEM] * 3,
+        in_specs=[SMEM] + [VMEM] * 2 + [pl.BlockSpec(memory_space=pl.ANY)],
         out_specs=(VMEM,) * 3,
+        scratch_shapes=[pltpu.VMEM((MEMBERS, ROWS, 512 if last else 256), F32), pltpu.SemaphoreType.DMA],
         name="solve",
-    )(where, parts, mix, slab)
+    )(where, in_vmem(parts), mix, slab)
 
 
 def exchange(blocks, axes):
@@ -237,16 +259,16 @@
     where = jnp.stack(
         [4 * z, core, 2 * e, block % 2, 3 * (block // 2), 3 + jnp.minimum(e, 9) // 2, (e < 10).astype(jnp.int32), e % 2]
     )
-    own, plane, ext = prepare(
+    own, plane, ext, mix = prepare(
         where, ensemble, inputs, query_index.reshape(96, 128), observed.reshape(1, -1), perturb
     )
     slab = lax.all_gather(own, ("z", "core"), axis=0, tiled=True)
     plane = exchange(plane, "core").reshape(4, ROWS, 256)
     plane = jnp.broadcast_to(plane[None], (8, 4, ROWS, 256))
     ext = lax.all_gather(ext, "x", axis=0, tiled=True)
-    mix = jnp.eye(MEMBERS, dtype=F32)
     for repeat in range(SUBSTEPS):
         half = exchange(plane.reshape(32, ROWS, 256), ("y", "x")).reshape(32 * ROWS, 256)
+        half, ext = lax.optimization_barrier((half, ext))
         other = lax.ppermute(half, "core", [(0, 1), (1, 0)])
         preds = evaluate(where, half, other, ext, features)
         preds = exchange(preds, ("x", "z"))

time: 232 us -> 208 us (0.90)
  Pallas kernels: 32.5 us -> 24.3 us
  starting transfers between devices: 18.4 us -> 11.3 us
  waiting for transfers between devices: 9.92 us -> 4 us
  other arithmetic: 3.55 us -> 0.07 us
  local copies, waits for them, and re-layouts: 4.96 us -> 1.56 us
  blocking collectives: 148 us -> 151 us
    all_to_all x1, waiting for transfers between devices: 8.2 us -> 0.58 us  [exchange(): return lax.all_to_all(blocks, axes, 0, 0, tiled=True)]
    pallas_call x2, Pallas kernels: 15.5 us -> 8.26 us  [solve(): pl.pallas_call(functools.partial(solve_kernel, last), out_shape=(square,...]
    all_to_all x1, starting transfers between devices: 11.3 us -> 4.3 us  [exchange(): return lax.all_to_all(blocks, axes, 0, 0, tiled=True)]
    unnamed x14 -> x0, local copies, waits for them, and re-layouts: 3.7 us -> none
    all_gather x1, blocking collectives: 14.7 us -> 18.2 us  [local(): ext = lax.all_gather(ext, 'x', axis=0, tiled=True)]
    all_to_all x2 -> x0, other arithmetic: 2.87 us -> none  [exchange(): return lax.all_to_all(blocks, axes, 0, 0, tiled=True)]
  transfers between devices with their start and end apart: 4 -> 4, of which waited for: 2 -> 3; matrix products, arithmetic and copies ran while one was open for 2% -> 0% of each run, Pallas kernels for 2% -> 2%
where the time goes in v3:
time: 208 us; the launch traced here: 206 us
  blocking collectives  151 us (73%)
  Pallas kernels  24.3 us (12%)
  between operations  14.2 us (7%)
  starting transfers between devices  11.3 us (5%)
  waiting for transfers between devices  4 us (2%)
    all_to_all x8, blocking collectives, exchange(): return lax.all_to_all(blocks, axes, 0, 0, tiled=True)  133 us
    all_gather x1, blocking collectives, local(): ext = lax.all_gather(ext, 'x', axis=0, tiled=True)  18.2 us
    pallas_call x2, Pallas kernels, solve(): pl.pallas_call(functools.partial(solve_kernel, last), out_shape=(square,...  8.26 us
    pallas_call x2, Pallas kernels, evaluate(): pl.pallas_call(evaluate_kernel, out_shape=jax.ShapeDtypeStruct((32, 6, 12...  7.1 us
    ppermute x2, starting transfers between devices, local(): other = lax.ppermute(half, 'core', [(0, 1), (1, 0)])  7 us
    pallas_call x2, Pallas kernels, member_sums(): pl.pallas_call(functools.partial(sums_kernel, first), out_shape=jax.Shape...  6.87 us
    all_to_all x1, starting transfers between devices, exchange(): return lax.all_to_all(blocks, axes, 0, 0, tiled=True)  4.3 us
  transfers between devices with their start and end apart: 4, of which 3 were waited for; matrix products, arithmetic and copies ran while one was open for 0% of the time, Pallas kernels for 2%

profile of v3, /device:TPU:1, one launch (start us, length us, event | category | flops | bytes accessed | tf_op | source)
XLA Modules:
  0.0 206.5 jit_solution(10413405986032599246)
XLA Ops:
  7.2 0.0 all-gather.2.cloned.1.call-start
  7.3 0.6 stack.39.where_ref
  7.9 2.1 prepare.1
  9.9 0.0 all-gather.2.cloned.1.call-update
  10.0 11.3 %all_to_all.45 = bf16[2,2,40,256]{3,2,1,0:T(8,128)(2,1)S(1)} all-to-all(bf16[2,2,40,256]{3,2,1,0:T(8,128)(2,1)} %get-tuple-element.14), channel_id=1, replica_groups=mesh['z'=8,'core'=2,'y'=8,'x'=4] {'core'}, dimensions={0} | all-to-all | bytes 163840 | tf_op jit(solution)/shard_map/all_to_all | solution.py:253
  21.2 0.9 broadcast_in_dim.9
  22.2 4.3 %all-to-all-start.1 = ((bf16[32,40,256]{2,1,0:T(8,128)(2,1)}), bf16[32,40,256]{2,1,0:T(8,128)(2,1)S(1)}, u32[]{:S(2)}, u32[]{:S(2)}) async-start(bf16[32,40,256]{2,1,0:T(8,128)(2,1)} %bitcast.11), calls=%async_computation.1 | async-start | bytes 1310720 | tf_op jit(solution)/shard_map/all_to_all | solution.py:253
  26.5 18.2 %all_gather.6.x_ref = bf16[384,1152]{1,0:T(8,128)(2,1)} all-gather(bf16[96,1152]{1,0:T(8,128)(2,1)} %get-tuple-element.15), channel_id=1, replica_groups=mesh['z'=8,'core'=2,'y'=8,'x'=4] {'x'}, dimensions={0}, use_global_device_ids=true | all-gather | bytes 1105920 | tf_op jit(solution)/shard_map/all_gather | solution.py:268
  44.7 0.6 all-to-all-done.1
  45.3 4.3 %collective-permute-start = (bf16[1280,256]{1,0:T(8,128)(2,1)S(1)}, bf16[1280,256]{1,0:T(8,128)(2,1)S(1)}, u32[]{:S(2)}, u32[]{:S(2)}) collective-permute-start(bf16[1280,256]{1,0:T(8,128)(2,1)S(1)} %bitcast.15), channel_id=1, source_target_pairs={{0,32},{32,0},{1,33},{33,1},{2,34},{34,2},{3,35},{35,3},{4,36},{36... | collective-permute-start | bytes 1966088 | tf_op jit(solution)/shard_map/ppermute | solution.py:272
  49.5 1.7 collective-permute-done.other_ref
  51.2 3.6 %evaluate.2 = bf16[32,6,128]{2,1,0:T(8,128)(2,1)} custom-call(s32[8]{0:T(128)} %stack.39.where_ref, bf16[1280,256]{1,0:T(8,128)(2,1)S(1)} %bitcast.16, bf16[1280,256]{1,0:T(8,128)(2,1)S(1)} %collective-permute-done.other_ref, bf16[384,1152]{1,0:T(8,128)(2,1)} %all_gather.6.x_ref, bf16[128,256]{1,0:T(8,128)(2,1)} %features_ref.3), custom_call_target="tpu_custom_call" | custom-call | tf_op jit(solution)/shard_map/evaluate/pallas_call | solution.py:115
  54.8 21.4 %all_to_all.46.preds_ref = bf16[32,6,128]{2,1,0:T(8,128)(2,1)S(1)} all-to-all(bf16[32,6,128]{2,1,0:T(8,128)(2,1)} %evaluate.2), channel_id=1, replica_groups=mesh['z'=8,'core'=2,'y'=8,'x'=4] {'x','z'}, dimensions={0} | all-to-all | bytes 98304 | tf_op jit(solution)/shard_map/all_to_all | solution.py:253
  76.2 0.0 all-gather.2.cloned.1.call-done.target_ref.state_ref.slab_ref
  76.2 3.4 %member_sums.2 = f32[32,16,128]{2,1,0:T(8,128)} custom-call(s32[8]{0:T(128)} %stack.39.where_ref, bf16[32,6,128]{2,1,0:T(8,128)(2,1)S(1)} %all_to_all.46.preds_ref, f32[32,64,512]{2,1,0:T(8,128)} %all-gather.2.cloned.1.call-done.target_ref.state_ref.slab_ref, f32[32,64,512]{2,1,0:T(8,128)} %all-gather.2.cloned.1.call-done.target_ref.state_ref.slab_ref, ...), custom_call_target="tpu_custom_call" | custom-call | tf_op jit(solution)/shard_map/member_sums/pallas_call | solution.py:163
  79.6 14.4 %all_to_all.47 = f32[32,16,128]{2,1,0:T(8,128)S(1)} all-to-all(f32[32,16,128]{2,1,0:T(8,128)} %member_sums.2), channel_id=1, replica_groups=mesh['z'=8,'core'=2,'y'=8,'x'=4] {'z','x'}, dimensions={0} | all-to-all | bytes 524288 | tf_op jit(solution)/shard_map/all_to_all | solution.py:253
  94.1 18.3 %all_to_all.48.parts_ref = f32[16,16,128]{2,1,0:T(8,128)S(1)} all-to-all(f32[16,16,128]{2,1,0:T(8,128)S(1)} %broadcast_in_dim.10), channel_id=1, replica_groups=mesh['z'=8,'core'=2,'y'=8,'x'=4] {'y','core'}, dimensions={0} | all-to-all | bytes 262144 | tf_op jit(solution)/shard_map/all_to_all | solution.py:253
  112.4 4.1 %solve.2 = (f32[32,32]{1,0:T(8,128)}, f32[32,32]{1,0:T(8,128)}, bf16[8,4,40,256]{3,2,1,0:T(8,128)(2,1)}) custom-call(s32[8]{0:T(128)} %stack.39.where_ref, f32[16,16,128]{2,1,0:T(8,128)S(1)} %all_to_all.48.parts_ref, f32[32,32]{1,0:T(8,128)} %get-tuple-element.19.mix_ref, f32[32,64,512]{2,1,0:T(8,128)} %all-gather.2.cloned.1.call-done.target_ref.state_ref.slab_ref), custom_call_target="tpu_custom_call" | custom-call | tf_op jit(solution)/shard_map/solve/pallas_call | solution.py:242
  116.5 24.0 %all_to_all.49 = bf16[32,40,256]{2,1,0:T(8,128)(2,1)S(1)} all-to-all(bf16[32,40,256]{2,1,0:T(8,128)(2,1)} %bitcast.19), channel_id=1, replica_groups=mesh['z'=8,'core'=2,'y'=8,'x'=4] {'y','x'}, dimensions={0} | all-to-all | bytes 1310720 | tf_op jit(solution)/shard_map/all_to_all | solution.py:253
  140.5 2.7 %collective-permute-start.1 = (bf16[1280,256]{1,0:T(8,128)(2,1)S(1)}, bf16[1280,256]{1,0:T(8,128)(2,1)S(1)}, u32[]{:S(2)}, u32[]{:S(2)}) collective-permute-start(bf16[1280,256]{1,0:T(8,128)(2,1)S(1)} %bitcast.17), channel_id=1, source_target_pairs={{0,32},{32,0},{1,33},{33,1},{2,34},{34,2},{3,35},{35,3},{4,36},{36... | collective-permute-start | bytes 1966088 | tf_op jit(solution)/shard_map/ppermute | solution.py:272
  143.2 1.7 collective-permute-done.1.other_ref
  144.9 3.5 %evaluate.3 = bf16[32,6,128]{2,1,0:T(8,128)(2,1)} custom-call(s32[8]{0:T(128)} %stack.39.where_ref, bf16[1280,256]{1,0:T(8,128)(2,1)S(1)} %bitcast.18, bf16[1280,256]{1,0:T(8,128)(2,1)S(1)} %collective-permute-done.1.other_ref, bf16[384,1152]{1,0:T(8,128)(2,1)} %all_gather.6.x_ref, bf16[128,256]{1,0:T(8,128)(2,1)} %features_ref.3), custom_call_target="tpu_custom_call" | custom-call | tf_op jit(solution)/shard_map/evaluate/pallas_call | solution.py:115
  148.5 13.9 %all_to_all.50.preds_ref = bf16[32,6,128]{2,1,0:T(8,128)(2,1)S(1)} all-to-all(bf16[32,6,128]{2,1,0:T(8,128)(2,1)} %evaluate.3), channel_id=1, replica_groups=mesh['z'=8,'core'=2,'y'=8,'x'=4] {'x','z'}, dimensions={0} | all-to-all | bytes 98304 | tf_op jit(solution)/shard_map/all_to_all | solution.py:253
  162.4 3.5 %member_sums.3 = f32[32,16,128]{2,1,0:T(8,128)} custom-call(s32[8]{0:T(128)} %stack.39.where_ref, bf16[32,6,128]{2,1,0:T(8,128)(2,1)S(1)} %all_to_all.50.preds_ref, f32[32,64,512]{2,1,0:T(8,128)} %all-gather.2.cloned.1.call-done.target_ref.state_ref.slab_ref, f32[32,64,512]{2,1,0:T(8,128)} %all-gather.2.cloned.1.call-done.target_ref.state_ref.slab_ref, ...), custom_call_target="tpu_custom_call" | custom-call | tf_op jit(solution)/shard_map/member_sums/pallas_call | solution.py:163
  165.9 14.3 %all_to_all.51 = f32[32,16,128]{2,1,0:T(8,128)S(1)} all-to-all(f32[32,16,128]{2,1,0:T(8,128)} %member_sums.3), channel_id=1, replica_groups=mesh['z'=8,'core'=2,'y'=8,'x'=4] {'z','x'}, dimensions={0} | all-to-all | bytes 524288 | tf_op jit(solution)/shard_map/all_to_all | solution.py:253
  180.3 15.2 %all_to_all.52.parts_ref = f32[16,16,128]{2,1,0:T(8,128)S(1)} all-to-all(f32[16,16,128]{2,1,0:T(8,128)S(1)} %broadcast_in_dim.22), channel_id=1, replica_groups=mesh['z'=8,'core'=2,'y'=8,'x'=4] {'y','core'}, dimensions={0} | all-to-all | bytes 262144 | tf_op jit(solution)/shard_map/all_to_all | solution.py:253
  195.5 4.1 %solve.3 = (f32[32,32]{1,0:T(8,128)}, f32[32,32]{1,0:T(8,128)}, f32[2,20480]{1,0:T(2,128)}) custom-call(s32[8]{0:T(128)} %stack.39.where_ref, f32[16,16,128]{2,1,0:T(8,128)S(1)} %all_to_all.52.parts_ref, f32[32,32]{1,0:T(8,128)} %get-tuple-element.23.mix_ref, f32[32,64,512]{2,1,0:T(8,128)} %all-gather.2.cloned.1.call-done.target_ref.state_ref.slab_ref), custom_call_target="tpu_custom_call" | custom-call | tf_op jit(solution)/shard_map/solve/pallas_call | solution.py:242
  (4 shorter events, 0.1 us)
Async XLA Ops:
  7.2 69.1 %all-gather.2.cloned.1.call-start = ((), (), s32[]{:S(2)}) async-start(), calls=%async_computation.9 | async-start | bytes 4456448 | tf_op jit(solution)/shard_map/all_gather | solution.py:265
  22.2 23.1 %all-to-all-start.1 = ((bf16[32,40,256]{2,1,0:T(8,128)(2,1)}), bf16[32,40,256]{2,1,0:T(8,128)(2,1)S(1)}, u32[]{:S(2)}, u32[]{:S(2)}) async-start(bf16[32,40,256]{2,1,0:T(8,128)(2,1)} %bitcast.11), calls=%async_computation.1 | async-start | bytes 1310720 | tf_op jit(solution)/shard_map/all_to_all | solution.py:253
  45.3 6.0 %collective-permute-start = (bf16[1280,256]{1,0:T(8,128)(2,1)S(1)}, bf16[1280,256]{1,0:T(8,128)(2,1)S(1)}, u32[]{:S(2)}, u32[]{:S(2)}) collective-permute-start(bf16[1280,256]{1,0:T(8,128)(2,1)S(1)} %bitcast.15), channel_id=1, source_target_pairs={{0,32},{32,0},{1,33},{33,1},{2,34},{34,2},{3,35},{35,3},{4,36},{36... | collective-permute-start | bytes 1966088 | tf_op jit(solution)/shard_map/ppermute | solution.py:272
  140.5 4.4 %collective-permute-start.1 = (bf16[1280,256]{1,0:T(8,128)(2,1)S(1)}, bf16[1280,256]{1,0:T(8,128)(2,1)S(1)}, u32[]{:S(2)}, u32[]{:S(2)}) collective-permute-start(bf16[1280,256]{1,0:T(8,128)(2,1)S(1)} %bitcast.17), channel_id=1, source_target_pairs={{0,32},{32,0},{1,33},{33,1},{2,34},{34,2},{3,35},{35,3},{4,36},{36... | collective-permute-start | bytes 1966088 | tf_op jit(solution)/shard_map/ppermute | solution.py:272
Sparse Core Ops, SparseCore 0:
  10.1 51.5 all-gather.1

commit v4 on v3

--- a/solution.py
+++ b/solution.py
@@ -17,7 +17,7 @@
 NOISE_STD = 0.5
 RIDGE_SHARE = 0.5
 ROWS = 40
-NOTES = 24
+NOTES = 32
 F32, BF16 = jnp.float32, jnp.bfloat16
 HIGHEST = lax.Precision.HIGHEST
 VMEM = pl.BlockSpec(memory_space=pltpu.VMEM)
@@ -32,23 +32,21 @@
     return jnp.dot(a, b, preferred_element_type=F32)
 
 
-def prepare_kernel(where_ref, ensemble_ref, inputs_ref, picks_ref, observed_ref, perturb_ref, own_ref, plane_ref, ext_ref, mix_ref):
+def prepare_kernel(where_ref, ensemble_ref, inputs_ref, picks_ref, observed_ref, perturb_ref, own_ref, keep_ref, give_ref, ext_ref):
+    core = where_ref[1]
     for i in range(2):
         for e in range(16):
-            for part in range(3):
-                at = 768 * e + 256 * part
-                row, left = 3 * (e // 2) + part, 256 * (e % 2)
-                own_ref[i, row : row + 1, left : left + 256] = (
-                    observed_ref[0:1, at : at + 256] + perturb_ref[i : i + 1, at : at + 256]
+            for part in range(6):
+                at = 768 * e + 128 * part
+                row, left = 8 * (e // 4) + part, 128 * (e % 4)
+                own_ref[i, row : row + 1, left : left + 128] = (
+                    observed_ref[0:1, at : at + 128] + perturb_ref[i : i + 1, at : at + 128]
                 )
+            own_ref[i, 8 * (e // 4) + 6 : 8 * (e // 4) + 8, 128 * (e % 4) : 128 * (e % 4) + 128] = jnp.zeros((2, 128), F32)
         for row in range(ROWS):
             own_ref[i, NOTES + row : NOTES + row + 1, :] = ensemble_ref[i : i + 1, 512 * row : 512 * row + 512]
-        for c in range(2):
-            plane_ref[c, i] = own_ref[i, NOTES:, 256 * c : 256 * c + 256].astype(BF16)
-    r = lax.broadcasted_iota(jnp.int32, (32, 32), 0)
-    s = lax.broadcasted_iota(jnp.int32, (32, 32), 1)
-    mix_ref[...] = (r == s).astype(F32)
-    core = where_ref[1]
+        keep_ref[i] = own_ref[i, NOTES:, pl.ds(pl.multiple_of(core * 256, 256), 256)].astype(BF16)
+        give_ref[i] = own_ref[i, NOTES:, pl.ds(pl.multiple_of((1 - core) * 256, 256), 256)].astype(BF16)
     ext_ref[:, :SENSORS] = inputs_ref[pl.ds(pl.multiple_of(core * 96, 32), 96), :]
     picks = picks_ref[pl.ds(pl.multiple_of(core * 48, 16), 48), :]
     ext_ref[:48, SENSORS:] = picks.astype(F32).astype(BF16)
@@ -60,9 +58,9 @@
         prepare_kernel,
         out_shape=(
             jax.ShapeDtypeStruct((2, NOTES + ROWS, 512), F32),
-            jax.ShapeDtypeStruct((2, 2, ROWS, 256), BF16),
-            jax.ShapeDtypeStruct((96, SENSORS + 128), BF16),
-            jax.ShapeDtypeStruct((32, 32), F32),
+            pltpu.VMEM((2, ROWS, 256), BF16),
+            pltpu.VMEM((2, ROWS, 256), BF16),
+            pltpu.VMEM((96, SENSORS + 128), BF16),
         ),
         in_specs=[SMEM] + [VMEM] * 5,
         out_specs=(VMEM,) * 4,
@@ -114,12 +112,12 @@
 def evaluate(where, own, other, inputs_ext, features):
     return pl.pallas_call(
         evaluate_kernel,
-        out_shape=jax.ShapeDtypeStruct((32, 6, 128), BF16),
+        out_shape=pltpu.VMEM((32, 6, 128), BF16),
         in_specs=[SMEM] + [VMEM] * 4,
         out_specs=VMEM,
         scratch_shapes=[pltpu.VMEM((384, 128), F32), pltpu.VMEM((192, 128), F32)],
         name="evaluate",
-    )(where, in_vmem(own), in_vmem(other), inputs_ext, features)
+    )(where, in_vmem(own), in_vmem(other), in_vmem(inputs_ext), features)
 
 
 def split(x):
@@ -129,20 +127,20 @@
     return high, middle, (rest - middle.astype(F32)).astype(BF16)
 
 
-def sums_kernel(first, where_ref, preds_ref, target_ref, state_ref, mix_ref, out_ref, preds_f32_ref):
+def sums_kernel(where_ref, preds_ref, target_ref, state_ref, *rest):
+    *mix_ref, out_ref, preds_f32_ref = rest
     r = lax.broadcasted_iota(jnp.int32, (32, 32), 0)
     s = lax.broadcasted_iota(jnp.int32, (32, 32), 1)
     order = (s == (r % 4) * 8 + r // 4).astype(F32).astype(BF16)
     preds_f32_ref[...] = preds_ref[...].astype(F32)
     preds = jnp.concatenate([preds_f32_ref[:, i, :] for i in range(6)], 1)
     preds = mxu(order, preds.astype(BF16))
-    row = where_ref[4]
-    target = jnp.concatenate([target_ref[:, row + i, :] for i in range(3)], 1)
+    target = jnp.concatenate([target_ref[:, i, :] for i in range(6)], 1)
     innov = ((target - preds) / NOISE_STD).astype(BF16)
     anom = (preds - jnp.mean(preds, axis=0, keepdims=True)) / (NOISE_STD * (MEMBERS - 1) ** 0.5)
     state = jnp.concatenate([state_ref[:, i, :] for i in range(8)], 1)
-    if not first:
-        state = jnp.dot(mix_ref[...], state, precision=HIGHEST, preferred_element_type=F32)
+    if mix_ref:
+        state = jnp.dot(mix_ref[0][...], state, precision=HIGHEST, preferred_element_type=F32)
     share = where_ref[6].astype(F32)
     par_anom = (state - jnp.mean(state, axis=0, keepdims=True)) * (share / (MEMBERS - 1) ** 0.5)
     lefts = [jnp.concatenate(pair, 1) for pair in zip(split(anom), split(par_anom))]
@@ -158,28 +156,29 @@
         out_ref[i] = packed
 
 
-def member_sums(first, where, preds, slab, mix):
+def member_sums(where, preds, slab, *mix):
     whole = lambda shape: pl.BlockSpec(shape, lambda i, w: (0,) * len(shape))
     return pl.pallas_call(
-        functools.partial(sums_kernel, first),
-        out_shape=jax.ShapeDtypeStruct((32, 16, 128), F32),
+        sums_kernel,
+        out_shape=pltpu.VMEM((32, 16, 128), F32),
         grid_spec=pltpu.PrefetchScalarGridSpec(
             num_scalar_prefetch=1,
             grid=(1,),
             in_specs=[
                 whole((32, 6, 128)),
-                pl.BlockSpec((32, NOTES, 256), lambda i, w: (0, 0, w[3])),
+                pl.BlockSpec((32, 8, 128), lambda i, w: (0, w[3], w[4])),
                 pl.BlockSpec((32, 8, 256), lambda i, w: (0, w[5], w[7])),
-                whole((32, 32)),
-            ],
+            ]
+            + [whole((32, 32)) for _ in mix],
             out_specs=whole((32, 16, 128)),
             scratch_shapes=[pltpu.VMEM((32, 6, 128), F32)],
         ),
         name="member_sums",
-    )(where, in_vmem(preds), slab, slab, mix)
-
-
-def solve_kernel(last, where_ref, parts_ref, mix_ref, slab_ref, coefficients_ref, mix_out_ref, state_ref, held_ref, sem):
+    )(where, in_vmem(preds), slab, slab, *mix)
+
+
+def solve_kernel(last, where_ref, parts_ref, slab_ref, *rest):
+    *mix_ref, given_ref, state_ref, held_ref, step_ref, sem = rest
     if last:
         wanted = slab_ref.at[:, pl.ds(NOTES, ROWS), :]
     else:
@@ -209,17 +208,17 @@
         rest = table - first * new_upper - second * new_lower
         table = jnp.where(line == k, new_upper, jnp.where(line == k + 1, new_lower, rest))
     coefficients = table[:, 32:64]
-    coefficients_ref[...] = coefficients
     turned = lax.dot_general(
         coefficients, eye, (((0,), (0,)), ((), ())), precision=HIGHEST, preferred_element_type=F32
     )
     centred = turned - jnp.mean(turned, axis=1, keepdims=True)
     step = eye + centred / (MEMBERS - 1) ** 0.5
-    if last:
-        step = jnp.dot(step, mix_ref[...], precision=HIGHEST, preferred_element_type=F32)
-    mix_out_ref[...] = step
+    if mix_ref:
+        step = jnp.dot(step, mix_ref[0][...], precision=HIGHEST, preferred_element_type=F32)
+    step_ref[...] = step
+    given_ref[...] = coefficients if last else step
     count = 2 if last else 4
-    rows = mix_out_ref[pl.ds(where_ref[2 if last else 0], count), :]
+    rows = step_ref[pl.ds(where_ref[2 if last else 0], count), :]
     fetch.wait()
     for i in range(count):
         total = None
@@ -234,49 +233,60 @@
                 state_ref[y, i] = total.astype(BF16)
 
 
-def solve(last, where, parts, mix, slab):
-    square = jax.ShapeDtypeStruct((32, 32), F32)
-    state = (
-        jax.ShapeDtypeStruct((2, ROWS * 512), F32) if last else jax.ShapeDtypeStruct((8, 4, ROWS, 256), BF16)
-    )
+def solve(last, where, parts, slab, *mix):
+    if last:
+        outs = jax.ShapeDtypeStruct((32, 32), F32), jax.ShapeDtypeStruct((2, ROWS * 512), F32)
+    else:
+        outs = pltpu.VMEM((32, 32), F32), pltpu.VMEM((8, 4, ROWS, 256), BF16)
     return pl.pallas_call(
         functools.partial(solve_kernel, last),
-        out_shape=(square, square, state),
-        in_specs=[SMEM] + [VMEM] * 2 + [pl.BlockSpec(memory_space=pl.ANY)],
-        out_specs=(VMEM,) * 3,
-        scratch_shapes=[pltpu.VMEM((MEMBERS, ROWS, 512 if last else 256), F32), pltpu.SemaphoreType.DMA],
+        out_shape=outs,
+        in_specs=[SMEM, VMEM, pl.BlockSpec(memory_space=pl.ANY)] + [VMEM for _ in mix],
+        out_specs=(VMEM,) * 2,
+        scratch_shapes=[
+            pltpu.VMEM((MEMBERS, ROWS, 512 if last else 256), F32),
+            pltpu.VMEM((32, 32), F32),
+            pltpu.SemaphoreType.DMA,
+        ],
         name="solve",
-    )(where, in_vmem(parts), mix, slab)
+    )(where, in_vmem(parts), slab, *mix)
 
 
 def exchange(blocks, axes):
     return lax.all_to_all(blocks, axes, 0, 0, tiled=True)
+
+
+def swap(block):
+    return lax.ppermute(block, "core", [(0, 1), (1, 0)])
 
 
 def local(ensemble, inputs, features, query_index, observed, perturb):
     z, core = lax.axis_index("z"), lax.axis_index("core")
     e, block = z * 2 + core, core * 8 + z
     where = jnp.stack(
-        [4 * z, core, 2 * e, block % 2, 3 * (block // 2), 3 + jnp.minimum(e, 9) // 2, (e < 10).astype(jnp.int32), e % 2]
+        [4 * z, core, 2 * e, block // 4, block % 4, 4 + jnp.minimum(e, 9) // 2, (e < 10).astype(jnp.int32), e % 2]
     )
-    own, plane, ext, mix = prepare(
+    own, keep, give, ext = prepare(
         where, ensemble, inputs, query_index.reshape(96, 128), observed.reshape(1, -1), perturb
     )
     slab = lax.all_gather(own, ("z", "core"), axis=0, tiled=True)
-    plane = exchange(plane, "core").reshape(4, ROWS, 256)
+    taken = swap(give)
+    plane = jnp.where(core == 0, jnp.concatenate([keep, taken]), jnp.concatenate([taken, keep]))
     plane = jnp.broadcast_to(plane[None], (8, 4, ROWS, 256))
     ext = lax.all_gather(ext, "x", axis=0, tiled=True)
+    mix = []
     for repeat in range(SUBSTEPS):
         half = exchange(plane.reshape(32, ROWS, 256), ("y", "x")).reshape(32 * ROWS, 256)
         half, ext = lax.optimization_barrier((half, ext))
-        other = lax.ppermute(half, "core", [(0, 1), (1, 0)])
+        other = swap(half)
         preds = evaluate(where, half, other, ext, features)
         preds = exchange(preds, ("x", "z"))
-        parts = exchange(member_sums(repeat == 0, where, preds, slab, mix), ("z", "x"))
+        parts = exchange(member_sums(where, preds, slab, *mix), ("z", "x"))
         part = jnp.sum(parts, axis=0)
         parts = exchange(jnp.broadcast_to(part[None], (16, 16, 128)), ("y", "core"))
-        coefficients, mix, plane = solve(repeat == SUBSTEPS - 1, where, parts, mix, slab)
-    return (plane, coefficients)
+        given, plane = solve(repeat == SUBSTEPS - 1, where, parts, slab, *mix)
+        mix = [in_vmem(given)]
+    return (plane, given)
 
 
 def solution(mesh):

time: 208 us -> 198 us (0.952)
  blocking collectives: 151 us -> 133 us
  starting transfers between devices: 11.3 us -> 21.4 us
  Pallas kernels: 24.3 us -> 21 us
    all_to_all x8 -> x7, blocking collectives: 133 us -> 116 us  [exchange(): return lax.all_to_all(blocks, axes, 0, 0, tiled=True)]
    ppermute x2 -> x3, starting transfers between devices: 7 us -> 17.1 us  [swap(): return lax.ppermute(block, 'core', [(0, 1), (1, 0)])]
    pallas_call x6, Pallas kernels: 22.2 us -> 18.9 us  [the longest x2 8.64 us: solve(): pl.pallas_call(functools.partial(solve_kernel, last), out_shape=outs, in_...]
    ppermute x2 -> x3, waiting for transfers between devices: 3.4 us -> 4.35 us  [swap(): return lax.ppermute(block, 'core', [(0, 1), (1, 0)])]
  transfers between devices with their start and end apart: 4 -> 5, of which waited for: 3 -> 4; matrix products, arithmetic and copies ran while one was open for 0% -> 0% of each run, Pallas kernels for 2% -> 1%
where the time goes in v4:
time: 198 us
  blocking collectives  133 us (67%)
  starting transfers between devices  21.4 us (11%)
  Pallas kernels  21 us (11%)
  between operations  14.2 us (7%)
  waiting for transfers between devices  5.87 us (3%)
    all_to_all x7, blocking collectives, exchange(): return lax.all_to_all(blocks, axes, 0, 0, tiled=True)  116 us
    all_gather x1, blocking collectives, local(): ext = lax.all_gather(ext, 'x', axis=0, tiled=True)  17.3 us
    ppermute x3, starting transfers between devices, swap(): return lax.ppermute(block, 'core', [(0, 1), (1, 0)])  17.1 us
    pallas_call x2, Pallas kernels, solve(): pl.pallas_call(functools.partial(solve_kernel, last), out_shape=outs, in_...  8.64 us
    pallas_call x2, Pallas kernels, evaluate(): pl.pallas_call(evaluate_kernel, out_shape=pltpu.VMEM((32, 6, 128), BF16),...  5.16 us
    pallas_call x2, Pallas kernels, member_sums(): pl.pallas_call(sums_kernel, out_shape=pltpu.VMEM((32, 16, 128), F32), gri...  5.13 us
    ppermute x3, waiting for transfers between devices, swap(): return lax.ppermute(block, 'core', [(0, 1), (1, 0)])  4.35 us
    all_to_all x1, starting transfers between devices, exchange(): return lax.all_to_all(blocks, axes, 0, 0, tiled=True)  4.3 us
  transfers between devices with their start and end apart: 5, of which 4 were waited for; matrix products, arithmetic and copies ran while one was open for 0% of the time, Pallas kernels for 1%

profile of v4, /device:TPU:1, one launch (start us, length us, event | category | flops | bytes accessed | tf_op | source)
XLA Modules:
  0.0 197.6 jit_solution(4818719305535683791)
XLA Ops:
  7.2 0.0 all-gather.2.cloned.1.call-start
  7.3 0.7 stack.39.where_ref
  7.9 2.0 %prepare.1 = (f32[2,72,512]{2,1,0:T(8,128)}, bf16[2,40,256]{2,1,0:T(8,128)(2,1)S(1)}, bf16[2,40,256]{2,1,0:T(8,128)(2,1)S(1)}, bf16[96,1152]{1,0:T(8,128)(2,1)S(1)}) custom-call(s32[8]{0:T(128)} %stack.39.where_ref, f32[2,20480]{1,0:T(2,128)} %ensemble_ref.1, bf16[192,1024]{1,0:T(8,128)(2,1)} %inputs_ref.1, s32[96,128]{1,0:T(8,128)} %bitcast.19, ...), custom_call_target="tpu_custom_call" | custom-call | tf_op jit(solution)/shard_map/prepare/pallas_call | solution.py:57
  10.0 0.0 all-gather.2.cloned.1.call-update
  10.0 8.8 %collective-permute-start = (bf16[2,40,256]{2,1,0:T(8,128)(2,1)S(1)}, bf16[2,40,256]{2,1,0:T(8,128)(2,1)S(1)}, u32[]{:S(2)}, u32[]{:S(2)}) collective-permute-start(bf16[2,40,256]{2,1,0:T(8,128)(2,1)S(1)} %get-tuple-element.15), channel_id=1, source_target_pairs={{0,32},{32,0},{1,33},{33,1},{2,34},{34,2},{3,35},{35,3},{4,36},{36... | collective-permute-start | bytes 122888 | tf_op jit(solution)/shard_map/ppermute | solution.py:260
  18.8 0.8 collective-permute-done
  19.7 0.9 broadcast_in_dim.6
  20.6 4.3 %all-to-all-start = ((bf16[32,40,256]{2,1,0:T(8,128)(2,1)}), bf16[32,40,256]{2,1,0:T(8,128)(2,1)S(1)}, u32[]{:S(2)}, u32[]{:S(2)}) async-start(bf16[32,40,256]{2,1,0:T(8,128)(2,1)} %bitcast.10), calls=%async_computation | async-start | bytes 1310720 | tf_op jit(solution)/shard_map/all_to_all | solution.py:256
  24.9 17.3 %all_gather.6.x_ref = bf16[384,1152]{1,0:T(8,128)(2,1)S(1)} all-gather(bf16[96,1152]{1,0:T(8,128)(2,1)S(1)} %get-tuple-element.16), channel_id=1, replica_groups=mesh['z'=8,'core'=2,'y'=8,'x'=4] {'x'}, dimensions={0}, use_global_device_ids=true | all-gather | bytes 1105920 | tf_op jit(solution)/shard_map/all_gather | solution.py:276
  42.1 1.5 all-to-all-done
  43.6 4.3 %collective-permute-start.1 = (bf16[1280,256]{1,0:T(8,128)(2,1)S(1)}, bf16[1280,256]{1,0:T(8,128)(2,1)S(1)}, u32[]{:S(2)}, u32[]{:S(2)}) collective-permute-start(bf16[1280,256]{1,0:T(8,128)(2,1)S(1)} %bitcast.14), channel_id=1, source_target_pairs={{0,32},{32,0},{1,33},{33,1},{2,34},{34,2},{3,35},{35,3},{4,36},{36... | collective-permute-start | bytes 1966088 | tf_op jit(solution)/shard_map/ppermute | solution.py:260
  47.9 1.8 collective-permute-done.1.other_ref
  49.7 2.6 %evaluate.2 = bf16[32,6,128]{2,1,0:T(8,128)(2,1)S(1)} custom-call(s32[8]{0:T(128)} %stack.39.where_ref, bf16[1280,256]{1,0:T(8,128)(2,1)S(1)} %bitcast.15, bf16[1280,256]{1,0:T(8,128)(2,1)S(1)} %collective-permute-done.1.other_ref, bf16[384,1152]{1,0:T(8,128)(2,1)S(1)} %all_gather.6.x_ref, bf16[128,256]{1,0:T(8,128)(2,1)} %features_ref.3), custom_call_target="tpu_custom_call" | custom-call | tf_op jit(solution)/shard_map/evaluate/pallas_call | solution.py:113
  52.3 21.3 %all_to_all.40.preds_ref = bf16[32,6,128]{2,1,0:T(8,128)(2,1)S(1)} all-to-all(bf16[32,6,128]{2,1,0:T(8,128)(2,1)S(1)} %evaluate.2), channel_id=1, replica_groups=mesh['z'=8,'core'=2,'y'=8,'x'=4] {'x','z'}, dimensions={0} | all-to-all | bytes 98304 | tf_op jit(solution)/shard_map/all_to_all | solution.py:256
  73.6 0.0 all-gather.2.cloned.1.call-done.target_ref.state_ref.slab_ref
  73.6 2.5 %member_sums.2 = f32[32,16,128]{2,1,0:T(8,128)S(1)} custom-call(s32[8]{0:T(128)} %stack.39.where_ref, bf16[32,6,128]{2,1,0:T(8,128)(2,1)S(1)} %all_to_all.40.preds_ref, f32[32,72,512]{2,1,0:T(8,128)} %all-gather.2.cloned.1.call-done.target_ref.state_ref.slab_ref, f32[32,72,512]{2,1,0:T(8,128)} %all-gather.2.cloned.1.call-done.target_ref.state_ref.slab_ref), custom_call_target="tpu_custom_call" | custom-call | tf_op jit(solution)/shard_map/member_sums/pallas_call | solution.py:161
  76.1 13.5 %all_to_all.41 = f32[32,16,128]{2,1,0:T(8,128)S(1)} all-to-all(f32[32,16,128]{2,1,0:T(8,128)S(1)} %member_sums.2), channel_id=1, replica_groups=mesh['z'=8,'core'=2,'y'=8,'x'=4] {'z','x'}, dimensions={0} | all-to-all | bytes 524288 | tf_op jit(solution)/shard_map/all_to_all | solution.py:256
  89.6 17.2 %all_to_all.42.parts_ref = f32[16,16,128]{2,1,0:T(8,128)S(1)} all-to-all(f32[16,16,128]{2,1,0:T(8,128)S(1)} %broadcast_in_dim.7), channel_id=1, replica_groups=mesh['z'=8,'core'=2,'y'=8,'x'=4] {'y','core'}, dimensions={0} | all-to-all | bytes 262144 | tf_op jit(solution)/shard_map/all_to_all | solution.py:256
  106.9 3.2 %solve.2 = (f32[32,32]{1,0:T(8,128)S(1)}, bf16[8,4,40,256]{3,2,1,0:T(8,128)(2,1)S(1)}) custom-call(s32[8]{0:T(128)} %stack.39.where_ref, f32[16,16,128]{2,1,0:T(8,128)S(1)} %all_to_all.42.parts_ref, f32[32,72,512]{2,1,0:T(8,128)} %all-gather.2.cloned.1.call-done.target_ref.state_ref.slab_ref), custom_call_target="tpu_custom_call" | custom-call | tf_op jit(solution)/shard_map/solve/pallas_call | solution.py:241
  110.1 22.0 %all_to_all.43 = bf16[32,40,256]{2,1,0:T(8,128)(2,1)S(1)} all-to-all(bf16[32,40,256]{2,1,0:T(8,128)(2,1)S(1)} %bitcast.18), channel_id=1, replica_groups=mesh['z'=8,'core'=2,'y'=8,'x'=4] {'y','x'}, dimensions={0} | all-to-all | bytes 1310720 | tf_op jit(solution)/shard_map/all_to_all | solution.py:256
  132.1 4.0 %collective-permute-start.2 = (bf16[1280,256]{1,0:T(8,128)(2,1)S(1)}, bf16[1280,256]{1,0:T(8,128)(2,1)S(1)}, u32[]{:S(2)}, u32[]{:S(2)}) collective-permute-start(bf16[1280,256]{1,0:T(8,128)(2,1)S(1)} %bitcast.16), channel_id=1, source_target_pairs={{0,32},{32,0},{1,33},{33,1},{2,34},{34,2},{3,35},{35,3},{4,36},{36... | collective-permute-start | bytes 1966088 | tf_op jit(solution)/shard_map/ppermute | solution.py:260
  136.1 1.7 collective-permute-done.2.other_ref
  137.8 2.6 %evaluate.3 = bf16[32,6,128]{2,1,0:T(8,128)(2,1)S(1)} custom-call(s32[8]{0:T(128)} %stack.39.where_ref, bf16[1280,256]{1,0:T(8,128)(2,1)S(1)} %bitcast.17, bf16[1280,256]{1,0:T(8,128)(2,1)S(1)} %collective-permute-done.2.other_ref, bf16[384,1152]{1,0:T(8,128)(2,1)S(1)} %all_gather.6.x_ref, bf16[128,256]{1,0:T(8,128)(2,1)} %features_ref.3), custom_call_target="tpu_custom_call" | custom-call | tf_op jit(solution)/shard_map/evaluate/pallas_call | solution.py:113
  140.4 13.3 %all_to_all.44.preds_ref = bf16[32,6,128]{2,1,0:T(8,128)(2,1)S(1)} all-to-all(bf16[32,6,128]{2,1,0:T(8,128)(2,1)S(1)} %evaluate.3), channel_id=1, replica_groups=mesh['z'=8,'core'=2,'y'=8,'x'=4] {'x','z'}, dimensions={0} | all-to-all | bytes 98304 | tf_op jit(solution)/shard_map/all_to_all | solution.py:256
  153.8 2.7 %member_sums.3 = f32[32,16,128]{2,1,0:T(8,128)S(1)} custom-call(s32[8]{0:T(128)} %stack.39.where_ref, bf16[32,6,128]{2,1,0:T(8,128)(2,1)S(1)} %all_to_all.44.preds_ref, f32[32,72,512]{2,1,0:T(8,128)} %all-gather.2.cloned.1.call-done.target_ref.state_ref.slab_ref, f32[32,72,512]{2,1,0:T(8,128)} %all-gather.2.cloned.1.call-done.target_ref.state_ref.slab_ref, ...), custom_call_target="tpu_custom_call" | custom-call | tf_op jit(solution)/shard_map/member_sums/pallas_call | solution.py:161
  156.4 13.5 %all_to_all.45 = f32[32,16,128]{2,1,0:T(8,128)S(1)} all-to-all(f32[32,16,128]{2,1,0:T(8,128)S(1)} %member_sums.3), channel_id=1, replica_groups=mesh['z'=8,'core'=2,'y'=8,'x'=4] {'z','x'}, dimensions={0} | all-to-all | bytes 524288 | tf_op jit(solution)/shard_map/all_to_all | solution.py:256
  170.0 15.4 %all_to_all.46.parts_ref = f32[16,16,128]{2,1,0:T(8,128)S(1)} all-to-all(f32[16,16,128]{2,1,0:T(8,128)S(1)} %broadcast_in_dim.8), channel_id=1, replica_groups=mesh['z'=8,'core'=2,'y'=8,'x'=4] {'y','core'}, dimensions={0} | all-to-all | bytes 262144 | tf_op jit(solution)/shard_map/all_to_all | solution.py:256
  185.3 5.4 %solve.3 = (f32[32,32]{1,0:T(8,128)}, f32[2,20480]{1,0:T(2,128)}) custom-call(s32[8]{0:T(128)} %stack.39.where_ref, f32[16,16,128]{2,1,0:T(8,128)S(1)} %all_to_all.46.parts_ref, f32[32,72,512]{2,1,0:T(8,128)} %all-gather.2.cloned.1.call-done.target_ref.state_ref.slab_ref, f32[32,32]{1,0:T(8,128)S(1)} %get-tuple-element.23.rest_0_), custom_call_target="tpu_custom_call" | custom-call | tf_op jit(solution)/shard_map/solve/pallas_call | solution.py:241
  (5 shorter events, 0.1 us)
Async XLA Ops:
  7.2 66.5 %all-gather.2.cloned.1.call-start = ((), (), s32[]{:S(2)}) async-start(), calls=%async_computation.8 | async-start | bytes 5013504 | tf_op jit(solution)/shard_map/all_gather | solution.py:272
  10.0 9.6 %collective-permute-start = (bf16[2,40,256]{2,1,0:T(8,128)(2,1)S(1)}, bf16[2,40,256]{2,1,0:T(8,128)(2,1)S(1)}, u32[]{:S(2)}, u32[]{:S(2)}) collective-permute-start(bf16[2,40,256]{2,1,0:T(8,128)(2,1)S(1)} %get-tuple-element.15), channel_id=1, source_target_pairs={{0,32},{32,0},{1,33},{33,1},{2,34},{34,2},{3,35},{35,3},{4,36},{36... | collective-permute-start | bytes 122888 | tf_op jit(solution)/shard_map/ppermute | solution.py:260
  20.6 23.1 %all-to-all-start = ((bf16[32,40,256]{2,1,0:T(8,128)(2,1)}), bf16[32,40,256]{2,1,0:T(8,128)(2,1)S(1)}, u32[]{:S(2)}, u32[]{:S(2)}) async-start(bf16[32,40,256]{2,1,0:T(8,128)(2,1)} %bitcast.10), calls=%async_computation | async-start | bytes 1310720 | tf_op jit(solution)/shard_map/all_to_all | solution.py:256
  43.6 6.1 %collective-permute-start.1 = (bf16[1280,256]{1,0:T(8,128)(2,1)S(1)}, bf16[1280,256]{1,0:T(8,128)(2,1)S(1)}, u32[]{:S(2)}, u32[]{:S(2)}) collective-permute-start(bf16[1280,256]{1,0:T(8,128)(2,1)S(1)} %bitcast.14), channel_id=1, source_target_pairs={{0,32},{32,0},{1,33},{33,1},{2,34},{34,2},{3,35},{35,3},{4,36},{36... | collective-permute-start | bytes 1966088 | tf_op jit(solution)/shard_map/ppermute | solution.py:260
  132.1 5.7 %collective-permute-start.2 = (bf16[1280,256]{1,0:T(8,128)(2,1)S(1)}, bf16[1280,256]{1,0:T(8,128)(2,1)S(1)}, u32[]{:S(2)}, u32[]{:S(2)}) collective-permute-start(bf16[1280,256]{1,0:T(8,128)(2,1)S(1)} %bitcast.16), channel_id=1, source_target_pairs={{0,32},{32,0},{1,33},{33,1},{2,34},{34,2},{3,35},{35,3},{4,36},{36... | collective-permute-start | bytes 1966088 | tf_op jit(solution)/shard_map/ppermute | solution.py:260
Sparse Core Ops, SparseCore 0:
  10.1 51.9 all-gather.1

commit v5 on v4

--- a/solution.py
+++ b/solution.py
@@ -32,8 +32,8 @@
     return jnp.dot(a, b, preferred_element_type=F32)
 
 
-def prepare_kernel(where_ref, ensemble_ref, inputs_ref, picks_ref, observed_ref, perturb_ref, own_ref, keep_ref, give_ref, ext_ref):
-    core = where_ref[1]
+def prepare_kernel(ensemble_ref, inputs_ref, picks_ref, observed_ref, perturb_ref, own_ref, keep_ref, give_ref, ext_ref):
+    core = lax.axis_index("core")
     for i in range(2):
         for e in range(16):
             for part in range(6):
@@ -53,7 +53,7 @@
     ext_ref[48:, SENSORS:] = jnp.zeros((48, 128), BF16)
 
 
-def prepare(where, ensemble, inputs, picks, observed, perturb):
+def prepare(ensemble, inputs, picks, observed, perturb):
     return pl.pallas_call(
         prepare_kernel,
         out_shape=(
@@ -62,10 +62,10 @@
             pltpu.VMEM((2, ROWS, 256), BF16),
             pltpu.VMEM((96, SENSORS + 128), BF16),
         ),
-        in_specs=[SMEM] + [VMEM] * 5,
+        in_specs=[VMEM] * 5,
         out_specs=(VMEM,) * 4,
         name="prepare",
-    )(where, ensemble, inputs, picks, observed, perturb)
+    )(ensemble, inputs, picks, observed, perturb)
 
 
 def evaluate_kernel(where_ref, own_ref, other_ref, x_ref, features_ref, out_ref, whole_ref, chosen_ref):
@@ -105,8 +105,10 @@
             jnp.take_along_axis(even, picks, axis=1, mode="promise_in_bounds"),
             jnp.take_along_axis(odd, picks, axis=1, mode="promise_in_bounds"),
         )
-    for i in range(32):
-        out_ref[i] = chosen_ref[6 * i : 6 * i + 6, :].astype(BF16)
+    for x in range(4):
+        for z in range(8):
+            at = 48 * x + 6 * z
+            out_ref[4 * z + x] = chosen_ref[at : at + 6, :].astype(BF16)
 
 
 def evaluate(where, own, other, inputs_ext, features):
@@ -129,12 +131,8 @@
 
 def sums_kernel(where_ref, preds_ref, target_ref, state_ref, *rest):
     *mix_ref, out_ref, preds_f32_ref = rest
-    r = lax.broadcasted_iota(jnp.int32, (32, 32), 0)
-    s = lax.broadcasted_iota(jnp.int32, (32, 32), 1)
-    order = (s == (r % 4) * 8 + r // 4).astype(F32).astype(BF16)
     preds_f32_ref[...] = preds_ref[...].astype(F32)
     preds = jnp.concatenate([preds_f32_ref[:, i, :] for i in range(6)], 1)
-    preds = mxu(order, preds.astype(BF16))
     target = jnp.concatenate([target_ref[:, i, :] for i in range(6)], 1)
     innov = ((target - preds) / NOISE_STD).astype(BF16)
     anom = (preds - jnp.mean(preds, axis=0, keepdims=True)) / (NOISE_STD * (MEMBERS - 1) ** 0.5)
@@ -267,7 +265,7 @@
         [4 * z, core, 2 * e, block // 4, block % 4, 4 + jnp.minimum(e, 9) // 2, (e < 10).astype(jnp.int32), e % 2]
     )
     own, keep, give, ext = prepare(
-        where, ensemble, inputs, query_index.reshape(96, 128), observed.reshape(1, -1), perturb
+        ensemble, inputs, query_index.reshape(96, 128), observed.reshape(1, -1), perturb
     )
     slab = lax.all_gather(own, ("z", "core"), axis=0, tiled=True)
     taken = swap(give)
@@ -280,10 +278,10 @@
         half, ext = lax.optimization_barrier((half, ext))
         other = swap(half)
         preds = evaluate(where, half, other, ext, features)
-        preds = exchange(preds, ("x", "z"))
-        parts = exchange(member_sums(where, preds, slab, *mix), ("z", "x"))
+        preds = exchange(preds, ("z", "x"))
+        parts = exchange(member_sums(where, preds, slab, *mix), ("x", "z"))
         part = jnp.sum(parts, axis=0)
-        parts = exchange(jnp.broadcast_to(part[None], (16, 16, 128)), ("y", "core"))
+        parts = exchange(jnp.broadcast_to(part[None], (16, 16, 128)), ("core", "y"))
         given, plane = solve(repeat == SUBSTEPS - 1, where, parts, slab, *mix)
         mix = [in_vmem(given)]
     return (plane, given)

time: 198 us -> 195 us (0.985)
  blocking collectives: 133 us -> 130 us
    all_to_all x7, blocking collectives: 116 us -> 113 us  [exchange(): return lax.all_to_all(blocks, axes, 0, 0, tiled=True)]
  transfers between devices with their start and end apart: 5 -> 5, of which waited for: 4 -> 4; matrix products, arithmetic and copies ran while one was open for 0% -> 1% of each run, Pallas kernels for 1% -> 1%
where the time goes in v5:
time: 195 us; the launch traced here: 194 us
  blocking collectives  130 us (67%)
  starting transfers between devices  21.8 us (11%)
  Pallas kernels  20.9 us (11%)
  between operations  14.2 us (7%)
  waiting for transfers between devices  4.98 us (3%)
    all_to_all x7, blocking collectives, exchange(): return lax.all_to_all(blocks, axes, 0, 0, tiled=True)  113 us
    ppermute x3, starting transfers between devices, swap(): return lax.ppermute(block, 'core', [(0, 1), (1, 0)])  17.5 us
    all_gather x1, blocking collectives, local(): ext = lax.all_gather(ext, 'x', axis=0, tiled=True)  17.4 us
    pallas_call x2, Pallas kernels, solve(): pl.pallas_call(functools.partial(solve_kernel, last), out_shape=outs, in_...  8.64 us
    pallas_call x2, Pallas kernels, evaluate(): pl.pallas_call(evaluate_kernel, out_shape=pltpu.VMEM((32, 6, 128), BF16),...  5.16 us
    pallas_call x2, Pallas kernels, member_sums(): pl.pallas_call(sums_kernel, out_shape=pltpu.VMEM((32, 16, 128), F32), gri...  5.02 us
    all_to_all x1, starting transfers between devices, exchange(): return lax.all_to_all(blocks, axes, 0, 0, tiled=True)  4.3 us
  transfers between devices with their start and end apart: 5, of which 4 were waited for; matrix products, arithmetic and copies ran while one was open for 1% of the time, Pallas kernels for 1%

profile of v5, /device:TPU:1, one launch (start us, length us, event | category | flops | bytes accessed | tf_op | source)
XLA Modules:
  0.0 193.9 jit_solution(1820307467695833491)
XLA Ops:
  7.2 0.0 all-gather.2.cloned.1.call-start
  7.2 2.0 %prepare.1 = (f32[2,72,512]{2,1,0:T(8,128)}, bf16[2,40,256]{2,1,0:T(8,128)(2,1)S(1)}, bf16[2,40,256]{2,1,0:T(8,128)(2,1)S(1)}, bf16[96,1152]{1,0:T(8,128)(2,1)S(1)}) custom-call(f32[2,20480]{1,0:T(2,128)} %ensemble_ref.1, bf16[192,1024]{1,0:T(8,128)(2,1)} %inputs_ref.1, s32[96,128]{1,0:T(8,128)} %bitcast.19, f32[1,12288]{1,0:T(1,128)} %bitcast.20, ...), custom_call_target="tpu_custom_call" | custom-call | tf_op jit(solution)/shard_map/prepare/pallas_call | solution.py:57
  9.2 0.0 all-gather.2.cloned.1.call-update
  9.3 8.8 %collective-permute-start = (bf16[2,40,256]{2,1,0:T(8,128)(2,1)S(1)}, bf16[2,40,256]{2,1,0:T(8,128)(2,1)S(1)}, u32[]{:S(2)}, u32[]{:S(2)}) collective-permute-start(bf16[2,40,256]{2,1,0:T(8,128)(2,1)S(1)} %get-tuple-element.15), channel_id=1, source_target_pairs={{0,32},{32,0},{1,33},{33,1},{2,34},{34,2},{3,35},{35,3},{4,36},{36... | collective-permute-start | bytes 122888 | tf_op jit(solution)/shard_map/ppermute | solution.py:258
  18.1 0.8 collective-permute-done
  18.9 0.9 broadcast_in_dim.6
  19.8 4.3 %all-to-all-start = ((bf16[32,40,256]{2,1,0:T(8,128)(2,1)}), bf16[32,40,256]{2,1,0:T(8,128)(2,1)S(1)}, u32[]{:S(2)}, u32[]{:S(2)}) async-start(bf16[32,40,256]{2,1,0:T(8,128)(2,1)} %bitcast.10), calls=%async_computation | async-start | bytes 1310720 | tf_op jit(solution)/shard_map/all_to_all | solution.py:254
  24.1 17.4 %all_gather.6.x_ref = bf16[384,1152]{1,0:T(8,128)(2,1)S(1)} all-gather(bf16[96,1152]{1,0:T(8,128)(2,1)S(1)} %get-tuple-element.16), channel_id=1, replica_groups=mesh['z'=8,'core'=2,'y'=8,'x'=4] {'x'}, dimensions={0}, use_global_device_ids=true | all-gather | bytes 1105920 | tf_op jit(solution)/shard_map/all_gather | solution.py:274
  41.5 1.4 all-to-all-done
  42.9 4.3 %collective-permute-start.1 = (bf16[1280,256]{1,0:T(8,128)(2,1)S(1)}, bf16[1280,256]{1,0:T(8,128)(2,1)S(1)}, u32[]{:S(2)}, u32[]{:S(2)}) collective-permute-start(bf16[1280,256]{1,0:T(8,128)(2,1)S(1)} %bitcast.14), channel_id=1, source_target_pairs={{0,32},{32,0},{1,33},{33,1},{2,34},{34,2},{3,35},{35,3},{4,36},{36... | collective-permute-start | bytes 1966088 | tf_op jit(solution)/shard_map/ppermute | solution.py:258
  47.3 0.6 stack.39.where_ref
  47.9 1.0 collective-permute-done.1.other_ref
  48.9 2.6 %evaluate.2 = bf16[32,6,128]{2,1,0:T(8,128)(2,1)S(1)} custom-call(s32[8]{0:T(128)} %stack.39.where_ref, bf16[1280,256]{1,0:T(8,128)(2,1)S(1)} %bitcast.15, bf16[1280,256]{1,0:T(8,128)(2,1)S(1)} %collective-permute-done.1.other_ref, bf16[384,1152]{1,0:T(8,128)(2,1)S(1)} %all_gather.6.x_ref, bf16[128,256]{1,0:T(8,128)(2,1)} %features_ref.3), custom_call_target="tpu_custom_call" | custom-call | tf_op jit(solution)/shard_map/evaluate/pallas_call | solution.py:115
  51.5 21.3 %all_to_all.40.preds_ref = bf16[32,6,128]{2,1,0:T(8,128)(2,1)S(1)} all-to-all(bf16[32,6,128]{2,1,0:T(8,128)(2,1)S(1)} %evaluate.2), channel_id=1, replica_groups=mesh['z'=8,'core'=2,'y'=8,'x'=4] {'z','x'}, dimensions={0} | all-to-all | bytes 98304 | tf_op jit(solution)/shard_map/all_to_all | solution.py:254
  72.8 0.0 all-gather.2.cloned.1.call-done.target_ref.state_ref.slab_ref
  72.8 2.4 %member_sums.2 = f32[32,16,128]{2,1,0:T(8,128)S(1)} custom-call(s32[8]{0:T(128)} %stack.39.where_ref, bf16[32,6,128]{2,1,0:T(8,128)(2,1)S(1)} %all_to_all.40.preds_ref, f32[32,72,512]{2,1,0:T(8,128)} %all-gather.2.cloned.1.call-done.target_ref.state_ref.slab_ref, f32[32,72,512]{2,1,0:T(8,128)} %all-gather.2.cloned.1.call-done.target_ref.state_ref.slab_ref), custom_call_target="tpu_custom_call" | custom-call | tf_op jit(solution)/shard_map/member_sums/pallas_call | solution.py:159
  75.2 12.8 %all_to_all.41 = f32[32,16,128]{2,1,0:T(8,128)S(1)} all-to-all(f32[32,16,128]{2,1,0:T(8,128)S(1)} %member_sums.2), channel_id=1, replica_groups=mesh['z'=8,'core'=2,'y'=8,'x'=4] {'x','z'}, dimensions={0} | all-to-all | bytes 524288 | tf_op jit(solution)/shard_map/all_to_all | solution.py:254
  88.0 15.3 %all_to_all.42.parts_ref = f32[16,16,128]{2,1,0:T(8,128)S(1)} all-to-all(f32[16,16,128]{2,1,0:T(8,128)S(1)} %broadcast_in_dim.7), channel_id=1, replica_groups=mesh['z'=8,'core'=2,'y'=8,'x'=4] {'core','y'}, dimensions={0} | all-to-all | bytes 262144 | tf_op jit(solution)/shard_map/all_to_all | solution.py:254
  103.3 3.2 %solve.2 = (f32[32,32]{1,0:T(8,128)S(1)}, bf16[8,4,40,256]{3,2,1,0:T(8,128)(2,1)S(1)}) custom-call(s32[8]{0:T(128)} %stack.39.where_ref, f32[16,16,128]{2,1,0:T(8,128)S(1)} %all_to_all.42.parts_ref, f32[32,72,512]{2,1,0:T(8,128)} %all-gather.2.cloned.1.call-done.target_ref.state_ref.slab_ref), custom_call_target="tpu_custom_call" | custom-call | tf_op jit(solution)/shard_map/solve/pallas_call | solution.py:239
  106.6 23.4 %all_to_all.43 = bf16[32,40,256]{2,1,0:T(8,128)(2,1)S(1)} all-to-all(bf16[32,40,256]{2,1,0:T(8,128)(2,1)S(1)} %bitcast.18), channel_id=1, replica_groups=mesh['z'=8,'core'=2,'y'=8,'x'=4] {'y','x'}, dimensions={0} | all-to-all | bytes 1310720 | tf_op jit(solution)/shard_map/all_to_all | solution.py:254
  130.0 4.4 %collective-permute-start.2 = (bf16[1280,256]{1,0:T(8,128)(2,1)S(1)}, bf16[1280,256]{1,0:T(8,128)(2,1)S(1)}, u32[]{:S(2)}, u32[]{:S(2)}) collective-permute-start(bf16[1280,256]{1,0:T(8,128)(2,1)S(1)} %bitcast.16), channel_id=1, source_target_pairs={{0,32},{32,0},{1,33},{33,1},{2,34},{34,2},{3,35},{35,3},{4,36},{36... | collective-permute-start | bytes 1966088 | tf_op jit(solution)/shard_map/ppermute | solution.py:258
  134.4 1.7 collective-permute-done.2.other_ref
  136.1 2.6 %evaluate.3 = bf16[32,6,128]{2,1,0:T(8,128)(2,1)S(1)} custom-call(s32[8]{0:T(128)} %stack.39.where_ref, bf16[1280,256]{1,0:T(8,128)(2,1)S(1)} %bitcast.17, bf16[1280,256]{1,0:T(8,128)(2,1)S(1)} %collective-permute-done.2.other_ref, bf16[384,1152]{1,0:T(8,128)(2,1)S(1)} %all_gather.6.x_ref, bf16[128,256]{1,0:T(8,128)(2,1)} %features_ref.3), custom_call_target="tpu_custom_call" | custom-call | tf_op jit(solution)/shard_map/evaluate/pallas_call | solution.py:115
  138.7 14.0 %all_to_all.44.preds_ref = bf16[32,6,128]{2,1,0:T(8,128)(2,1)S(1)} all-to-all(bf16[32,6,128]{2,1,0:T(8,128)(2,1)S(1)} %evaluate.3), channel_id=1, replica_groups=mesh['z'=8,'core'=2,'y'=8,'x'=4] {'z','x'}, dimensions={0} | all-to-all | bytes 98304 | tf_op jit(solution)/shard_map/all_to_all | solution.py:254
  152.7 2.6 %member_sums.3 = f32[32,16,128]{2,1,0:T(8,128)S(1)} custom-call(s32[8]{0:T(128)} %stack.39.where_ref, bf16[32,6,128]{2,1,0:T(8,128)(2,1)S(1)} %all_to_all.44.preds_ref, f32[32,72,512]{2,1,0:T(8,128)} %all-gather.2.cloned.1.call-done.target_ref.state_ref.slab_ref, f32[32,72,512]{2,1,0:T(8,128)} %all-gather.2.cloned.1.call-done.target_ref.state_ref.slab_ref, ...), custom_call_target="tpu_custom_call" | custom-call | tf_op jit(solution)/shard_map/member_sums/pallas_call | solution.py:159
  155.3 12.8 %all_to_all.45 = f32[32,16,128]{2,1,0:T(8,128)S(1)} all-to-all(f32[32,16,128]{2,1,0:T(8,128)S(1)} %member_sums.3), channel_id=1, replica_groups=mesh['z'=8,'core'=2,'y'=8,'x'=4] {'x','z'}, dimensions={0} | all-to-all | bytes 524288 | tf_op jit(solution)/shard_map/all_to_all | solution.py:254
  168.1 13.4 %all_to_all.46.parts_ref = f32[16,16,128]{2,1,0:T(8,128)S(1)} all-to-all(f32[16,16,128]{2,1,0:T(8,128)S(1)} %broadcast_in_dim.8), channel_id=1, replica_groups=mesh['z'=8,'core'=2,'y'=8,'x'=4] {'core','y'}, dimensions={0} | all-to-all | bytes 262144 | tf_op jit(solution)/shard_map/all_to_all | solution.py:254
  181.6 5.4 %solve.3 = (f32[32,32]{1,0:T(8,128)}, f32[2,20480]{1,0:T(2,128)}) custom-call(s32[8]{0:T(128)} %stack.39.where_ref, f32[16,16,128]{2,1,0:T(8,128)S(1)} %all_to_all.46.parts_ref, f32[32,72,512]{2,1,0:T(8,128)} %all-gather.2.cloned.1.call-done.target_ref.state_ref.slab_ref, f32[32,32]{1,0:T(8,128)S(1)} %get-tuple-element.23.rest_0_), custom_call_target="tpu_custom_call" | custom-call | tf_op jit(solution)/shard_map/solve/pallas_call | solution.py:239
  (5 shorter events, 0.1 us)
Async XLA Ops:
  7.2 65.6 %all-gather.2.cloned.1.call-start = ((), (), s32[]{:S(2)}) async-start(), calls=%async_computation.8 | async-start | bytes 5013504 | tf_op jit(solution)/shard_map/all_gather | solution.py:270
  9.3 9.6 %collective-permute-start = (bf16[2,40,256]{2,1,0:T(8,128)(2,1)S(1)}, bf16[2,40,256]{2,1,0:T(8,128)(2,1)S(1)}, u32[]{:S(2)}, u32[]{:S(2)}) collective-permute-start(bf16[2,40,256]{2,1,0:T(8,128)(2,1)S(1)} %get-tuple-element.15), channel_id=1, source_target_pairs={{0,32},{32,0},{1,33},{33,1},{2,34},{34,2},{3,35},{35,3},{4,36},{36... | collective-permute-start | bytes 122888 | tf_op jit(solution)/shard_map/ppermute | solution.py:258
  19.8 23.1 %all-to-all-start = ((bf16[32,40,256]{2,1,0:T(8,128)(2,1)}), bf16[32,40,256]{2,1,0:T(8,128)(2,1)S(1)}, u32[]{:S(2)}, u32[]{:S(2)}) async-start(bf16[32,40,256]{2,1,0:T(8,128)(2,1)} %bitcast.10), calls=%async_computation | async-start | bytes 1310720 | tf_op jit(solution)/shard_map/all_to_all | solution.py:254
  42.9 6.0 %collective-permute-start.1 = (bf16[1280,256]{1,0:T(8,128)(2,1)S(1)}, bf16[1280,256]{1,0:T(8,128)(2,1)S(1)}, u32[]{:S(2)}, u32[]{:S(2)}) collective-permute-start(bf16[1280,256]{1,0:T(8,128)(2,1)S(1)} %bitcast.14), channel_id=1, source_target_pairs={{0,32},{32,0},{1,33},{33,1},{2,34},{34,2},{3,35},{35,3},{4,36},{36... | collective-permute-start | bytes 1966088 | tf_op jit(solution)/shard_map/ppermute | solution.py:258
  130.0 6.1 %collective-permute-start.2 = (bf16[1280,256]{1,0:T(8,128)(2,1)S(1)}, bf16[1280,256]{1,0:T(8,128)(2,1)S(1)}, u32[]{:S(2)}, u32[]{:S(2)}) collective-permute-start(bf16[1280,256]{1,0:T(8,128)(2,1)S(1)} %bitcast.16), channel_id=1, source_target_pairs={{0,32},{32,0},{1,33},{33,1},{2,34},{34,2},{3,35},{35,3},{4,36},{36... | collective-permute-start | bytes 1966088 | tf_op jit(solution)/shard_map/ppermute | solution.py:258
Sparse Core Ops, SparseCore 0:
  10.1 51.9 all-gather.1

commit v6 on v5

--- a/solution.py
+++ b/solution.py
@@ -21,7 +21,7 @@
 F32, BF16 = jnp.float32, jnp.bfloat16
 HIGHEST = lax.Precision.HIGHEST
 VMEM = pl.BlockSpec(memory_space=pltpu.VMEM)
-SMEM = pl.BlockSpec(memory_space=pltpu.SMEM)
+ANY = pl.BlockSpec(memory_space=pl.ANY)
 
 
 def in_vmem(x):
@@ -68,10 +68,12 @@
     )(ensemble, inputs, picks, observed, perturb)
 
 
-def evaluate_kernel(where_ref, own_ref, other_ref, x_ref, features_ref, out_ref, whole_ref, chosen_ref):
+def evaluate_kernel(own_ref, other_ref, x_ref, features_hbm, out_ref, whole_ref, chosen_ref, features_ref, sem):
+    fetch = pltpu.make_async_copy(features_hbm, features_ref, sem)
+    fetch.start()
     r = lax.broadcasted_iota(jnp.int32, (256, 256), 0)
     s = lax.broadcasted_iota(jnp.int32, (256, 256), 1)
-    mix = (s == ((r + where_ref[1]) % 2) * 128 + r // 2).astype(F32).astype(BF16)
+    mix = (s == ((r + lax.axis_index("core")) % 2) * 128 + r // 2).astype(F32).astype(BF16)
 
     def narrow(start):
         both = jnp.concatenate([own_ref[start : start + 128, :], other_ref[start : start + 128, :]], 0)
@@ -79,16 +81,17 @@
 
     branch_in, branch_mid, branch_out, trunk_in, trunk_out = 0, 512, 640, 896, 1024
     halves = (own_ref, other_ref)
-    trunk_hidden = jnp.tanh(mxu(features_ref[...], narrow(trunk_in)) * FEATS ** (-0.5)).astype(BF16)
-    trunk = [
-        (mxu(trunk_hidden, half[trunk_out : trunk_out + 256, :]) * WIDTH ** (-0.5)).astype(BF16) for half in halves
-    ]
     total = None
     for i in range(4):
         part = mxu(x_ref[:, 256 * i : 256 * i + 256], narrow(branch_in + 128 * i))
         total = part if total is None else total + part
     hidden = jnp.tanh(total * SENSORS ** (-0.5)).astype(BF16)
     hidden = jnp.tanh(mxu(hidden, narrow(branch_mid)) * WIDTH ** (-0.5)).astype(BF16)
+    fetch.wait()
+    trunk_hidden = jnp.tanh(mxu(features_ref[...], narrow(trunk_in)) * FEATS ** (-0.5)).astype(BF16)
+    trunk = [
+        (mxu(trunk_hidden, half[trunk_out : trunk_out + 256, :]) * WIDTH ** (-0.5)).astype(BF16) for half in halves
+    ]
     whole = None
     for c, half in enumerate(halves):
         branch = (mxu(hidden, half[branch_out : branch_out + 256, :]) * WIDTH ** (-0.5)).astype(BF16)
@@ -111,15 +114,20 @@
             out_ref[4 * z + x] = chosen_ref[at : at + 6, :].astype(BF16)
 
 
-def evaluate(where, own, other, inputs_ext, features):
+def evaluate(own, other, inputs_ext, features):
     return pl.pallas_call(
         evaluate_kernel,
         out_shape=pltpu.VMEM((32, 6, 128), BF16),
-        in_specs=[SMEM] + [VMEM] * 4,
+        in_specs=[VMEM] * 3 + [ANY],
         out_specs=VMEM,
-        scratch_shapes=[pltpu.VMEM((384, 128), F32), pltpu.VMEM((192, 128), F32)],
+        scratch_shapes=[
+            pltpu.VMEM((384, 128), F32),
+            pltpu.VMEM((192, 128), F32),
+            pltpu.VMEM((128, FEATS), BF16),
+            pltpu.SemaphoreType.DMA,
+        ],
         name="evaluate",
-    )(where, in_vmem(own), in_vmem(other), in_vmem(inputs_ext), features)
+    )(in_vmem(own), in_vmem(other), in_vmem(inputs_ext), features)
 
 
 def split(x):
@@ -129,19 +137,40 @@
     return high, middle, (rest - middle.astype(F32)).astype(BF16)
 
 
-def sums_kernel(where_ref, preds_ref, target_ref, state_ref, *rest):
-    *mix_ref, out_ref, preds_f32_ref = rest
+def sums_kernel(preds_ref, slab_ref, *rest):
+    *mix_hbm, out_ref, preds_f32_ref, target_ref, state_ref, mix_ref, sems = rest
+    z, core = lax.axis_index("z"), lax.axis_index("core")
+    block = core * 8 + z
+    place = z * 2 + core
+    share = (place < 10).astype(F32)
+    place = jnp.minimum(place, 9)
+    row = pl.multiple_of(8 * (block // 4), 8)
+    column = pl.multiple_of(128 * (block % 4), 128)
+    fetches = [
+        pltpu.make_async_copy(slab_ref.at[:, pl.ds(row, 8), pl.ds(column, 128)], target_ref, sems.at[0])
+    ]
+    row = pl.multiple_of(NOTES + 8 * (place // 2), 8)
+    column = pl.multiple_of(256 * (place % 2), 256)
+    fetches.append(
+        pltpu.make_async_copy(slab_ref.at[:, pl.ds(row, 8), pl.ds(column, 256)], state_ref, sems.at[1])
+    )
+    if mix_hbm:
+        fetches.append(pltpu.make_async_copy(mix_hbm[0], mix_ref, sems.at[2]))
+    for fetch in fetches:
+        fetch.start()
     preds_f32_ref[...] = preds_ref[...].astype(F32)
     preds = jnp.concatenate([preds_f32_ref[:, i, :] for i in range(6)], 1)
+    anom = (preds - jnp.mean(preds, axis=0, keepdims=True)) / (NOISE_STD * (MEMBERS - 1) ** 0.5)
+    lefts_seen = split(anom)
+    for fetch in fetches:
+        fetch.wait()
     target = jnp.concatenate([target_ref[:, i, :] for i in range(6)], 1)
     innov = ((target - preds) / NOISE_STD).astype(BF16)
-    anom = (preds - jnp.mean(preds, axis=0, keepdims=True)) / (NOISE_STD * (MEMBERS - 1) ** 0.5)
     state = jnp.concatenate([state_ref[:, i, :] for i in range(8)], 1)
-    if mix_ref:
-        state = jnp.dot(mix_ref[0][...], state, precision=HIGHEST, preferred_element_type=F32)
-    share = where_ref[6].astype(F32)
+    if mix_hbm:
+        state = jnp.dot(mix_ref[...], state, precision=HIGHEST, preferred_element_type=F32)
     par_anom = (state - jnp.mean(state, axis=0, keepdims=True)) * (share / (MEMBERS - 1) ** 0.5)
-    lefts = [jnp.concatenate(pair, 1) for pair in zip(split(anom), split(par_anom))]
+    lefts = [jnp.concatenate(pair, 1) for pair in zip(lefts_seen, split(par_anom))]
     nothing = jnp.zeros_like(innov)
     rights = [jnp.concatenate(pair, 1) for pair in zip((innov, nothing, nothing), split(-state))]
     lhs = jnp.concatenate(lefts, 0)
@@ -154,33 +183,33 @@
         out_ref[i] = packed
 
 
-def member_sums(where, preds, slab, *mix):
-    whole = lambda shape: pl.BlockSpec(shape, lambda i, w: (0,) * len(shape))
+def member_sums(preds, slab, *mix):
     return pl.pallas_call(
         sums_kernel,
         out_shape=pltpu.VMEM((32, 16, 128), F32),
-        grid_spec=pltpu.PrefetchScalarGridSpec(
-            num_scalar_prefetch=1,
-            grid=(1,),
-            in_specs=[
-                whole((32, 6, 128)),
-                pl.BlockSpec((32, 8, 128), lambda i, w: (0, w[3], w[4])),
-                pl.BlockSpec((32, 8, 256), lambda i, w: (0, w[5], w[7])),
-            ]
-            + [whole((32, 32)) for _ in mix],
-            out_specs=whole((32, 16, 128)),
-            scratch_shapes=[pltpu.VMEM((32, 6, 128), F32)],
-        ),
+        in_specs=[VMEM, ANY] + [ANY for _ in mix],
+        out_specs=VMEM,
+        scratch_shapes=[
+            pltpu.VMEM((32, 6, 128), F32),
+            pltpu.VMEM((32, 8, 128), F32),
+            pltpu.VMEM((32, 8, 256), F32),
+            pltpu.VMEM((32, 32), F32),
+            pltpu.SemaphoreType.DMA((3,)),
+        ],
         name="member_sums",
-    )(where, in_vmem(preds), slab, slab, *mix)
-
-
-def solve_kernel(last, where_ref, parts_ref, slab_ref, *rest):
-    *mix_ref, given_ref, state_ref, held_ref, step_ref, sem = rest
+    )(in_vmem(preds), slab, *mix)
+
+
+def solve_kernel(last, parts_ref, slab_ref, *rest):
+    *mix_hbm, given_ref, state_ref, held_ref, step_ref, mix_ref, sem, mix_sem = rest
+    z, core = lax.axis_index("z"), lax.axis_index("core")
+    if mix_hbm:
+        mix_fetch = pltpu.make_async_copy(mix_hbm[0], mix_ref, mix_sem)
+        mix_fetch.start()
     if last:
         wanted = slab_ref.at[:, pl.ds(NOTES, ROWS), :]
     else:
-        wanted = slab_ref.at[:, pl.ds(NOTES, ROWS), pl.ds(pl.multiple_of(where_ref[1] * 256, 256), 256)]
+        wanted = slab_ref.at[:, pl.ds(NOTES, ROWS), pl.ds(pl.multiple_of(core * 256, 256), 256)]
     fetch = pltpu.make_async_copy(wanted, held_ref, sem)
     fetch.start()
     both = parts_ref[0]
@@ -211,12 +240,13 @@
     )
     centred = turned - jnp.mean(turned, axis=1, keepdims=True)
     step = eye + centred / (MEMBERS - 1) ** 0.5
-    if mix_ref:
-        step = jnp.dot(step, mix_ref[0][...], precision=HIGHEST, preferred_element_type=F32)
+    if mix_hbm:
+        mix_fetch.wait()
+        step = jnp.dot(step, mix_ref[...], precision=HIGHEST, preferred_element_type=F32)
     step_ref[...] = step
     given_ref[...] = coefficients if last else step
     count = 2 if last else 4
-    rows = step_ref[pl.ds(where_ref[2 if last else 0], count), :]
+    rows = step_ref[pl.ds(z * 4 + core * 2 if last else z * 4, count), :]
     fetch.wait()
     for i in range(count):
         total = None
@@ -231,23 +261,25 @@
                 state_ref[y, i] = total.astype(BF16)
 
 
-def solve(last, where, parts, slab, *mix):
+def solve(last, parts, slab, *mix):
     if last:
         outs = jax.ShapeDtypeStruct((32, 32), F32), jax.ShapeDtypeStruct((2, ROWS * 512), F32)
     else:
-        outs = pltpu.VMEM((32, 32), F32), pltpu.VMEM((8, 4, ROWS, 256), BF16)
+        outs = jax.ShapeDtypeStruct((32, 32), F32), pltpu.VMEM((8, 4, ROWS, 256), BF16)
     return pl.pallas_call(
         functools.partial(solve_kernel, last),
         out_shape=outs,
-        in_specs=[SMEM, VMEM, pl.BlockSpec(memory_space=pl.ANY)] + [VMEM for _ in mix],
+        in_specs=[VMEM, ANY] + [ANY for _ in mix],
         out_specs=(VMEM,) * 2,
         scratch_shapes=[
             pltpu.VMEM((MEMBERS, ROWS, 512 if last else 256), F32),
             pltpu.VMEM((32, 32), F32),
+            pltpu.VMEM((32, 32), F32),
+            pltpu.SemaphoreType.DMA,
             pltpu.SemaphoreType.DMA,
         ],
         name="solve",
-    )(where, in_vmem(parts), slab, *mix)
+    )(in_vmem(parts), slab, *mix)
 
 
 def exchange(blocks, axes):
@@ -259,11 +291,7 @@
 
 
 def local(ensemble, inputs, features, query_index, observed, perturb):
-    z, core = lax.axis_index("z"), lax.axis_index("core")
-    e, block = z * 2 + core, core * 8 + z
-    where = jnp.stack(
-        [4 * z, core, 2 * e, block // 4, block % 4, 4 + jnp.minimum(e, 9) // 2, (e < 10).astype(jnp.int32), e % 2]
-    )
+    core = lax.axis_index("core")
     own, keep, give, ext = prepare(
         ensemble, inputs, query_index.reshape(96, 128), observed.reshape(1, -1), perturb
     )
@@ -277,13 +305,13 @@
         half = exchange(plane.reshape(32, ROWS, 256), ("y", "x")).reshape(32 * ROWS, 256)
         half, ext = lax.optimization_barrier((half, ext))
         other = swap(half)
-        preds = evaluate(where, half, other, ext, features)
+        preds = evaluate(half, other, ext, features)
         preds = exchange(preds, ("z", "x"))
-        parts = exchange(member_sums(where, preds, slab, *mix), ("x", "z"))
+        parts = exchange(member_sums(preds, slab, *mix), ("x", "z"))
         part = jnp.sum(parts, axis=0)
         parts = exchange(jnp.broadcast_to(part[None], (16, 16, 128)), ("core", "y"))
-        given, plane = solve(repeat == SUBSTEPS - 1, where, parts, slab, *mix)
-        mix = [in_vmem(given)]
+        given, plane = solve(repeat == SUBSTEPS - 1, parts, slab, *mix)
+        mix = [given]
     return (plane, given)
 
 

time: 195 us -> 190 us (0.974)
  Pallas kernels: 20.9 us -> 16 us
    pallas_call x2, Pallas kernels: 8.64 us -> 6.4 us  [solve(): pl.pallas_call(functools.partial(solve_kernel, last), out_shape=outs, in_...]
  transfers between devices with their start and end apart: 5 -> 5, of which waited for: 4 -> 4; matrix products, arithmetic and copies ran while one was open for 1% -> 0% of each run, Pallas kernels for 1% -> 1%
where the time goes in v6:
time: 190 us; the launch traced here: 189 us
  blocking collectives  130 us (68%)
  starting transfers between devices  21.8 us (11%)
  Pallas kernels  16 us (8%)
  between operations  14.2 us (7%)
  waiting for transfers between devices  5.66 us (3%)
    all_to_all x7, blocking collectives, exchange(): return lax.all_to_all(blocks, axes, 0, 0, tiled=True)  113 us
    ppermute x3, starting transfers between devices, swap(): return lax.ppermute(block, 'core', [(0, 1), (1, 0)])  17.5 us
    all_gather x1, blocking collectives, local(): ext = lax.all_gather(ext, 'x', axis=0, tiled=True)  17.4 us
    pallas_call x2, Pallas kernels, solve(): pl.pallas_call(functools.partial(solve_kernel, last), out_shape=outs, in_...  6.4 us
    all_to_all x1, starting transfers between devices, exchange(): return lax.all_to_all(blocks, axes, 0, 0, tiled=True)  4.3 us
    ppermute x3, waiting for transfers between devices, swap(): return lax.ppermute(block, 'core', [(0, 1), (1, 0)])  4.25 us
    pallas_call x2, Pallas kernels, evaluate(): pl.pallas_call(evaluate_kernel, out_shape=pltpu.VMEM((32, 6, 128), BF16),...  3.89 us
  transfers between devices with their start and end apart: 5, of which 4 were waited for; matrix products, arithmetic and copies ran while one was open for 0% of the time, Pallas kernels for 1%

profile of v6, /device:TPU:1, one launch (start us, length us, event | category | flops | bytes accessed | tf_op | source)
XLA Modules:
  0.0 189.1 jit_solution(8712241787530711397)
XLA Ops:
  7.2 0.0 all-gather.2.cloned.1.call-start
  7.2 2.0 %prepare.1 = (f32[2,72,512]{2,1,0:T(8,128)}, bf16[2,40,256]{2,1,0:T(8,128)(2,1)S(1)}, bf16[2,40,256]{2,1,0:T(8,128)(2,1)S(1)}, bf16[96,1152]{1,0:T(8,128)(2,1)S(1)}) custom-call(f32[2,20480]{1,0:T(2,128)} %ensemble_ref.1, bf16[192,1024]{1,0:T(8,128)(2,1)} %inputs_ref.1, s32[96,128]{1,0:T(8,128)} %bitcast.11, f32[1,12288]{1,0:T(1,128)} %bitcast.12, ...), custom_call_target="tpu_custom_call" | custom-call | tf_op jit(solution)/shard_map/prepare/pallas_call | solution.py:57
  9.2 0.0 all-gather.2.cloned.1.call-update
  9.3 8.8 %collective-permute-start = (bf16[2,40,256]{2,1,0:T(8,128)(2,1)S(1)}, bf16[2,40,256]{2,1,0:T(8,128)(2,1)S(1)}, u32[]{:S(2)}, u32[]{:S(2)}) collective-permute-start(bf16[2,40,256]{2,1,0:T(8,128)(2,1)S(1)} %get-tuple-element.15), channel_id=1, source_target_pairs={{0,32},{32,0},{1,33},{33,1},{2,34},{34,2},{3,35},{35,3},{4,36},{36... | collective-permute-start | bytes 122888 | tf_op jit(solution)/shard_map/ppermute | solution.py:290
  18.1 0.8 collective-permute-done
  18.9 0.9 broadcast_in_dim.6
  19.8 4.3 %all-to-all-start = ((bf16[32,40,256]{2,1,0:T(8,128)(2,1)}), bf16[32,40,256]{2,1,0:T(8,128)(2,1)S(1)}, u32[]{:S(2)}, u32[]{:S(2)}) async-start(bf16[32,40,256]{2,1,0:T(8,128)(2,1)} %bitcast.2), calls=%async_computation | async-start | bytes 1310720 | tf_op jit(solution)/shard_map/all_to_all | solution.py:286
  24.1 17.4 %all_gather.6.x_ref = bf16[384,1152]{1,0:T(8,128)(2,1)S(1)} all-gather(bf16[96,1152]{1,0:T(8,128)(2,1)S(1)} %get-tuple-element.16), channel_id=1, replica_groups=mesh['z'=8,'core'=2,'y'=8,'x'=4] {'x'}, dimensions={0}, use_global_device_ids=true | all-gather | bytes 1105920 | tf_op jit(solution)/shard_map/all_gather | solution.py:302
  41.5 1.4 all-to-all-done
  42.9 4.3 %collective-permute-start.1 = (bf16[1280,256]{1,0:T(8,128)(2,1)S(1)}, bf16[1280,256]{1,0:T(8,128)(2,1)S(1)}, u32[]{:S(2)}, u32[]{:S(2)}) collective-permute-start(bf16[1280,256]{1,0:T(8,128)(2,1)S(1)} %bitcast.6), channel_id=1, source_target_pairs={{0,32},{32,0},{1,33},{33,1},{2,34},{34,2},{3,35},{35,3},{4,36},{36... | collective-permute-start | bytes 1966088 | tf_op jit(solution)/shard_map/ppermute | solution.py:290
  47.2 1.7 collective-permute-done.1.other_ref
  48.9 1.9 %evaluate.2 = bf16[32,6,128]{2,1,0:T(8,128)(2,1)S(1)} custom-call(bf16[1280,256]{1,0:T(8,128)(2,1)S(1)} %bitcast.7, bf16[1280,256]{1,0:T(8,128)(2,1)S(1)} %collective-permute-done.1.other_ref, bf16[384,1152]{1,0:T(8,128)(2,1)S(1)} %all_gather.6.x_ref, bf16[128,256]{1,0:T(8,128)(2,1)} %features_hbm.3), custom_call_target="tpu_custom_call" | custom-call | tf_op jit(solution)/shard_map/evaluate/pallas_call | solution.py:118
  50.9 21.3 %all_to_all.40.preds_ref = bf16[32,6,128]{2,1,0:T(8,128)(2,1)S(1)} all-to-all(bf16[32,6,128]{2,1,0:T(8,128)(2,1)S(1)} %evaluate.2), channel_id=1, replica_groups=mesh['z'=8,'core'=2,'y'=8,'x'=4] {'z','x'}, dimensions={0} | all-to-all | bytes 98304 | tf_op jit(solution)/shard_map/all_to_all | solution.py:286
  72.1 0.0 all-gather.2.cloned.1.call-done.slab_ref
  72.1 1.7 member_sums.2
  73.9 12.8 %all_to_all.41 = f32[32,16,128]{2,1,0:T(8,128)S(1)} all-to-all(f32[32,16,128]{2,1,0:T(8,128)S(1)} %member_sums.2), channel_id=1, replica_groups=mesh['z'=8,'core'=2,'y'=8,'x'=4] {'x','z'}, dimensions={0} | all-to-all | bytes 524288 | tf_op jit(solution)/shard_map/all_to_all | solution.py:286
  86.7 15.3 %all_to_all.42.parts_ref = f32[16,16,128]{2,1,0:T(8,128)S(1)} all-to-all(f32[16,16,128]{2,1,0:T(8,128)S(1)} %broadcast_in_dim.7), channel_id=1, replica_groups=mesh['z'=8,'core'=2,'y'=8,'x'=4] {'core','y'}, dimensions={0} | all-to-all | bytes 262144 | tf_op jit(solution)/shard_map/all_to_all | solution.py:286
  102.1 3.0 %solve.2 = (f32[32,32]{1,0:T(8,128)}, bf16[8,4,40,256]{3,2,1,0:T(8,128)(2,1)S(1)}) custom-call(f32[16,16,128]{2,1,0:T(8,128)S(1)} %all_to_all.42.parts_ref, f32[32,72,512]{2,1,0:T(8,128)} %all-gather.2.cloned.1.call-done.slab_ref), custom_call_target="tpu_custom_call" | custom-call | tf_op jit(solution)/shard_map/solve/pallas_call | solution.py:269
  105.1 23.4 %all_to_all.43 = bf16[32,40,256]{2,1,0:T(8,128)(2,1)S(1)} all-to-all(bf16[32,40,256]{2,1,0:T(8,128)(2,1)S(1)} %bitcast.10), channel_id=1, replica_groups=mesh['z'=8,'core'=2,'y'=8,'x'=4] {'y','x'}, dimensions={0} | all-to-all | bytes 1310720 | tf_op jit(solution)/shard_map/all_to_all | solution.py:286
  128.5 4.4 %collective-permute-start.2 = (bf16[1280,256]{1,0:T(8,128)(2,1)S(1)}, bf16[1280,256]{1,0:T(8,128)(2,1)S(1)}, u32[]{:S(2)}, u32[]{:S(2)}) collective-permute-start(bf16[1280,256]{1,0:T(8,128)(2,1)S(1)} %bitcast.8), channel_id=1, source_target_pairs={{0,32},{32,0},{1,33},{33,1},{2,34},{34,2},{3,35},{35,3},{4,36},{36... | collective-permute-start | bytes 1966088 | tf_op jit(solution)/shard_map/ppermute | solution.py:290
  132.9 1.7 collective-permute-done.2.other_ref
  134.6 1.9 %evaluate.3 = bf16[32,6,128]{2,1,0:T(8,128)(2,1)S(1)} custom-call(bf16[1280,256]{1,0:T(8,128)(2,1)S(1)} %bitcast.9, bf16[1280,256]{1,0:T(8,128)(2,1)S(1)} %collective-permute-done.2.other_ref, bf16[384,1152]{1,0:T(8,128)(2,1)S(1)} %all_gather.6.x_ref, bf16[128,256]{1,0:T(8,128)(2,1)} %features_hbm.3), custom_call_target="tpu_custom_call" | custom-call | tf_op jit(solution)/shard_map/evaluate/pallas_call | solution.py:118
  136.5 14.0 %all_to_all.44.preds_ref = bf16[32,6,128]{2,1,0:T(8,128)(2,1)S(1)} all-to-all(bf16[32,6,128]{2,1,0:T(8,128)(2,1)S(1)} %evaluate.3), channel_id=1, replica_groups=mesh['z'=8,'core'=2,'y'=8,'x'=4] {'z','x'}, dimensions={0} | all-to-all | bytes 98304 | tf_op jit(solution)/shard_map/all_to_all | solution.py:286
  150.5 1.9 %member_sums.3 = f32[32,16,128]{2,1,0:T(8,128)S(1)} custom-call(bf16[32,6,128]{2,1,0:T(8,128)(2,1)S(1)} %all_to_all.44.preds_ref, f32[32,72,512]{2,1,0:T(8,128)} %all-gather.2.cloned.1.call-done.slab_ref, f32[32,32]{1,0:T(8,128)} %get-tuple-element.23.rest_0_), custom_call_target="tpu_custom_call" | custom-call | tf_op jit(solution)/shard_map/member_sums/pallas_call | solution.py:187
  152.5 12.8 %all_to_all.45 = f32[32,16,128]{2,1,0:T(8,128)S(1)} all-to-all(f32[32,16,128]{2,1,0:T(8,128)S(1)} %member_sums.3), channel_id=1, replica_groups=mesh['z'=8,'core'=2,'y'=8,'x'=4] {'x','z'}, dimensions={0} | all-to-all | bytes 524288 | tf_op jit(solution)/shard_map/all_to_all | solution.py:286
  165.3 13.4 %all_to_all.46.parts_ref = f32[16,16,128]{2,1,0:T(8,128)S(1)} all-to-all(f32[16,16,128]{2,1,0:T(8,128)S(1)} %broadcast_in_dim.8), channel_id=1, replica_groups=mesh['z'=8,'core'=2,'y'=8,'x'=4] {'core','y'}, dimensions={0} | all-to-all | bytes 262144 | tf_op jit(solution)/shard_map/all_to_all | solution.py:286
  178.8 3.4 %solve.3 = (f32[32,32]{1,0:T(8,128)}, f32[2,20480]{1,0:T(2,128)}) custom-call(f32[16,16,128]{2,1,0:T(8,128)S(1)} %all_to_all.46.parts_ref, f32[32,72,512]{2,1,0:T(8,128)} %all-gather.2.cloned.1.call-done.slab_ref, f32[32,32]{1,0:T(8,128)} %get-tuple-element.23.rest_0_), custom_call_target="tpu_custom_call" | custom-call | tf_op jit(solution)/shard_map/solve/pallas_call | solution.py:269
  (5 shorter events, 0.1 us)
Async XLA Ops:
  7.2 65.0 %all-gather.2.cloned.1.call-start = ((), (), s32[]{:S(2)}) async-start(), calls=%async_computation.8 | async-start | bytes 5013504 | tf_op jit(solution)/shard_map/all_gather | solution.py:298
  9.3 9.6 %collective-permute-start = (bf16[2,40,256]{2,1,0:T(8,128)(2,1)S(1)}, bf16[2,40,256]{2,1,0:T(8,128)(2,1)S(1)}, u32[]{:S(2)}, u32[]{:S(2)}) collective-permute-start(bf16[2,40,256]{2,1,0:T(8,128)(2,1)S(1)} %get-tuple-element.15), channel_id=1, source_target_pairs={{0,32},{32,0},{1,33},{33,1},{2,34},{34,2},{3,35},{35,3},{4,36},{36... | collective-permute-start | bytes 122888 | tf_op jit(solution)/shard_map/ppermute | solution.py:290
  19.8 23.1 %all-to-all-start = ((bf16[32,40,256]{2,1,0:T(8,128)(2,1)}), bf16[32,40,256]{2,1,0:T(8,128)(2,1)S(1)}, u32[]{:S(2)}, u32[]{:S(2)}) async-start(bf16[32,40,256]{2,1,0:T(8,128)(2,1)} %bitcast.2), calls=%async_computation | async-start | bytes 1310720 | tf_op jit(solution)/shard_map/all_to_all | solution.py:286
  42.9 6.0 %collective-permute-start.1 = (bf16[1280,256]{1,0:T(8,128)(2,1)S(1)}, bf16[1280,256]{1,0:T(8,128)(2,1)S(1)}, u32[]{:S(2)}, u32[]{:S(2)}) collective-permute-start(bf16[1280,256]{1,0:T(8,128)(2,1)S(1)} %bitcast.6), channel_id=1, source_target_pairs={{0,32},{32,0},{1,33},{33,1},{2,34},{34,2},{3,35},{35,3},{4,36},{36... | collective-permute-start | bytes 1966088 | tf_op jit(solution)/shard_map/ppermute | solution.py:290
  128.5 6.1 %collective-permute-start.2 = (bf16[1280,256]{1,0:T(8,128)(2,1)S(1)}, bf16[1280,256]{1,0:T(8,128)(2,1)S(1)}, u32[]{:S(2)}, u32[]{:S(2)}) collective-permute-start(bf16[1280,256]{1,0:T(8,128)(2,1)S(1)} %bitcast.8), channel_id=1, source_target_pairs={{0,32},{32,0},{1,33},{33,1},{2,34},{34,2},{3,35},{35,3},{4,36},{36... | collective-permute-start | bytes 1966088 | tf_op jit(solution)/shard_map/ppermute | solution.py:290
Sparse Core Ops, SparseCore 0:
  10.1 51.9 all-gather.1

commit v7 on v6

--- a/solution.py
+++ b/solution.py
@@ -200,6 +200,33 @@
     )(in_vmem(preds), slab, *mix)
 
 
+STEP = 4
+
+
+def solve_block(block, right):
+    half = len(block) // 2
+    if half == 1:
+        (a, b), (c, d) = block
+        inverse = 1.0 / (a * d - b * c)
+        return [
+            [(d * u - b * l) * inverse for u, l in zip(*right)],
+            [(a * l - c * u) * inverse for u, l in zip(*right)],
+        ]
+
+    def less(rows, factors, others):
+        return [
+            [x - sum(f * o[j] for f, o in zip(factor, others)) for j, x in enumerate(row)]
+            for row, factor in zip(rows, factors)
+        ]
+
+    upper, lower = block[:half], block[half:]
+    solved = solve_block([row[:half] for row in upper], [row[half:] + r for row, r in zip(upper, right)])
+    edge, top = [row[:half] for row in solved], [row[half:] for row in solved]
+    left = [row[:half] for row in lower]
+    bottom = solve_block(less([row[half:] for row in lower], left, edge), less(right[half:], left, top))
+    return less(top, edge, bottom) + bottom
+
+
 def solve_kernel(last, parts_ref, slab_ref, *rest):
     *mix_hbm, given_ref, state_ref, held_ref, step_ref, mix_ref, sem, mix_sem = rest
     z, core = lax.axis_index("z"), lax.axis_index("core")
@@ -224,16 +251,14 @@
     system = gram + (RIDGE_SHARE / MEMBERS) * trace * eye
     table = jnp.concatenate([system, cross], 1)
     line = lax.broadcasted_iota(jnp.int32, (32, 64), 0)
-    for k in range(0, 32, 2):
-        first = jnp.broadcast_to(table[:, k : k + 1], (32, 64))
-        second = jnp.broadcast_to(table[:, k + 1 : k + 2], (32, 64))
-        upper, lower = table[k : k + 1, :], table[k + 1 : k + 2, :]
-        a, b, c, d = first[k : k + 1], second[k : k + 1], first[k + 1 : k + 2], second[k + 1 : k + 2]
-        inverse = 1.0 / (a * d - b * c)
-        new_upper = (d * upper - b * lower) * inverse
-        new_lower = (a * lower - c * upper) * inverse
-        rest = table - first * new_upper - second * new_lower
-        table = jnp.where(line == k, new_upper, jnp.where(line == k + 1, new_lower, rest))
+    for k in range(0, 32, STEP):
+        columns = [jnp.broadcast_to(table[:, k + j : k + j + 1], (32, 64)) for j in range(STEP)]
+        block = [[column[k + i : k + i + 1] for column in columns] for i in range(STEP)]
+        rows = solve_block(block, [[table[k + i : k + i + 1, :]] for i in range(STEP)])
+        for column, (row,) in zip(columns, rows):
+            table = table - column * row
+        for i, (row,) in enumerate(rows):
+            table = jnp.where(line == k + i, row, table)
     coefficients = table[:, 32:64]
     turned = lax.dot_general(
         coefficients, eye, (((0,), (0,)), ((), ())), precision=HIGHEST, preferred_element_type=F32

time: 190 us -> 190 us (level)
  no operation moved by 1% of the time
where the time goes in v7:
time: 190 us; the launch traced here: 189 us
  blocking collectives  130 us (68%)
  starting transfers between devices  21.8 us (11%)
  Pallas kernels  16.1 us (8%)
  between operations  14.2 us (7%)
  waiting for transfers between devices  5.66 us (3%)
    all_to_all x7, blocking collectives, exchange(): return lax.all_to_all(blocks, axes, 0, 0, tiled=True)  113 us
    ppermute x3, starting transfers between devices, swap(): return lax.ppermute(block, 'core', [(0, 1), (1, 0)])  17.5 us
    all_gather x1, blocking collectives, local(): ext = lax.all_gather(ext, 'x', axis=0, tiled=True)  17.4 us
    pallas_call x2, Pallas kernels, solve(): pl.pallas_call(functools.partial(solve_kernel, last), out_shape=outs, in_...  6.52 us
    all_to_all x1, starting transfers between devices, exchange(): return lax.all_to_all(blocks, axes, 0, 0, tiled=True)  4.3 us
    ppermute x3, waiting for transfers between devices, swap(): return lax.ppermute(block, 'core', [(0, 1), (1, 0)])  4.25 us
    pallas_call x2, Pallas kernels, evaluate(): pl.pallas_call(evaluate_kernel, out_shape=pltpu.VMEM((32, 6, 128), BF16),...  3.89 us
  transfers between devices with their start and end apart: 5, of which 4 were waited for; matrix products, arithmetic and copies ran while one was open for 0% of the time, Pallas kernels for 1%

profile of v7, /device:TPU:1, one launch (start us, length us, event | category | flops | bytes accessed | tf_op | source)
XLA Modules:
  0.0 189.2 jit_solution(8680358975848615161)
XLA Ops:
  7.2 0.0 all-gather.2.cloned.1.call-start
  7.2 2.0 %prepare.1 = (f32[2,72,512]{2,1,0:T(8,128)}, bf16[2,40,256]{2,1,0:T(8,128)(2,1)S(1)}, bf16[2,40,256]{2,1,0:T(8,128)(2,1)S(1)}, bf16[96,1152]{1,0:T(8,128)(2,1)S(1)}) custom-call(f32[2,20480]{1,0:T(2,128)} %ensemble_ref.1, bf16[192,1024]{1,0:T(8,128)(2,1)} %inputs_ref.1, s32[96,128]{1,0:T(8,128)} %bitcast.11, f32[1,12288]{1,0:T(1,128)} %bitcast.12, ...), custom_call_target="tpu_custom_call" | custom-call | tf_op jit(solution)/shard_map/prepare/pallas_call | solution.py:57
  9.2 0.0 all-gather.2.cloned.1.call-update
  9.3 8.8 %collective-permute-start = (bf16[2,40,256]{2,1,0:T(8,128)(2,1)S(1)}, bf16[2,40,256]{2,1,0:T(8,128)(2,1)S(1)}, u32[]{:S(2)}, u32[]{:S(2)}) collective-permute-start(bf16[2,40,256]{2,1,0:T(8,128)(2,1)S(1)} %get-tuple-element.15), channel_id=1, source_target_pairs={{0,32},{32,0},{1,33},{33,1},{2,34},{34,2},{3,35},{35,3},{4,36},{36... | collective-permute-start | bytes 122888 | tf_op jit(solution)/shard_map/ppermute | solution.py:315
  18.1 0.8 collective-permute-done
  18.9 0.9 broadcast_in_dim.6
  19.8 4.3 %all-to-all-start = ((bf16[32,40,256]{2,1,0:T(8,128)(2,1)}), bf16[32,40,256]{2,1,0:T(8,128)(2,1)S(1)}, u32[]{:S(2)}, u32[]{:S(2)}) async-start(bf16[32,40,256]{2,1,0:T(8,128)(2,1)} %bitcast.2), calls=%async_computation | async-start | bytes 1310720 | tf_op jit(solution)/shard_map/all_to_all | solution.py:311
  24.1 17.4 %all_gather.6.x_ref = bf16[384,1152]{1,0:T(8,128)(2,1)S(1)} all-gather(bf16[96,1152]{1,0:T(8,128)(2,1)S(1)} %get-tuple-element.16), channel_id=1, replica_groups=mesh['z'=8,'core'=2,'y'=8,'x'=4] {'x'}, dimensions={0}, use_global_device_ids=true | all-gather | bytes 1105920 | tf_op jit(solution)/shard_map/all_gather | solution.py:327
  41.5 1.4 all-to-all-done
  42.9 4.3 %collective-permute-start.1 = (bf16[1280,256]{1,0:T(8,128)(2,1)S(1)}, bf16[1280,256]{1,0:T(8,128)(2,1)S(1)}, u32[]{:S(2)}, u32[]{:S(2)}) collective-permute-start(bf16[1280,256]{1,0:T(8,128)(2,1)S(1)} %bitcast.6), channel_id=1, source_target_pairs={{0,32},{32,0},{1,33},{33,1},{2,34},{34,2},{3,35},{35,3},{4,36},{36... | collective-permute-start | bytes 1966088 | tf_op jit(solution)/shard_map/ppermute | solution.py:315
  47.2 1.7 collective-permute-done.1.other_ref
  48.9 1.9 %evaluate.2 = bf16[32,6,128]{2,1,0:T(8,128)(2,1)S(1)} custom-call(bf16[1280,256]{1,0:T(8,128)(2,1)S(1)} %bitcast.7, bf16[1280,256]{1,0:T(8,128)(2,1)S(1)} %collective-permute-done.1.other_ref, bf16[384,1152]{1,0:T(8,128)(2,1)S(1)} %all_gather.6.x_ref, bf16[128,256]{1,0:T(8,128)(2,1)} %features_hbm.3), custom_call_target="tpu_custom_call" | custom-call | tf_op jit(solution)/shard_map/evaluate/pallas_call | solution.py:118
  50.9 21.3 %all_to_all.40.preds_ref = bf16[32,6,128]{2,1,0:T(8,128)(2,1)S(1)} all-to-all(bf16[32,6,128]{2,1,0:T(8,128)(2,1)S(1)} %evaluate.2), channel_id=1, replica_groups=mesh['z'=8,'core'=2,'y'=8,'x'=4] {'z','x'}, dimensions={0} | all-to-all | bytes 98304 | tf_op jit(solution)/shard_map/all_to_all | solution.py:311
  72.1 0.0 all-gather.2.cloned.1.call-done.slab_ref
  72.1 1.7 member_sums.2
  73.9 12.8 %all_to_all.41 = f32[32,16,128]{2,1,0:T(8,128)S(1)} all-to-all(f32[32,16,128]{2,1,0:T(8,128)S(1)} %member_sums.2), channel_id=1, replica_groups=mesh['z'=8,'core'=2,'y'=8,'x'=4] {'x','z'}, dimensions={0} | all-to-all | bytes 524288 | tf_op jit(solution)/shard_map/all_to_all | solution.py:311
  86.7 15.3 %all_to_all.42.parts_ref = f32[16,16,128]{2,1,0:T(8,128)S(1)} all-to-all(f32[16,16,128]{2,1,0:T(8,128)S(1)} %broadcast_in_dim.7), channel_id=1, replica_groups=mesh['z'=8,'core'=2,'y'=8,'x'=4] {'core','y'}, dimensions={0} | all-to-all | bytes 262144 | tf_op jit(solution)/shard_map/all_to_all | solution.py:311
  102.1 2.5 %solve.2 = (f32[32,32]{1,0:T(8,128)}, bf16[8,4,40,256]{3,2,1,0:T(8,128)(2,1)S(1)}) custom-call(f32[16,16,128]{2,1,0:T(8,128)S(1)} %all_to_all.42.parts_ref, f32[32,72,512]{2,1,0:T(8,128)} %all-gather.2.cloned.1.call-done.slab_ref), custom_call_target="tpu_custom_call" | custom-call | tf_op jit(solution)/shard_map/solve/pallas_call | solution.py:294
  104.5 23.4 %all_to_all.43 = bf16[32,40,256]{2,1,0:T(8,128)(2,1)S(1)} all-to-all(bf16[32,40,256]{2,1,0:T(8,128)(2,1)S(1)} %bitcast.10), channel_id=1, replica_groups=mesh['z'=8,'core'=2,'y'=8,'x'=4] {'y','x'}, dimensions={0} | all-to-all | bytes 1310720 | tf_op jit(solution)/shard_map/all_to_all | solution.py:311
  127.9 4.4 %collective-permute-start.2 = (bf16[1280,256]{1,0:T(8,128)(2,1)S(1)}, bf16[1280,256]{1,0:T(8,128)(2,1)S(1)}, u32[]{:S(2)}, u32[]{:S(2)}) collective-permute-start(bf16[1280,256]{1,0:T(8,128)(2,1)S(1)} %bitcast.8), channel_id=1, source_target_pairs={{0,32},{32,0},{1,33},{33,1},{2,34},{34,2},{3,35},{35,3},{4,36},{36... | collective-permute-start | bytes 1966088 | tf_op jit(solution)/shard_map/ppermute | solution.py:315
  132.3 1.7 collective-permute-done.2.other_ref
  134.0 1.9 %evaluate.3 = bf16[32,6,128]{2,1,0:T(8,128)(2,1)S(1)} custom-call(bf16[1280,256]{1,0:T(8,128)(2,1)S(1)} %bitcast.9, bf16[1280,256]{1,0:T(8,128)(2,1)S(1)} %collective-permute-done.2.other_ref, bf16[384,1152]{1,0:T(8,128)(2,1)S(1)} %all_gather.6.x_ref, bf16[128,256]{1,0:T(8,128)(2,1)} %features_hbm.3), custom_call_target="tpu_custom_call" | custom-call | tf_op jit(solution)/shard_map/evaluate/pallas_call | solution.py:118
  136.0 14.0 %all_to_all.44.preds_ref = bf16[32,6,128]{2,1,0:T(8,128)(2,1)S(1)} all-to-all(bf16[32,6,128]{2,1,0:T(8,128)(2,1)S(1)} %evaluate.3), channel_id=1, replica_groups=mesh['z'=8,'core'=2,'y'=8,'x'=4] {'z','x'}, dimensions={0} | all-to-all | bytes 98304 | tf_op jit(solution)/shard_map/all_to_all | solution.py:311
  150.0 1.9 %member_sums.3 = f32[32,16,128]{2,1,0:T(8,128)S(1)} custom-call(bf16[32,6,128]{2,1,0:T(8,128)(2,1)S(1)} %all_to_all.44.preds_ref, f32[32,72,512]{2,1,0:T(8,128)} %all-gather.2.cloned.1.call-done.slab_ref, f32[32,32]{1,0:T(8,128)} %get-tuple-element.23.rest_0_), custom_call_target="tpu_custom_call" | custom-call | tf_op jit(solution)/shard_map/member_sums/pallas_call | solution.py:187
  152.0 12.8 %all_to_all.45 = f32[32,16,128]{2,1,0:T(8,128)S(1)} all-to-all(f32[32,16,128]{2,1,0:T(8,128)S(1)} %member_sums.3), channel_id=1, replica_groups=mesh['z'=8,'core'=2,'y'=8,'x'=4] {'x','z'}, dimensions={0} | all-to-all | bytes 524288 | tf_op jit(solution)/shard_map/all_to_all | solution.py:311
  164.8 13.4 %all_to_all.46.parts_ref = f32[16,16,128]{2,1,0:T(8,128)S(1)} all-to-all(f32[16,16,128]{2,1,0:T(8,128)S(1)} %broadcast_in_dim.8), channel_id=1, replica_groups=mesh['z'=8,'core'=2,'y'=8,'x'=4] {'core','y'}, dimensions={0} | all-to-all | bytes 262144 | tf_op jit(solution)/shard_map/all_to_all | solution.py:311
  178.2 4.1 %solve.3 = (f32[32,32]{1,0:T(8,128)}, f32[2,20480]{1,0:T(2,128)}) custom-call(f32[16,16,128]{2,1,0:T(8,128)S(1)} %all_to_all.46.parts_ref, f32[32,72,512]{2,1,0:T(8,128)} %all-gather.2.cloned.1.call-done.slab_ref, f32[32,32]{1,0:T(8,128)} %get-tuple-element.23.rest_0_), custom_call_target="tpu_custom_call" | custom-call | tf_op jit(solution)/shard_map/solve/pallas_call | solution.py:294
  (5 shorter events, 0.1 us)
Async XLA Ops:
  7.2 65.0 %all-gather.2.cloned.1.call-start = ((), (), s32[]{:S(2)}) async-start(), calls=%async_computation.8 | async-start | bytes 5013504 | tf_op jit(solution)/shard_map/all_gather | solution.py:323
  9.3 9.6 %collective-permute-start = (bf16[2,40,256]{2,1,0:T(8,128)(2,1)S(1)}, bf16[2,40,256]{2,1,0:T(8,128)(2,1)S(1)}, u32[]{:S(2)}, u32[]{:S(2)}) collective-permute-start(bf16[2,40,256]{2,1,0:T(8,128)(2,1)S(1)} %get-tuple-element.15), channel_id=1, source_target_pairs={{0,32},{32,0},{1,33},{33,1},{2,34},{34,2},{3,35},{35,3},{4,36},{36... | collective-permute-start | bytes 122888 | tf_op jit(solution)/shard_map/ppermute | solution.py:315
  19.8 23.1 %all-to-all-start = ((bf16[32,40,256]{2,1,0:T(8,128)(2,1)}), bf16[32,40,256]{2,1,0:T(8,128)(2,1)S(1)}, u32[]{:S(2)}, u32[]{:S(2)}) async-start(bf16[32,40,256]{2,1,0:T(8,128)(2,1)} %bitcast.2), calls=%async_computation | async-start | bytes 1310720 | tf_op jit(solution)/shard_map/all_to_all | solution.py:311
  42.9 6.0 %collective-permute-start.1 = (bf16[1280,256]{1,0:T(8,128)(2,1)S(1)}, bf16[1280,256]{1,0:T(8,128)(2,1)S(1)}, u32[]{:S(2)}, u32[]{:S(2)}) collective-permute-start(bf16[1280,256]{1,0:T(8,128)(2,1)S(1)} %bitcast.6), channel_id=1, source_target_pairs={{0,32},{32,0},{1,33},{33,1},{2,34},{34,2},{3,35},{35,3},{4,36},{36... | collective-permute-start | bytes 1966088 | tf_op jit(solution)/shard_map/ppermute | solution.py:315
  127.9 6.1 %collective-permute-start.2 = (bf16[1280,256]{1,0:T(8,128)(2,1)S(1)}, bf16[1280,256]{1,0:T(8,128)(2,1)S(1)}, u32[]{:S(2)}, u32[]{:S(2)}) collective-permute-start(bf16[1280,256]{1,0:T(8,128)(2,1)S(1)} %bitcast.8), channel_id=1, source_target_pairs={{0,32},{32,0},{1,33},{33,1},{2,34},{34,2},{3,35},{35,3},{4,36},{36... | collective-permute-start | bytes 1966088 | tf_op jit(solution)/shard_map/ppermute | solution.py:315
Sparse Core Ops, SparseCore 0:
  10.1 51.9 all-gather.1

commit v8 on v7

--- a/solution.py
+++ b/solution.py
@@ -200,9 +200,6 @@
     )(in_vmem(preds), slab, *mix)
 
 
-STEP = 4
-
-
 def solve_block(block, right):
     half = len(block) // 2
     if half == 1:
@@ -228,7 +225,7 @@
 
 
 def solve_kernel(last, parts_ref, slab_ref, *rest):
-    *mix_hbm, given_ref, state_ref, held_ref, step_ref, mix_ref, sem, mix_sem = rest
+    *mix_hbm, given_ref, state_ref, held_ref, mixing_ref, mix_ref, sem, mix_sem = rest
     z, core = lax.axis_index("z"), lax.axis_index("core")
     if mix_hbm:
         mix_fetch = pltpu.make_async_copy(mix_hbm[0], mix_ref, mix_sem)
@@ -251,10 +248,11 @@
     system = gram + (RIDGE_SHARE / MEMBERS) * trace * eye
     table = jnp.concatenate([system, cross], 1)
     line = lax.broadcasted_iota(jnp.int32, (32, 64), 0)
-    for k in range(0, 32, STEP):
-        columns = [jnp.broadcast_to(table[:, k + j : k + j + 1], (32, 64)) for j in range(STEP)]
-        block = [[column[k + i : k + i + 1] for column in columns] for i in range(STEP)]
-        rows = solve_block(block, [[table[k + i : k + i + 1, :]] for i in range(STEP)])
+    step = 2 if last else 4
+    for k in range(0, 32, step):
+        columns = [jnp.broadcast_to(table[:, k + j : k + j + 1], (32, 64)) for j in range(step)]
+        block = [[column[k + i : k + i + 1] for column in columns] for i in range(step)]
+        rows = solve_block(block, [[table[k + i : k + i + 1, :]] for i in range(step)])
         for column, (row,) in zip(columns, rows):
             table = table - column * row
         for i, (row,) in enumerate(rows):
@@ -264,14 +262,14 @@
         coefficients, eye, (((0,), (0,)), ((), ())), precision=HIGHEST, preferred_element_type=F32
     )
     centred = turned - jnp.mean(turned, axis=1, keepdims=True)
-    step = eye + centred / (MEMBERS - 1) ** 0.5
+    mixing = eye + centred / (MEMBERS - 1) ** 0.5
     if mix_hbm:
         mix_fetch.wait()
-        step = jnp.dot(step, mix_ref[...], precision=HIGHEST, preferred_element_type=F32)
-    step_ref[...] = step
-    given_ref[...] = coefficients if last else step
+        mixing = jnp.dot(mixing, mix_ref[...], precision=HIGHEST, preferred_element_type=F32)
+    mixing_ref[...] = mixing
+    given_ref[...] = coefficients if last else mixing
     count = 2 if last else 4
-    rows = step_ref[pl.ds(z * 4 + core * 2 if last else z * 4, count), :]
+    rows = mixing_ref[pl.ds(z * 4 + core * 2 if last else z * 4, count), :]
     fetch.wait()
     for i in range(count):
         total = None

time: 190 us -> 189 us (level)
  no operation moved by 1% of the time
where the time goes in v8:
time: 189 us
  blocking collectives  130 us (69%)
  starting transfers between devices  21.8 us (12%)
  Pallas kernels  15.5 us (8%)
  between operations  14.2 us (8%)
  waiting for transfers between devices  5.66 us (3%)
    all_to_all x7, blocking collectives, exchange(): return lax.all_to_all(blocks, axes, 0, 0, tiled=True)  113 us
    ppermute x3, starting transfers between devices, swap(): return lax.ppermute(block, 'core', [(0, 1), (1, 0)])  17.5 us
    all_gather x1, blocking collectives, local(): ext = lax.all_gather(ext, 'x', axis=0, tiled=True)  17.4 us
    pallas_call x2, Pallas kernels, solve(): pl.pallas_call(functools.partial(solve_kernel, last), out_shape=outs, in_...  5.86 us
    all_to_all x1, starting transfers between devices, exchange(): return lax.all_to_all(blocks, axes, 0, 0, tiled=True)  4.3 us
    ppermute x3, waiting for transfers between devices, swap(): return lax.ppermute(block, 'core', [(0, 1), (1, 0)])  4.25 us
    pallas_call x2, Pallas kernels, evaluate(): pl.pallas_call(evaluate_kernel, out_shape=pltpu.VMEM((32, 6, 128), BF16),...  3.89 us
  transfers between devices with their start and end apart: 5, of which 4 were waited for; matrix products, arithmetic and copies ran while one was open for 0% of the time, Pallas kernels for 1%

profile of v8, /device:TPU:1, one launch (start us, length us, event | category | flops | bytes accessed | tf_op | source)
XLA Modules:
  0.0 188.5 jit_solution(17964842652993309701)
XLA Ops:
  7.2 0.0 all-gather.2.cloned.1.call-start
  7.2 2.0 %prepare.1 = (f32[2,72,512]{2,1,0:T(8,128)}, bf16[2,40,256]{2,1,0:T(8,128)(2,1)S(1)}, bf16[2,40,256]{2,1,0:T(8,128)(2,1)S(1)}, bf16[96,1152]{1,0:T(8,128)(2,1)S(1)}) custom-call(f32[2,20480]{1,0:T(2,128)} %ensemble_ref.1, bf16[192,1024]{1,0:T(8,128)(2,1)} %inputs_ref.1, s32[96,128]{1,0:T(8,128)} %bitcast.11, f32[1,12288]{1,0:T(1,128)} %bitcast.12, ...), custom_call_target="tpu_custom_call" | custom-call | tf_op jit(solution)/shard_map/prepare/pallas_call | solution.py:57
  9.2 0.0 all-gather.2.cloned.1.call-update
  9.3 8.8 %collective-permute-start = (bf16[2,40,256]{2,1,0:T(8,128)(2,1)S(1)}, bf16[2,40,256]{2,1,0:T(8,128)(2,1)S(1)}, u32[]{:S(2)}, u32[]{:S(2)}) collective-permute-start(bf16[2,40,256]{2,1,0:T(8,128)(2,1)S(1)} %get-tuple-element.15), channel_id=1, source_target_pairs={{0,32},{32,0},{1,33},{33,1},{2,34},{34,2},{3,35},{35,3},{4,36},{36... | collective-permute-start | bytes 122888 | tf_op jit(solution)/shard_map/ppermute | solution.py:313
  18.1 0.8 collective-permute-done
  18.9 0.9 broadcast_in_dim.6
  19.8 4.3 %all-to-all-start = ((bf16[32,40,256]{2,1,0:T(8,128)(2,1)}), bf16[32,40,256]{2,1,0:T(8,128)(2,1)S(1)}, u32[]{:S(2)}, u32[]{:S(2)}) async-start(bf16[32,40,256]{2,1,0:T(8,128)(2,1)} %bitcast.2), calls=%async_computation | async-start | bytes 1310720 | tf_op jit(solution)/shard_map/all_to_all | solution.py:309
  24.1 17.4 %all_gather.6.x_ref = bf16[384,1152]{1,0:T(8,128)(2,1)S(1)} all-gather(bf16[96,1152]{1,0:T(8,128)(2,1)S(1)} %get-tuple-element.16), channel_id=1, replica_groups=mesh['z'=8,'core'=2,'y'=8,'x'=4] {'x'}, dimensions={0}, use_global_device_ids=true | all-gather | bytes 1105920 | tf_op jit(solution)/shard_map/all_gather | solution.py:325
  41.5 1.4 all-to-all-done
  42.9 4.3 %collective-permute-start.1 = (bf16[1280,256]{1,0:T(8,128)(2,1)S(1)}, bf16[1280,256]{1,0:T(8,128)(2,1)S(1)}, u32[]{:S(2)}, u32[]{:S(2)}) collective-permute-start(bf16[1280,256]{1,0:T(8,128)(2,1)S(1)} %bitcast.6), channel_id=1, source_target_pairs={{0,32},{32,0},{1,33},{33,1},{2,34},{34,2},{3,35},{35,3},{4,36},{36... | collective-permute-start | bytes 1966088 | tf_op jit(solution)/shard_map/ppermute | solution.py:313
  47.2 1.7 collective-permute-done.1.other_ref
  48.9 1.9 %evaluate.2 = bf16[32,6,128]{2,1,0:T(8,128)(2,1)S(1)} custom-call(bf16[1280,256]{1,0:T(8,128)(2,1)S(1)} %bitcast.7, bf16[1280,256]{1,0:T(8,128)(2,1)S(1)} %collective-permute-done.1.other_ref, bf16[384,1152]{1,0:T(8,128)(2,1)S(1)} %all_gather.6.x_ref, bf16[128,256]{1,0:T(8,128)(2,1)} %features_hbm.3), custom_call_target="tpu_custom_call" | custom-call | tf_op jit(solution)/shard_map/evaluate/pallas_call | solution.py:118
  50.9 21.3 %all_to_all.40.preds_ref = bf16[32,6,128]{2,1,0:T(8,128)(2,1)S(1)} all-to-all(bf16[32,6,128]{2,1,0:T(8,128)(2,1)S(1)} %evaluate.2), channel_id=1, replica_groups=mesh['z'=8,'core'=2,'y'=8,'x'=4] {'z','x'}, dimensions={0} | all-to-all | bytes 98304 | tf_op jit(solution)/shard_map/all_to_all | solution.py:309
  72.1 0.0 all-gather.2.cloned.1.call-done.slab_ref
  72.1 1.7 member_sums.2
  73.9 12.8 %all_to_all.41 = f32[32,16,128]{2,1,0:T(8,128)S(1)} all-to-all(f32[32,16,128]{2,1,0:T(8,128)S(1)} %member_sums.2), channel_id=1, replica_groups=mesh['z'=8,'core'=2,'y'=8,'x'=4] {'x','z'}, dimensions={0} | all-to-all | bytes 524288 | tf_op jit(solution)/shard_map/all_to_all | solution.py:309
  86.7 15.3 %all_to_all.42.parts_ref = f32[16,16,128]{2,1,0:T(8,128)S(1)} all-to-all(f32[16,16,128]{2,1,0:T(8,128)S(1)} %broadcast_in_dim.7), channel_id=1, replica_groups=mesh['z'=8,'core'=2,'y'=8,'x'=4] {'core','y'}, dimensions={0} | all-to-all | bytes 262144 | tf_op jit(solution)/shard_map/all_to_all | solution.py:309
  102.1 2.5 %solve.2 = (f32[32,32]{1,0:T(8,128)}, bf16[8,4,40,256]{3,2,1,0:T(8,128)(2,1)S(1)}) custom-call(f32[16,16,128]{2,1,0:T(8,128)S(1)} %all_to_all.42.parts_ref, f32[32,72,512]{2,1,0:T(8,128)} %all-gather.2.cloned.1.call-done.slab_ref), custom_call_target="tpu_custom_call" | custom-call | tf_op jit(solution)/shard_map/solve/pallas_call | solution.py:292
  104.5 23.4 %all_to_all.43 = bf16[32,40,256]{2,1,0:T(8,128)(2,1)S(1)} all-to-all(bf16[32,40,256]{2,1,0:T(8,128)(2,1)S(1)} %bitcast.10), channel_id=1, replica_groups=mesh['z'=8,'core'=2,'y'=8,'x'=4] {'y','x'}, dimensions={0} | all-to-all | bytes 1310720 | tf_op jit(solution)/shard_map/all_to_all | solution.py:309
  127.9 4.4 %collective-permute-start.2 = (bf16[1280,256]{1,0:T(8,128)(2,1)S(1)}, bf16[1280,256]{1,0:T(8,128)(2,1)S(1)}, u32[]{:S(2)}, u32[]{:S(2)}) collective-permute-start(bf16[1280,256]{1,0:T(8,128)(2,1)S(1)} %bitcast.8), channel_id=1, source_target_pairs={{0,32},{32,0},{1,33},{33,1},{2,34},{34,2},{3,35},{35,3},{4,36},{36... | collective-permute-start | bytes 1966088 | tf_op jit(solution)/shard_map/ppermute | solution.py:313
  132.3 1.7 collective-permute-done.2.other_ref
  134.0 1.9 %evaluate.3 = bf16[32,6,128]{2,1,0:T(8,128)(2,1)S(1)} custom-call(bf16[1280,256]{1,0:T(8,128)(2,1)S(1)} %bitcast.9, bf16[1280,256]{1,0:T(8,128)(2,1)S(1)} %collective-permute-done.2.other_ref, bf16[384,1152]{1,0:T(8,128)(2,1)S(1)} %all_gather.6.x_ref, bf16[128,256]{1,0:T(8,128)(2,1)} %features_hbm.3), custom_call_target="tpu_custom_call" | custom-call | tf_op jit(solution)/shard_map/evaluate/pallas_call | solution.py:118
  136.0 14.0 %all_to_all.44.preds_ref = bf16[32,6,128]{2,1,0:T(8,128)(2,1)S(1)} all-to-all(bf16[32,6,128]{2,1,0:T(8,128)(2,1)S(1)} %evaluate.3), channel_id=1, replica_groups=mesh['z'=8,'core'=2,'y'=8,'x'=4] {'z','x'}, dimensions={0} | all-to-all | bytes 98304 | tf_op jit(solution)/shard_map/all_to_all | solution.py:309
  150.0 1.9 %member_sums.3 = f32[32,16,128]{2,1,0:T(8,128)S(1)} custom-call(bf16[32,6,128]{2,1,0:T(8,128)(2,1)S(1)} %all_to_all.44.preds_ref, f32[32,72,512]{2,1,0:T(8,128)} %all-gather.2.cloned.1.call-done.slab_ref, f32[32,32]{1,0:T(8,128)} %get-tuple-element.23.rest_0_), custom_call_target="tpu_custom_call" | custom-call | tf_op jit(solution)/shard_map/member_sums/pallas_call | solution.py:187
  152.0 12.8 %all_to_all.45 = f32[32,16,128]{2,1,0:T(8,128)S(1)} all-to-all(f32[32,16,128]{2,1,0:T(8,128)S(1)} %member_sums.3), channel_id=1, replica_groups=mesh['z'=8,'core'=2,'y'=8,'x'=4] {'x','z'}, dimensions={0} | all-to-all | bytes 524288 | tf_op jit(solution)/shard_map/all_to_all | solution.py:309
  164.8 13.4 %all_to_all.46.parts_ref = f32[16,16,128]{2,1,0:T(8,128)S(1)} all-to-all(f32[16,16,128]{2,1,0:T(8,128)S(1)} %broadcast_in_dim.8), channel_id=1, replica_groups=mesh['z'=8,'core'=2,'y'=8,'x'=4] {'core','y'}, dimensions={0} | all-to-all | bytes 262144 | tf_op jit(solution)/shard_map/all_to_all | solution.py:309
  178.2 3.4 %solve.3 = (f32[32,32]{1,0:T(8,128)}, f32[2,20480]{1,0:T(2,128)}) custom-call(f32[16,16,128]{2,1,0:T(8,128)S(1)} %all_to_all.46.parts_ref, f32[32,72,512]{2,1,0:T(8,128)} %all-gather.2.cloned.1.call-done.slab_ref, f32[32,32]{1,0:T(8,128)} %get-tuple-element.23.rest_0_), custom_call_target="tpu_custom_call" | custom-call | tf_op jit(solution)/shard_map/solve/pallas_call | solution.py:292
  (5 shorter events, 0.1 us)
Async XLA Ops:
  7.2 65.0 %all-gather.2.cloned.1.call-start = ((), (), s32[]{:S(2)}) async-start(), calls=%async_computation.8 | async-start | bytes 5013504 | tf_op jit(solution)/shard_map/all_gather | solution.py:321
  9.3 9.6 %collective-permute-start = (bf16[2,40,256]{2,1,0:T(8,128)(2,1)S(1)}, bf16[2,40,256]{2,1,0:T(8,128)(2,1)S(1)}, u32[]{:S(2)}, u32[]{:S(2)}) collective-permute-start(bf16[2,40,256]{2,1,0:T(8,128)(2,1)S(1)} %get-tuple-element.15), channel_id=1, source_target_pairs={{0,32},{32,0},{1,33},{33,1},{2,34},{34,2},{3,35},{35,3},{4,36},{36... | collective-permute-start | bytes 122888 | tf_op jit(solution)/shard_map/ppermute | solution.py:313
  19.8 23.1 %all-to-all-start = ((bf16[32,40,256]{2,1,0:T(8,128)(2,1)}), bf16[32,40,256]{2,1,0:T(8,128)(2,1)S(1)}, u32[]{:S(2)}, u32[]{:S(2)}) async-start(bf16[32,40,256]{2,1,0:T(8,128)(2,1)} %bitcast.2), calls=%async_computation | async-start | bytes 1310720 | tf_op jit(solution)/shard_map/all_to_all | solution.py:309
  42.9 6.0 %collective-permute-start.1 = (bf16[1280,256]{1,0:T(8,128)(2,1)S(1)}, bf16[1280,256]{1,0:T(8,128)(2,1)S(1)}, u32[]{:S(2)}, u32[]{:S(2)}) collective-permute-start(bf16[1280,256]{1,0:T(8,128)(2,1)S(1)} %bitcast.6), channel_id=1, source_target_pairs={{0,32},{32,0},{1,33},{33,1},{2,34},{34,2},{3,35},{35,3},{4,36},{36... | collective-permute-start | bytes 1966088 | tf_op jit(solution)/shard_map/ppermute | solution.py:313
  127.9 6.1 %collective-permute-start.2 = (bf16[1280,256]{1,0:T(8,128)(2,1)S(1)}, bf16[1280,256]{1,0:T(8,128)(2,1)S(1)}, u32[]{:S(2)}, u32[]{:S(2)}) collective-permute-start(bf16[1280,256]{1,0:T(8,128)(2,1)S(1)} %bitcast.8), channel_id=1, source_target_pairs={{0,32},{32,0},{1,33},{33,1},{2,34},{34,2},{3,35},{35,3},{4,36},{36... | collective-permute-start | bytes 1966088 | tf_op jit(solution)/shard_map/ppermute | solution.py:313
Sparse Core Ops, SparseCore 0:
  10.1 51.9 all-gather.1

commit v9 on v8

--- a/solution.py
+++ b/solution.py
@@ -68,9 +68,15 @@
     )(ensemble, inputs, picks, observed, perturb)
 
 
-def evaluate_kernel(own_ref, other_ref, x_ref, features_hbm, out_ref, whole_ref, chosen_ref, features_ref, sem):
+def evaluate_kernel(
+    own_blocks, other_blocks, x_ref, features_hbm, out_ref, whole_ref, chosen_ref, features_ref, own_ref, other_ref, sem
+):
     fetch = pltpu.make_async_copy(features_hbm, features_ref, sem)
     fetch.start()
+    for blocks, rows in ((own_blocks, own_ref), (other_blocks, other_ref)):
+        for p in range(0, 32, 2):
+            pair = [blocks[(q % 4) * 8 + q // 4] for q in (p, p + 1)]
+            rows[ROWS * p : ROWS * p + 2 * ROWS, :] = jnp.concatenate(pair, 0)
     r = lax.broadcasted_iota(jnp.int32, (256, 256), 0)
     s = lax.broadcasted_iota(jnp.int32, (256, 256), 1)
     mix = (s == ((r + lax.axis_index("core")) % 2) * 128 + r // 2).astype(F32).astype(BF16)
@@ -124,6 +130,8 @@
             pltpu.VMEM((384, 128), F32),
             pltpu.VMEM((192, 128), F32),
             pltpu.VMEM((128, FEATS), BF16),
+            pltpu.VMEM((32 * ROWS, 256), BF16),
+            pltpu.VMEM((32 * ROWS, 256), BF16),
             pltpu.SemaphoreType.DMA,
         ],
         name="evaluate",
@@ -281,14 +289,14 @@
                 state_ref[i : i + 1, 512 * row : 512 * row + 512] = total[row : row + 1, :]
         else:
             for y in range(8):
-                state_ref[y, i] = total.astype(BF16)
+                state_ref[8 * i + y] = total.astype(BF16)
 
 
 def solve(last, parts, slab, *mix):
     if last:
         outs = jax.ShapeDtypeStruct((32, 32), F32), jax.ShapeDtypeStruct((2, ROWS * 512), F32)
     else:
-        outs = jax.ShapeDtypeStruct((32, 32), F32), pltpu.VMEM((8, 4, ROWS, 256), BF16)
+        outs = jax.ShapeDtypeStruct((32, 32), F32), pltpu.VMEM((32, ROWS, 256), BF16)
     return pl.pallas_call(
         functools.partial(solve_kernel, last),
         out_shape=outs,
@@ -321,11 +329,11 @@
     slab = lax.all_gather(own, ("z", "core"), axis=0, tiled=True)
     taken = swap(give)
     plane = jnp.where(core == 0, jnp.concatenate([keep, taken]), jnp.concatenate([taken, keep]))
-    plane = jnp.broadcast_to(plane[None], (8, 4, ROWS, 256))
+    plane = jnp.broadcast_to(plane[:, None], (4, 8, ROWS, 256)).reshape(32, ROWS, 256)
     ext = lax.all_gather(ext, "x", axis=0, tiled=True)
     mix = []
     for repeat in range(SUBSTEPS):
-        half = exchange(plane.reshape(32, ROWS, 256), ("y", "x")).reshape(32 * ROWS, 256)
+        half = exchange(plane, ("x", "y"))
         half, ext = lax.optimization_barrier((half, ext))
         other = swap(half)
         preds = evaluate(half, other, ext, features)

time: 189 us -> 188 us (level)
  starting transfers between devices: 21.8 us -> 25.7 us
  blocking collectives: 130 us -> 127 us
    ppermute x3, starting transfers between devices: 17.5 us -> 21.3 us  [swap(): return lax.ppermute(block, 'core', [(0, 1), (1, 0)])]
    all_to_all x7, blocking collectives: 113 us -> 110 us  [exchange(): return lax.all_to_all(blocks, axes, 0, 0, tiled=True)]
where the time goes in v9:
time: 188 us
  blocking collectives  127 us (68%)
  starting transfers between devices  25.7 us (14%)
  Pallas kernels  15.5 us (8%)
  between operations  14.2 us (8%)
  waiting for transfers between devices  4.44 us (2%)
    all_to_all x7, blocking collectives, exchange(): return lax.all_to_all(blocks, axes, 0, 0, tiled=True)  110 us
    ppermute x3, starting transfers between devices, swap(): return lax.ppermute(block, 'core', [(0, 1), (1, 0)])  21.3 us
    all_gather x1, blocking collectives, local(): ext = lax.all_gather(ext, 'x', axis=0, tiled=True)  16.7 us
    pallas_call x2, Pallas kernels, solve(): pl.pallas_call(functools.partial(solve_kernel, last), out_shape=outs, in_...  5.86 us
    all_to_all x1, starting transfers between devices, exchange(): return lax.all_to_all(blocks, axes, 0, 0, tiled=True)  4.3 us
    ppermute x3, waiting for transfers between devices, swap(): return lax.ppermute(block, 'core', [(0, 1), (1, 0)])  4.25 us
    pallas_call x2, Pallas kernels, evaluate(): pl.pallas_call(evaluate_kernel, out_shape=pltpu.VMEM((32, 6, 128), BF16),...  3.92 us
  transfers between devices with their start and end apart: 5, of which 4 were waited for; matrix products, arithmetic and copies ran while one was open for 0% of the time, Pallas kernels for 1%

profile of v9, /device:TPU:1, one launch (start us, length us, event | category | flops | bytes accessed | tf_op | source)
XLA Modules:
  0.0 187.8 jit_solution(16233183913284521890)
XLA Ops:
  7.2 0.0 all-gather.2.cloned.1.call-start
  7.2 2.0 %prepare.1 = (f32[2,72,512]{2,1,0:T(8,128)}, bf16[2,40,256]{2,1,0:T(8,128)(2,1)S(1)}, bf16[2,40,256]{2,1,0:T(8,128)(2,1)S(1)}, bf16[96,1152]{1,0:T(8,128)(2,1)S(1)}) custom-call(f32[2,20480]{1,0:T(2,128)} %ensemble_ref.1, bf16[192,1024]{1,0:T(8,128)(2,1)} %inputs_ref.1, s32[96,128]{1,0:T(8,128)} %bitcast.3, f32[1,12288]{1,0:T(1,128)} %bitcast.4, ...), custom_call_target="tpu_custom_call" | custom-call | tf_op jit(solution)/shard_map/prepare/pallas_call | solution.py:57
  9.2 0.0 all-gather.2.cloned.1.call-update
  9.3 8.8 %collective-permute-start = (bf16[2,40,256]{2,1,0:T(8,128)(2,1)S(1)}, bf16[2,40,256]{2,1,0:T(8,128)(2,1)S(1)}, u32[]{:S(2)}, u32[]{:S(2)}) collective-permute-start(bf16[2,40,256]{2,1,0:T(8,128)(2,1)S(1)} %get-tuple-element.15), channel_id=1, source_target_pairs={{0,32},{32,0},{1,33},{33,1},{2,34},{34,2},{3,35},{35,3},{4,36},{36... | collective-permute-start | bytes 122888 | tf_op jit(solution)/shard_map/ppermute | solution.py:321
  18.1 0.8 collective-permute-done
  18.9 0.9 broadcast_in_dim.6
  19.8 4.3 %all-to-all-start = ((bf16[32,40,256]{2,1,0:T(8,128)(2,1)}), bf16[32,40,256]{2,1,0:T(8,128)(2,1)S(1)}, u32[]{:S(2)}, u32[]{:S(2)}) async-start(bf16[32,40,256]{2,1,0:T(8,128)(2,1)} %bitcast.2), calls=%async_computation | async-start | bytes 1310720 | tf_op jit(solution)/shard_map/all_to_all | solution.py:317
  24.1 16.7 %all_gather.6.x_ref = bf16[384,1152]{1,0:T(8,128)(2,1)S(1)} all-gather(bf16[96,1152]{1,0:T(8,128)(2,1)S(1)} %get-tuple-element.16), channel_id=1, replica_groups=mesh['z'=8,'core'=2,'y'=8,'x'=4] {'x'}, dimensions={0}, use_global_device_ids=true | all-gather | bytes 1105920 | tf_op jit(solution)/shard_map/all_gather | solution.py:333
  40.8 0.2 all-to-all-done.own_blocks
  41.0 5.7 %collective-permute-start.1 = (bf16[32,40,256]{2,1,0:T(8,128)(2,1)S(1)}, bf16[32,40,256]{2,1,0:T(8,128)(2,1)S(1)}, u32[]{:S(2)}, u32[]{:S(2)}) collective-permute-start(bf16[32,40,256]{2,1,0:T(8,128)(2,1)S(1)} %all-to-all-done.own_blocks), channel_id=1, source_target_pairs={{0,32},{32,0},{1,33},{33,1},{2,34},{34,2},{3,35},{35,3},{4,36},{36... | collective-permute-start | bytes 1966088 | tf_op jit(solution)/shard_map/ppermute | solution.py:321
  46.6 1.7 collective-permute-done.1.other_blocks
  48.3 2.0 %evaluate.2 = bf16[32,6,128]{2,1,0:T(8,128)(2,1)S(1)} custom-call(bf16[32,40,256]{2,1,0:T(8,128)(2,1)S(1)} %all-to-all-done.own_blocks, bf16[32,40,256]{2,1,0:T(8,128)(2,1)S(1)} %collective-permute-done.1.other_blocks, bf16[384,1152]{1,0:T(8,128)(2,1)S(1)} %all_gather.6.x_ref, bf16[128,256]{1,0:T(8,128)(2,1)} %features_hbm.3), custom_call_target="tpu_custom_call" | custom-call | tf_op jit(solution)/shard_map/evaluate/pallas_call | solution.py:124
  50.3 19.6 %all_to_all.40.preds_ref = bf16[32,6,128]{2,1,0:T(8,128)(2,1)S(1)} all-to-all(bf16[32,6,128]{2,1,0:T(8,128)(2,1)S(1)} %evaluate.2), channel_id=1, replica_groups=mesh['z'=8,'core'=2,'y'=8,'x'=4] {'z','x'}, dimensions={0} | all-to-all | bytes 98304 | tf_op jit(solution)/shard_map/all_to_all | solution.py:317
  69.9 0.0 all-gather.2.cloned.1.call-done.slab_ref
  69.9 1.7 member_sums.2
  71.7 12.8 %all_to_all.41 = f32[32,16,128]{2,1,0:T(8,128)S(1)} all-to-all(f32[32,16,128]{2,1,0:T(8,128)S(1)} %member_sums.2), channel_id=1, replica_groups=mesh['z'=8,'core'=2,'y'=8,'x'=4] {'x','z'}, dimensions={0} | all-to-all | bytes 524288 | tf_op jit(solution)/shard_map/all_to_all | solution.py:317
  84.5 17.0 %all_to_all.42.parts_ref = f32[16,16,128]{2,1,0:T(8,128)S(1)} all-to-all(f32[16,16,128]{2,1,0:T(8,128)S(1)} %broadcast_in_dim.7), channel_id=1, replica_groups=mesh['z'=8,'core'=2,'y'=8,'x'=4] {'core','y'}, dimensions={0} | all-to-all | bytes 262144 | tf_op jit(solution)/shard_map/all_to_all | solution.py:317
  101.6 2.5 %solve.2 = (f32[32,32]{1,0:T(8,128)}, bf16[32,40,256]{2,1,0:T(8,128)(2,1)S(1)}) custom-call(f32[16,16,128]{2,1,0:T(8,128)S(1)} %all_to_all.42.parts_ref, f32[32,72,512]{2,1,0:T(8,128)} %all-gather.2.cloned.1.call-done.slab_ref), custom_call_target="tpu_custom_call" | custom-call | tf_op jit(solution)/shard_map/solve/pallas_call | solution.py:300
  104.0 21.1 %all_to_all.43.own_blocks = bf16[32,40,256]{2,1,0:T(8,128)(2,1)S(1)} all-to-all(bf16[32,40,256]{2,1,0:T(8,128)(2,1)S(1)} %get-tuple-element.20), channel_id=1, replica_groups=mesh['z'=8,'core'=2,'y'=8,'x'=4] {'x','y'}, dimensions={0} | all-to-all | bytes 1310720 | tf_op jit(solution)/shard_map/all_to_all | solution.py:317
  125.1 6.9 %collective-permute-start.2 = (bf16[32,40,256]{2,1,0:T(8,128)(2,1)S(1)}, bf16[32,40,256]{2,1,0:T(8,128)(2,1)S(1)}, u32[]{:S(2)}, u32[]{:S(2)}) collective-permute-start(bf16[32,40,256]{2,1,0:T(8,128)(2,1)S(1)} %all_to_all.43.own_blocks), channel_id=1, source_target_pairs={{0,32},{32,0},{1,33},{33,1},{2,34},{34,2},{3,35},{35,3},{4,36},{36... | collective-permute-start | bytes 1966088 | tf_op jit(solution)/shard_map/ppermute | solution.py:321
  132.0 1.7 collective-permute-done.2.other_blocks
  133.7 2.0 %evaluate.3 = bf16[32,6,128]{2,1,0:T(8,128)(2,1)S(1)} custom-call(bf16[32,40,256]{2,1,0:T(8,128)(2,1)S(1)} %all_to_all.43.own_blocks, bf16[32,40,256]{2,1,0:T(8,128)(2,1)S(1)} %collective-permute-done.2.other_blocks, bf16[384,1152]{1,0:T(8,128)(2,1)S(1)} %all_gather.6.x_ref, bf16[128,256]{1,0:T(8,128)(2,1)} %features_hbm.3), custom_call_target="tpu_custom_call" | custom-call | tf_op jit(solution)/shard_map/evaluate/pallas_call | solution.py:124
  135.7 12.0 %all_to_all.44.preds_ref = bf16[32,6,128]{2,1,0:T(8,128)(2,1)S(1)} all-to-all(bf16[32,6,128]{2,1,0:T(8,128)(2,1)S(1)} %evaluate.3), channel_id=1, replica_groups=mesh['z'=8,'core'=2,'y'=8,'x'=4] {'z','x'}, dimensions={0} | all-to-all | bytes 98304 | tf_op jit(solution)/shard_map/all_to_all | solution.py:317
  147.7 1.9 %member_sums.3 = f32[32,16,128]{2,1,0:T(8,128)S(1)} custom-call(bf16[32,6,128]{2,1,0:T(8,128)(2,1)S(1)} %all_to_all.44.preds_ref, f32[32,72,512]{2,1,0:T(8,128)} %all-gather.2.cloned.1.call-done.slab_ref, f32[32,32]{1,0:T(8,128)} %get-tuple-element.23.rest_0_), custom_call_target="tpu_custom_call" | custom-call | tf_op jit(solution)/shard_map/member_sums/pallas_call | solution.py:195
  149.6 12.8 %all_to_all.45 = f32[32,16,128]{2,1,0:T(8,128)S(1)} all-to-all(f32[32,16,128]{2,1,0:T(8,128)S(1)} %member_sums.3), channel_id=1, replica_groups=mesh['z'=8,'core'=2,'y'=8,'x'=4] {'x','z'}, dimensions={0} | all-to-all | bytes 524288 | tf_op jit(solution)/shard_map/all_to_all | solution.py:317
  162.5 15.1 %all_to_all.46.parts_ref = f32[16,16,128]{2,1,0:T(8,128)S(1)} all-to-all(f32[16,16,128]{2,1,0:T(8,128)S(1)} %broadcast_in_dim.8), channel_id=1, replica_groups=mesh['z'=8,'core'=2,'y'=8,'x'=4] {'core','y'}, dimensions={0} | all-to-all | bytes 262144 | tf_op jit(solution)/shard_map/all_to_all | solution.py:317
  177.6 3.4 %solve.3 = (f32[32,32]{1,0:T(8,128)}, f32[2,20480]{1,0:T(2,128)}) custom-call(f32[16,16,128]{2,1,0:T(8,128)S(1)} %all_to_all.46.parts_ref, f32[32,72,512]{2,1,0:T(8,128)} %all-gather.2.cloned.1.call-done.slab_ref, f32[32,32]{1,0:T(8,128)} %get-tuple-element.23.rest_0_), custom_call_target="tpu_custom_call" | custom-call | tf_op jit(solution)/shard_map/solve/pallas_call | solution.py:300
  (5 shorter events, 0.1 us)
Async XLA Ops:
  7.2 62.8 %all-gather.2.cloned.1.call-start = ((), (), s32[]{:S(2)}) async-start(), calls=%async_computation.8 | async-start | bytes 5013504 | tf_op jit(solution)/shard_map/all_gather | solution.py:329
  9.3 9.6 %collective-permute-start = (bf16[2,40,256]{2,1,0:T(8,128)(2,1)S(1)}, bf16[2,40,256]{2,1,0:T(8,128)(2,1)S(1)}, u32[]{:S(2)}, u32[]{:S(2)}) collective-permute-start(bf16[2,40,256]{2,1,0:T(8,128)(2,1)S(1)} %get-tuple-element.15), channel_id=1, source_target_pairs={{0,32},{32,0},{1,33},{33,1},{2,34},{34,2},{3,35},{35,3},{4,36},{36... | collective-permute-start | bytes 122888 | tf_op jit(solution)/shard_map/ppermute | solution.py:321
  19.8 21.1 %all-to-all-start = ((bf16[32,40,256]{2,1,0:T(8,128)(2,1)}), bf16[32,40,256]{2,1,0:T(8,128)(2,1)S(1)}, u32[]{:S(2)}, u32[]{:S(2)}) async-start(bf16[32,40,256]{2,1,0:T(8,128)(2,1)} %bitcast.2), calls=%async_computation | async-start | bytes 1310720 | tf_op jit(solution)/shard_map/all_to_all | solution.py:317
  41.0 7.4 %collective-permute-start.1 = (bf16[32,40,256]{2,1,0:T(8,128)(2,1)S(1)}, bf16[32,40,256]{2,1,0:T(8,128)(2,1)S(1)}, u32[]{:S(2)}, u32[]{:S(2)}) collective-permute-start(bf16[32,40,256]{2,1,0:T(8,128)(2,1)S(1)} %all-to-all-done.own_blocks), channel_id=1, source_target_pairs={{0,32},{32,0},{1,33},{33,1},{2,34},{34,2},{3,35},{35,3},{4,36},{36... | collective-permute-start | bytes 1966088 | tf_op jit(solution)/shard_map/ppermute | solution.py:321
  125.1 8.6 %collective-permute-start.2 = (bf16[32,40,256]{2,1,0:T(8,128)(2,1)S(1)}, bf16[32,40,256]{2,1,0:T(8,128)(2,1)S(1)}, u32[]{:S(2)}, u32[]{:S(2)}) collective-permute-start(bf16[32,40,256]{2,1,0:T(8,128)(2,1)S(1)} %all_to_all.43.own_blocks), channel_id=1, source_target_pairs={{0,32},{32,0},{1,33},{33,1},{2,34},{34,2},{3,35},{35,3},{4,36},{36... | collective-permute-start | bytes 1966088 | tf_op jit(solution)/shard_map/ppermute | solution.py:321
Sparse Core Ops, SparseCore 0:
  10.1 51.9 all-gather.1
